TPU v7x, 256 devices: a whole 4x4x8 slice. The times are simulated.
256 devices in a mesh: dp: 4 (over x), ctx: 64 (over z, y, core).
Axes of the slice: x: 4, y: 4, z: 8, core: 2. Of those that a mesh axis runs over, the one named last changes fastest.
Arguments:
- q_proj: bfloat16 [4, 8192, 4096], P('dp', 'ctx'), may hold values from -6 to 6
- k_proj: bfloat16 [4, 8192, 4096], P('dp', 'ctx'), may hold values from -6 to 6
- v_proj: bfloat16 [4, 8192, 4096], P('dp', 'ctx'), may hold values from -6 to 6
- out_grad: bfloat16 [4, 8192, 4096], P('dp', 'ctx'), may hold values from -6 to 6
- filters: bfloat16 [16, 256], replicated, may hold values from -0.375 to 0.375
- reaches: int32 [16], replicated, may hold values from 128 to 256, as said below
Outputs:
- grad_q: bfloat16 [4, 8192, 4096], P('dp', 'ctx')
- grad_k: bfloat16 [4, 8192, 4096], P('dp', 'ctx')
- grad_v: bfloat16 [4, 8192, 4096], P('dp', 'ctx')
- grad_filters: float32 [16, 256], replicated
Inputs may be any that keep to these rules, and one draw needn't show every extreme that they name: `reaches`: every reach is a multiple of 128, and at least one group has reach exactly 256.
All inputs are finite; a program needn't handle non-finite values.
Results may differ from a plain program's by a relative error of at most 0.0049.
Values may be sent and summed in bfloat16 or wider, within the bound.
No kernel may reach another device: no remote copies, remote signals or barrier semaphores. Data moves between devices by JAX's collectives and lax.ppermute only.
A program may use at most 64 MiB of HBM per device.

v0:
```python
import math

import jax
import jax.numpy as jnp
from jax import lax
from jax.sharding import PartitionSpec as P


def shifted_2(block, axis, distance):
    devices = range(lax.axis_size(axis))
    route = [(i - distance, i) for i in devices if i - distance in devices]
    return lax.ppermute(block, axis, route)


def toeplitz_blocks(masked, count, block_size):
    group_n, width = masked.shape
    total = (count + 2) * block_size
    front = jnp.zeros((group_n, block_size - 1), masked.dtype)
    back = jnp.zeros((group_n, total + 1 - (block_size - 1) - width), masked.dtype)
    row_line = jnp.concatenate([front, masked, back], axis=1)
    tiled = jnp.broadcast_to(row_line[:, None, :], (group_n, block_size, total + 1))
    flat = tiled.reshape(group_n, block_size * (total + 1))[:, : block_size * total]
    skewed = flat.reshape(group_n, block_size, total)
    window = skewed[:, :, block_size - 1 : block_size - 1 + (count + 1) * block_size]
    window = window.reshape(group_n, block_size, count + 1, block_size)
    return jnp.transpose(window, (2, 0, 3, 1))


def diagonal_sums(corr):
    block_size = corr.shape[-1]
    leading = corr.shape[:-2]
    flipped = jnp.flip(corr, -1)
    padded = jnp.concatenate([flipped, jnp.zeros_like(flipped)], axis=-1)
    flattened = padded.reshape(leading + (2 * block_size * block_size,))[
        ..., : block_size * (2 * block_size - 1)
    ]
    return flattened.reshape(leading + (block_size, 2 * block_size - 1)).sum(axis=-2)


def fold_diagonals(corr):
    count = corr.shape[0]
    block_size = corr.shape[-1]
    diag_sums = diagonal_sums(corr)
    shifted = jnp.concatenate([jnp.zeros_like(diag_sums[..., :1]), diag_sums], axis=-1)
    lower = shifted[..., :block_size]
    upper = shifted[..., block_size:]
    empty = jnp.zeros_like(lower[:1])
    placed = jnp.concatenate([lower, empty], 0) + jnp.concatenate([empty, upper], 0)
    kept = jnp.moveaxis(placed[1:count], 0, -2)
    return kept.reshape(kept.shape[:-2] + ((count - 1) * block_size,))


def body(q_proj, k_proj, v_proj, out_grad, filters, reaches):
    batch_n, tok_n, chan_n = q_proj.shape
    group_n, width = filters.shape
    group_width = chan_n // group_n
    slab_n = width // tok_n
    lags = jnp.arange(width, dtype=jnp.int32)
    keep = lags[None, :] < reaches[:, None]
    masked = jnp.where(keep, filters, jnp.zeros((), filters.dtype))
    kernels = toeplitz_blocks(masked, slab_n, tok_n)
    signal = (k_proj.astype(jnp.float32) * v_proj.astype(jnp.float32)).astype(jnp.bfloat16)
    dconv = (out_grad.astype(jnp.float32) * q_proj.astype(jnp.float32)).astype(jnp.bfloat16)
    earlier = [shifted_2(signal, "ctx", distance) for distance in range(1, slab_n + 1)]
    stacked = jnp.stack([signal] + earlier)
    sig_blocks = stacked.reshape(slab_n + 1, batch_n, tok_n, group_n, group_width)
    dcv_blocks = dconv.reshape(batch_n, tok_n, group_n, group_width)
    conv = jnp.einsum("mgab,mnbgc->nagc", kernels, sig_blocks, preferred_element_type=jnp.float32)
    grad_q = (out_grad.astype(jnp.float32) * conv.reshape(batch_n, tok_n, chan_n)).astype(
        jnp.bfloat16
    )
    corr = jnp.einsum(
        "nagc,mnbgc->mgab", dcv_blocks, sig_blocks, preferred_element_type=jnp.float32
    )
    local_taps = fold_diagonals(corr) * keep.astype(jnp.float32)
    terms = jnp.einsum("mgab,nagc->mnbgc", kernels, dcv_blocks, preferred_element_type=jnp.float32)
    terms = terms.reshape(slab_n + 1, batch_n, tok_n, chan_n)
    dsignal = terms[0]
    for distance in range(1, slab_n + 1):
        dsignal = dsignal + shifted_2(terms[distance], "ctx", -distance)
    grad_k = (dsignal * v_proj.astype(jnp.float32)).astype(jnp.bfloat16)
    grad_v = (dsignal * k_proj.astype(jnp.float32)).astype(jnp.bfloat16)
    scale = 1.0 / math.sqrt(
        batch_n * lax.axis_size("dp") * tok_n * lax.axis_size("ctx") * group_width
    )
    grad_filters = lax.psum(local_taps, ("dp", "ctx")) * scale
    return (grad_q, grad_k, grad_v, grad_filters)


def solution(mesh):
    return jax.shard_map(
        body,
        mesh=mesh,
        in_specs=(
            P("dp", "ctx", None),
            P("dp", "ctx", None),
            P("dp", "ctx", None),
            P("dp", "ctx", None),
            P(),
            P(),
        ),
        out_specs=(P("dp", "ctx", None), P("dp", "ctx", None), P("dp", "ctx", None), P()),
        check_vma=False,
    )
```

profile of v0, /device:TPU:1, one launch (start us, length us, event | category | flops | bytes accessed | tf_op | source)
XLA Modules:
  0.0 289.8 jit_solution(2452013702667571022)
XLA Ops:
  0.7 0.1 pad.6.clone
  0.7 0.0 copy-start.8
  0.7 0.0 copy-start.9
  0.7 1.8 fusion.1
  2.6 1.2 copy.68
  3.8 0.0 copy-done.8
  3.8 0.0 copy-done.9
  3.8 0.1 fusion.9
  3.9 0.1 maximum_maximum_fusion
  4.0 0.2 broadcast_in_dim.24
  4.2 4.0 %reshape.59 = bf16[16,65664]{1,0:T(8,128)(2,1)} reshape(bf16[16,128,513]{2,1,0:T(8,128)(2,1)S(1)} %broadcast_in_dim.24) | data formatting | bytes 4202496 | tf_op jit(solution)/shard_map/reshape | solution.py:22
  8.2 0.0 slice-start
  8.2 1.6 slice-done
  9.8 0.7 copy.67
  10.5 0.8 slice.40
  11.3 1.0 copy.47
  12.2 0.0 copy-start.1
  12.2 1.1 copy-done.1
  13.4 2.3 convolution_bitcast_fusion
  15.7 2.4 fusion.12
  18.1 2.9 copy.52
  21.0 1.3 collective-permute-start.3
  22.3 2.9 %copy.50 = f32[1,128,4096]{2,1,0:T(8,128)} copy(f32[1,128,4096]{1,2,0:T(8,128)} %bitcast.46) | data formatting | bytes 4194304 | tf_op jit(solution)/shard_map/squeeze | solution.py:80
  25.2 5.1 %collective-permute-start.2 = (f32[1,128,4096]{2,1,0:T(8,128)}, f32[1,128,4096]{2,1,0:T(8,128)}, u32[]{:S(2)}, u32[]{:S(2)}) collective-permute-start(f32[1,128,4096]{2,1,0:T(8,128)} %copy.50), channel_id=1, source_target_pairs={{1,0},{2,1},{3,2},{4,3},{5,4},{6,5},{7,6},{8,7},{9,8},{10,9},{11,1... | collective-permute-start | bytes 6291464 | tf_op jit(solution)/shard_map/ppermute | solution.py:12
  30.3 1.8 copy.51
  32.2 36.2 %collective-permute-done.3 = f32[1,128,4096]{2,1,0:T(8,128)} collective-permute-done((f32[1,128,4096]{2,1,0:T(8,128)}, f32[1,128,4096]{2,1,0:T(8,128)}, u32[]{:S(2)}, u32[]{:S(2)}) %collective-permute-start.3) | collective-permute-done | bytes 2097184 | tf_op jit(solution)/shard_map/ppermute | solution.py:12
  68.4 25.3 %collective-permute-done.2 = f32[1,128,4096]{2,1,0:T(8,128)} collective-permute-done((f32[1,128,4096]{2,1,0:T(8,128)}, f32[1,128,4096]{2,1,0:T(8,128)}, u32[]{:S(2)}, u32[]{:S(2)}) %collective-permute-start.2) | collective-permute-done | bytes 2097184 | tf_op jit(solution)/shard_map/ppermute | solution.py:12
  93.7 5.7 %fusion.2 = (bf16[1,128,4096]{2,1,0:T(8,128)(2,1)}, bf16[1,128,4096]{2,1,0:T(8,128)(2,1)}, bf16[1,128,4096]{2,1,0:T(8,128)(2,1)S(1)}) fusion(bf16[1,128,4096]{2,1,0:T(8,128)(2,1)} %param.7, f32[1,128,4096]{2,1,0:T(8,128)} %collective-permute-done.3, f32[1,128,4096]{2,1,0:T(8,128)} %copy.51, f32[1,128,4096]{2,1,0:T(8,128)} %collective-permute-done.2, ...), kind=kLoop, calls=%fused_computation.9 | loop fusion | flops 5242880 | bytes 11534336 | tf_op jit(solution)/shard_map/convert_element_type | solution.py:82
  99.4 4.4 %collective-permute-start.1 = (bf16[1,128,4096]{2,1,0:T(8,128)(2,1)S(1)}, bf16[1,128,4096]{2,1,0:T(8,128)(2,1)}, u32[]{:S(2)}, u32[]{:S(2)}) collective-permute-start(bf16[1,128,4096]{2,1,0:T(8,128)(2,1)S(1)} %get-tuple-element.9), channel_id=1, source_target_pairs={{0,2},{1,3},{2,4},{3,5},{4,6},{5,7},{6,8},{7,9},{8,10},{9,11},{10,... | collective-permute-start | bytes 3145736 | tf_op jit(solution)/shard_map/ppermute | solution.py:12
  103.7 2.1 collective-permute-start
  105.8 1.3 copy.44
  107.2 0.0 copy-start.2
  107.2 17.5 %collective-permute-done.1 = bf16[1,128,4096]{2,1,0:T(8,128)(2,1)} collective-permute-done((bf16[1,128,4096]{2,1,0:T(8,128)(2,1)S(1)}, bf16[1,128,4096]{2,1,0:T(8,128)(2,1)}, u32[]{:S(2)}, u32[]{:S(2)}) %collective-permute-start.1) | collective-permute-done | bytes 1048608 | tf_op jit(solution)/shard_map/ppermute | solution.py:12
  124.7 2.3 copy.46
  126.9 9.0 %collective-permute-done = bf16[1,128,4096]{2,1,0:T(8,128)(2,1)} collective-permute-done((bf16[1,128,4096]{2,1,0:T(8,128)(2,1)S(1)}, bf16[1,128,4096]{2,1,0:T(8,128)(2,1)}, u32[]{:S(2)}, u32[]{:S(2)}) %collective-permute-start) | collective-permute-done | bytes 1048608 | tf_op jit(solution)/shard_map/ppermute | solution.py:12
  135.9 0.0 copy-start.5
  135.9 2.4 copy.45
  138.3 0.0 copy-done.2
  138.3 0.0 copy-done.5
  138.3 0.0 copy-start.3
  138.3 0.0 copy-start.6
  138.3 0.0 copy-start.7
  138.3 4.0 %fusion.5 = f32[16,256,128,1]{2,1,3,0:T(8,128)} fusion(bf16[3,16,128,128]{3,2,0,1:T(8,128)(2,1)S(1)} %bitcast.50, bf16[1,1,128,16,256]{2,4,0,3,1:T(8,128)(2,1)} %bitcast.57, bf16[1,1,128,16,256]{2,4,0,3,1:T(8,128)(2,1)} %bitcast.59, bf16[1,1,128,16,256]{2,4,0,3,1:T(8,128)(2,1)S(1)} %bitcast.55), kind=kOutput, calls=%fused_computation.14 | convolution fusion | flops 405798912 | bytes 6815744 | tf_op jit(solution)/shard_map/mgab,mnbgc->nagc/dot_general | solution.py:68
  142.3 0.0 copy-done.3
  142.3 0.0 copy-done.6
  142.3 0.0 copy-done.7
  142.3 3.0 %convolution_bitcast_fusion.1 = f32[3,16,128,128]{2,3,0,1:T(8,128)} fusion(bf16[1,1,128,16,256]{2,4,0,3,1:T(8,128)(2,1)S(1)} %bitcast.58, bf16[1,1,128,16,256]{2,4,0,3,1:T(8,128)(2,1)S(1)} %bitcast.60, bf16[1,1,128,16,256]{2,4,0,3,1:T(8,128)(2,1)S(1)} %bitcast.56, bf16[128,16,256,1]{2,1,0,3:T(8,128)(2,1)S(1)} %bitcast.52), kind=kOutput, calls=%fused_computation.13 | convolution fusion | flops 405798912 | bytes 7340032 | tf_op jit(solution)/shard_map/nagc,mnbgc->mgab/dot_general | solution.py:72
  145.3 20.4 %rev.4 = f32[3,16,128,128]{2,3,0,1:T(8,128)S(1)} reverse(f32[3,16,128,128]{2,3,0,1:T(8,128)} %convolution_bitcast_fusion.1), dimensions={3} | reverse | bytes 6291456 | tf_op jit(solution)/shard_map/jit(_flip)/rev | solution.py:32
  165.7 2.3 copy.65
  168.1 0.0 copy-start.4
  168.1 2.0 copy.48
  170.1 0.0 copy-done.4
  170.1 0.0 copy-start
  170.1 1.2 fusion
  171.3 1.1 copy-done
  172.4 3.4 %concatenate.17.clone = f32[3,16,128,256]{3,2,1,0:T(8,128)} pad(f32[3,16,128,128]{3,2,1,0:T(8,128)S(1)} %copy-done, f32[]{:T(128)} %constant.4.clone.1), padding=0_0x0_0x0_0x0_128 | pad | bytes 9437188 | tf_op jit(solution)/shard_map/concatenate | solution.py:33
  175.8 7.2 %reshape.64 = f32[3,16,32768]{2,1,0:T(8,128)} reshape(f32[3,16,128,256]{3,2,1,0:T(8,128)} %concatenate.17.clone) | data formatting | bytes 12582912 | tf_op jit(solution)/shard_map/reshape | solution.py:34
  183.0 5.8 %slice.44 = f32[3,16,32640]{2,1,0:T(8,128)} slice(f32[3,16,32768]{2,1,0:T(8,128)} %reshape.64), slice={[0:3], [0:16], [0:32640]} | slice | bytes 12533760 | tf_op jit(solution)/shard_map/slice | solution.py:34
  188.8 12.7 %reshape.65 = f32[3,16,128,255]{3,2,1,0:T(8,128)} reshape(f32[3,16,32640]{2,1,0:T(8,128)} %slice.44) | data formatting | bytes 12533760 | tf_op jit(solution)/shard_map/reshape | solution.py:37
  201.5 3.5 %reduce_sum.9 = f32[3,16,255]{2,1,0:T(8,128)S(1)} reduce(f32[3,16,128,255]{3,2,1,0:T(8,128)} %reshape.65, f32[]{:T(128)} %constant.4.clone.1), dimensions={2}, to_apply=%region_0.1 | reduce | flops 1554480 | bytes 6315844 | tf_op jit(solution)/shard_map/reduce_sum | solution.py:37
  205.0 0.1 pad_slice_fusion
  205.0 0.1 bitcast_select_fusion
  205.1 84.1 %psum.7 = f32[16,256]{1,0:T(8,128)S(1)} all-reduce(f32[16,256]{1,0:T(8,128)S(1)} %bitcast_select_fusion), channel_id=1, replica_groups=mesh['dp'=4,'ctx'=64] {'dp','ctx'}, use_global_device_ids=true, to_apply=%region_1.2 | all-reduce | flops 4096 | bytes 32768 | tf_op jit(solution)/shard_map/psum | solution.py:86
  289.2 0.6 broadcast_multiply_fusion
  (3 shorter events, 0.0 us)
Async XLA Ops:
  0.7 3.1 %copy-start.8 = (bf16[16,256]{1,0:T(8,128)(2,1)S(1)}, bf16[16,256]{1,0:T(8,128)(2,1)}, u32[]{:S(2)}) copy-start(bf16[16,256]{1,0:T(8,128)(2,1)} %param.10) | copy-start | bytes 24580
  0.7 3.1 %copy-start.9 = (s32[16]{0:T(128)S(1)}, s32[16]{0:T(128)}, u32[]{:S(2)}) copy-start(s32[16]{0:T(128)} %param.11) | copy-start | bytes 196
  8.2 1.6 slice-start
  12.2 1.2 copy-start.1
  21.0 47.4 %collective-permute-start.3 = (f32[1,128,4096]{2,1,0:T(8,128)}, f32[1,128,4096]{2,1,0:T(8,128)}, u32[]{:S(2)}, u32[]{:S(2)}) collective-permute-start(f32[1,128,4096]{2,1,0:T(8,128)} %copy.52), channel_id=1, source_target_pairs={{2,0},{3,1},{4,2},{5,3},{6,4},{7,5},{8,6},{9,7},{10,8},{11,9},{12,... | collective-permute-start | bytes 6291464 | tf_op jit(solution)/shard_map/ppermute | solution.py:12
  25.2 68.5 %collective-permute-start.2 = (f32[1,128,4096]{2,1,0:T(8,128)}, f32[1,128,4096]{2,1,0:T(8,128)}, u32[]{:S(2)}, u32[]{:S(2)}) collective-permute-start(f32[1,128,4096]{2,1,0:T(8,128)} %copy.50), channel_id=1, source_target_pairs={{1,0},{2,1},{3,2},{4,3},{5,4},{6,5},{7,6},{8,7},{9,8},{10,9},{11,1... | collective-permute-start | bytes 6291464 | tf_op jit(solution)/shard_map/ppermute | solution.py:12
  99.4 25.3 %collective-permute-start.1 = (bf16[1,128,4096]{2,1,0:T(8,128)(2,1)S(1)}, bf16[1,128,4096]{2,1,0:T(8,128)(2,1)}, u32[]{:S(2)}, u32[]{:S(2)}) collective-permute-start(bf16[1,128,4096]{2,1,0:T(8,128)(2,1)S(1)} %get-tuple-element.9), channel_id=1, source_target_pairs={{0,2},{1,3},{2,4},{3,5},{4,6},{5,7},{6,8},{7,9},{8,10},{9,11},{10,... | collective-permute-start | bytes 3145736 | tf_op jit(solution)/shard_map/ppermute | solution.py:12
  103.7 32.2 %collective-permute-start = (bf16[1,128,4096]{2,1,0:T(8,128)(2,1)S(1)}, bf16[1,128,4096]{2,1,0:T(8,128)(2,1)}, u32[]{:S(2)}, u32[]{:S(2)}) collective-permute-start(bf16[1,128,4096]{2,1,0:T(8,128)(2,1)S(1)} %get-tuple-element.9), channel_id=1, source_target_pairs={{0,1},{1,2},{2,3},{3,4},{4,5},{5,6},{6,7},{7,8},{8,9},{9,10},{10,1... | collective-permute-start | bytes 3145736 | tf_op jit(solution)/shard_map/ppermute | solution.py:12
  107.2 31.1 %copy-start.2 = (bf16[16,128,384]{1,2,0:T(8,128)(2,1)S(1)}, bf16[16,128,384]{1,2,0:T(8,128)(2,1)}, u32[]{:S(2)}) copy-start(bf16[16,128,384]{1,2,0:T(8,128)(2,1)} %copy-done.1) | copy-start | bytes 4718596
  135.9 2.4 copy-start.5
  138.3 4.1 %copy-start.3 = (bf16[16,8,16,256]{3,2,1,0:T(8,128)(2,1)S(1)}, bf16[16,8,16,256]{3,2,1,0:T(8,128)(2,1)}, u32[]{:S(2)}) copy-start(bf16[16,8,16,256]{3,2,1,0:T(8,128)(2,1)} %copy.68) | copy-start | bytes 3145732
  138.3 4.1 %copy-start.6 = (bf16[1,128,4096]{1,2,0:T(8,128)(2,1)S(1)}, bf16[1,128,4096]{1,2,0:T(8,128)(2,1)}, u32[]{:S(2)}) copy-start(bf16[1,128,4096]{1,2,0:T(8,128)(2,1)} %copy.46) | copy-start | bytes 3145732
  138.3 4.1 %copy-start.7 = (bf16[1,128,4096]{1,2,0:T(8,128)(2,1)S(1)}, bf16[1,128,4096]{1,2,0:T(8,128)(2,1)}, u32[]{:S(2)}) copy-start(bf16[1,128,4096]{1,2,0:T(8,128)(2,1)} %copy.45) | copy-start | bytes 3145732
  168.1 2.0 copy-start.4
  170.1 2.3 copy-start
where the time goes:
time: 292 us; the launch traced here: 290 us
  waiting for transfers between devices  88 us (30%)
  blocking collectives  84.1 us (29%)
  local copies, waits for them, and re-layouts  81.8 us (28%)
  other arithmetic  13 us (4%)
  starting transfers between devices  12.9 us (4%)
  matrix products  9.31 us (3%)
    ppermute x4, waiting for transfers between devices, shifted_2(): return lax.ppermute(block, axis, route)  88 us
    psum x1, blocking collectives, body(): grad_filters = lax.psum(local_taps, ('dp', 'ctx')) * scale  84.1 us
    rev x1, local copies, waits for them, and re-layouts, diagonal_sums(): flipped = jnp.flip(corr, -1)  20.4 us
    ppermute x4, starting transfers between devices, shifted_2(): return lax.ppermute(block, axis, route)  12.9 us
    reshape x1, local copies, waits for them, and re-layouts, diagonal_sums(): flattened.reshape(leading + (block_size, 2 * block_size - 1)).sum(axis=-2)  12.7 us
    reshape x1, local copies, waits for them, and re-layouts, diagonal_sums(): padded.reshape(leading + (2 * block_size * block_size,))  7.17 us
    unnamed x23, local copies, waits for them, and re-layouts  6.51 us
  transfers between devices with their start and end apart: 4, of which 4 were waited for; matrix products, arithmetic and copies ran while one was open for 3% of the time, Pallas kernels for 0%

commit v1 on v0

v1 whole, which is shorter than its diff:
```python
import math

import jax
import jax.numpy as jnp
from jax import lax
from jax.experimental import pallas as pl
from jax.experimental.pallas import tpu as pltpu
from jax.sharding import PartitionSpec as P

F32 = jnp.float32
BF16 = jnp.bfloat16
TOK = 128
GW = 256


def gate_product_kernel(side_ref, a_ref, b_ref, c_ref, d_ref, out_ref):
    @pl.when(side_ref[0] == 1)
    def _():
        out_ref[...] = (a_ref[...].astype(F32) * b_ref[...].astype(F32)).astype(BF16)

    @pl.when(side_ref[0] == 0)
    def _():
        out_ref[...] = (c_ref[...].astype(F32) * d_ref[...].astype(F32)).astype(BF16)


def gate_product(side, a, b, c, d, blocks):
    tok_n, chan_n = a.shape
    width = chan_n // blocks
    first = pl.BlockSpec((tok_n, width), lambda i, s: (0, i * s[0]))
    second = pl.BlockSpec((tok_n, width), lambda i, s: (0, i * (1 - s[0])))
    return pl.pallas_call(
        gate_product_kernel,
        out_shape=jax.ShapeDtypeStruct(a.shape, BF16),
        grid_spec=pltpu.PrefetchScalarGridSpec(
            num_scalar_prefetch=1,
            grid=(blocks,),
            in_specs=[first, first, second, second],
            out_specs=pl.BlockSpec((tok_n, width), lambda i, s: (0, i)),
        ),
        cost_estimate=pl.CostEstimate(flops=a.size, bytes_accessed=6 * a.size, transcendentals=0),
    )(side, a, b, c, d)


def toeplitz(edges, reaches, filters):
    group_n = filters.shape[0]
    shape = jax.ShapeDtypeStruct((group_n, TOK, 3 * TOK), BF16)
    step = 8
    block = pl.BlockSpec((step, TOK, 3 * TOK), lambda i: (i, 0, 0))
    smem = pl.BlockSpec(memory_space=pltpu.SMEM)

    def kernel(edge_ref, reach_ref, filt_ref, ahead_ref, back_ref):
        base = pl.program_id(0) * step
        row = lax.broadcasted_iota(jnp.int32, (TOK, TOK), 0)
        col = lax.broadcasted_iota(jnp.int32, (TOK, TOK), 1)
        upper = col >= row
        lag = lax.broadcasted_iota(jnp.int32, (1, 2 * TOK), 1)
        back1, back2 = edge_ref[0].astype(F32), edge_ref[1].astype(F32)
        ahead1, ahead2 = edge_ref[2].astype(F32), edge_ref[3].astype(F32)
        zero = jnp.zeros((TOK, TOK), F32)
        lines = filt_ref[...].astype(F32)
        for g in range(step):
            line = jnp.where(lag < reach_ref[base + g], lines[g : g + 1, :], 0.0)
            near, far = (
                pltpu.roll(
                    jnp.broadcast_to(part, (TOK, TOK)), 0, axis=1, stride=1, stride_axis=0
                )
                for part in (line[:, :TOK], line[:, TOK:])
            )
            w0 = jnp.where(upper, near, zero)
            w1 = jnp.where(upper, far, near)
            w2 = jnp.where(upper, zero, far)
            ahead_ref[g, :, :TOK] = w0.astype(BF16)
            ahead_ref[g, :, TOK : 2 * TOK] = (w1 * ahead1).astype(BF16)
            ahead_ref[g, :, 2 * TOK :] = (w2 * ahead2).astype(BF16)
            back_ref[g, :, :TOK] = w0.T.astype(BF16)
            back_ref[g, :, TOK : 2 * TOK] = (w1 * back1).T.astype(BF16)
            back_ref[g, :, 2 * TOK :] = (w2 * back2).T.astype(BF16)

    return pl.pallas_call(
        kernel,
        out_shape=[shape, shape],
        grid=(group_n // step,),
        in_specs=[smem, smem, pl.BlockSpec((step, 2 * TOK), lambda i: (i, 0))],
        out_specs=[block, block],
        cost_estimate=pl.CostEstimate(
            flops=8 * group_n * TOK * TOK, bytes_accessed=12 * group_n * TOK * TOK, transcendentals=0
        ),
    )(edges, reaches, filters)


def taps_kernel(scale, step, flag_ref, reach_ref, mine_p, mine_x, got_p, got_x, out_ref):
    base = pl.program_id(0) * step
    row = lax.broadcasted_iota(jnp.int32, (TOK, TOK), 0)
    col = lax.broadcasted_iota(jnp.int32, (TOK, TOK), 1)
    upper = col >= row
    sub = lax.broadcasted_iota(jnp.int32, (8, TOK), 0)
    lane = lax.broadcasted_iota(jnp.int32, (1, TOK), 1)
    near_ok, far_ok = flag_ref[1].astype(F32), flag_ref[2].astype(F32)

    def diagonals(tile):
        acc = tile[0:8, :]
        for k in range(1, TOK // 8):
            acc = acc + pltpu.roll(tile[8 * k : 8 * k + 8, :], TOK - 8 * k, axis=1)
        for bit in (1, 2, 4):
            acc = jnp.where((sub & bit) != 0, pltpu.roll(acc, TOK - bit, axis=1), acc)
        return jnp.sum(acc, axis=0, keepdims=True)

    def pair(a, b):
        return lax.dot_general(a, b, (((1,), (1,)), ((), ())), preferred_element_type=F32)

    def work(sig, sig_back, dcv, dcv_ahead):
        for g in range(step):
            at = slice(g * GW, (g + 1) * GW)
            c0 = pair(sig[:, at], dcv[:, at])
            c1 = pair(sig_back[:, at], dcv[:, at]) * near_ok
            c2 = pair(sig_back[:, at], dcv_ahead[:, at]) * far_ok
            low = diagonals(jnp.where(upper, c0, c1))
            high = diagonals(jnp.where(upper, c1, c2))
            reach = reach_ref[base + g]
            out_ref[g : g + 1, :TOK] = jnp.where(lane < reach, low * scale, 0.0)
            out_ref[g : g + 1, TOK:] = jnp.where(lane + TOK < reach, high * scale, 0.0)

    @pl.when(flag_ref[0] == 1)
    def _():
        work(mine_p, got_x, mine_x, got_p)

    @pl.when(flag_ref[0] == 0)
    def _():
        work(mine_x, got_p, mine_p, got_x)


def taps(scale, flags, reaches, mine_p, mine_x, got_p, got_x):
    group_n = reaches.shape[0]
    step = 8
    smem = pl.BlockSpec(memory_space=pltpu.SMEM)
    block = pl.BlockSpec((TOK, step * GW), lambda i: (0, i))

    def kernel(*refs):
        taps_kernel(scale, step, *refs)

    return pl.pallas_call(
        kernel,
        out_shape=jax.ShapeDtypeStruct((group_n, 2 * TOK), F32),
        grid=(group_n // step,),
        in_specs=[smem, smem] + [block] * 4,
        out_specs=pl.BlockSpec((step, 2 * TOK), lambda i: (i, 0)),
        cost_estimate=pl.CostEstimate(
            flops=6 * group_n * TOK * TOK * GW, bytes_accessed=8 * mine_p.size, transcendentals=0
        ),
    )(flags, reaches, mine_p, mine_x, got_p, got_x)


def grads_piece(flags, ahead, back, fields, gates, outs, first, count, step):
    tok_n, chan_n = gates[0].shape
    smem = pl.BlockSpec(memory_space=pltpu.SMEM)
    start = first // step
    cols = pl.BlockSpec((tok_n, step * GW), lambda i: (0, i + start))
    mats = pl.BlockSpec((step, TOK, 3 * TOK), lambda i: (i + start, 0, 0))

    def kernel(flag_ref, ahead_ref, back_ref, *refs):
        mine_p, mine_x, got_p, got_x, got2_p, got2_x, grad, kpart, vpart = refs[:9]
        gq, gk, gv = refs[-3:]

        def dot(a, b):
            return jnp.dot(a, b, preferred_element_type=F32)

        def work(sig, sig1, sig2, dcv, dcv1, dcv2):
            for g in range(step):
                at = slice(g * GW, (g + 1) * GW)
                conv = (
                    dot(back_ref[g, :, :TOK], sig[:, at])
                    + dot(back_ref[g, :, TOK : 2 * TOK], sig1[:, at])
                    + dot(back_ref[g, :, 2 * TOK :], sig2[:, at])
                )
                gq[:, at] = (grad[:, at].astype(F32) * conv).astype(BF16)
                dsig = (
                    dot(ahead_ref[g, :, :TOK], dcv[:, at])
                    + dot(ahead_ref[g, :, TOK : 2 * TOK], dcv1[:, at])
                    + dot(ahead_ref[g, :, 2 * TOK :], dcv2[:, at])
                )
                gk[:, at] = (dsig * vpart[:, at].astype(F32)).astype(BF16)
                gv[:, at] = (dsig * kpart[:, at].astype(F32)).astype(BF16)

        @pl.when(flag_ref[0] == 1)
        def _():
            work(mine_p, got_x, got2_x, mine_x, got_p, got2_p)

        @pl.when(flag_ref[0] == 0)
        def _():
            work(mine_x, got_p, got2_p, mine_p, got_x, got2_x)

    shape = jax.ShapeDtypeStruct((tok_n, chan_n), BF16)
    earlier = [] if outs is None else list(outs)
    part = count * TOK * GW
    return pl.pallas_call(
        kernel,
        out_shape=[shape] * 3,
        grid=(count // step,),
        in_specs=[smem, mats, mats] + [cols] * 9 + [pl.BlockSpec(memory_space=pl.ANY)] * len(earlier),
        out_specs=[cols] * 3,
        input_output_aliases={12 + i: i for i in range(len(earlier))},
        cost_estimate=pl.CostEstimate(
            flops=12 * part * TOK, bytes_accessed=27 * part, transcendentals=0
        ),
    )(flags, ahead, back, *fields, *gates, *earlier)


def body(q_proj, k_proj, v_proj, out_grad, filters, reaches):
    batch_n, tok_n, chan_n = q_proj.shape
    group_n = filters.shape[0]
    ctx_n, dp_n = lax.axis_size("ctx"), lax.axis_size("dp")
    scale = 1.0 / math.sqrt(batch_n * dp_n * tok_n * ctx_n * (chan_n // group_n))
    q, k, v, grad = (x.reshape(tok_n, chan_n) for x in (q_proj, k_proj, v_proj, out_grad))

    me = lax.axis_index("ctx")
    odd = (me & 1).astype(jnp.int32)
    flags = jnp.stack([odd, me > 0, (me > 0) & (me < ctx_n - 1)]).astype(jnp.int32)
    edges = jnp.stack([me > 0, me > 1, me < ctx_n - 1, me < ctx_n - 2]).astype(jnp.int32)

    across = [(i, (i + 1) % ctx_n if i & 1 else (i - 1) % ctx_n) for i in range(ctx_n)]
    within = [(i, i ^ 1) for i in range(ctx_n)]

    mine_p = gate_product(odd[None], k, v, grad, q, 8)
    got_p = lax.ppermute(mine_p, "ctx", across)
    mine_x = gate_product(odd[None], grad, q, k, v, 8)
    got_x = lax.ppermute(mine_x, "ctx", within)
    got2_p = lax.ppermute(got_x, "ctx", across)
    ahead, back = toeplitz(edges, reaches, filters)
    local = taps(scale, flags, reaches, mine_p, mine_x, got_p, got_x)
    got2_x = lax.ppermute(got_p, "ctx", within)

    def trade_ctx(x, mask):
        return x + lax.ppermute(x, "ctx", [(i, i ^ mask) for i in range(ctx_n)])

    def trade_dp(x, mask):
        route = [
            (d * ctx_n + i, (d ^ mask) * ctx_n + (i ^ 1)) for d in range(dp_n) for i in range(ctx_n)
        ]
        return x + lax.ppermute(x, ("dp", "ctx"), route)

    total = trade_ctx(local, 1)
    total = trade_dp(total, 1)
    total = trade_dp(total, 3)
    total = trade_ctx(total, 8 | 1)
    outs = None
    fields = (mine_p, mine_x, got_p, got_x, got2_p, got2_x)
    pieces = 4
    for at, mask in enumerate((16 | 1, 56 | 1, 2 | 1, 6 | 1)):
        total, fields = lax.optimization_barrier((total, fields))
        outs = grads_piece(
            flags, ahead, back, fields, (grad, k, v), outs,
            at * group_n // pieces, group_n // pieces, 2,
        )
        total = trade_ctx(total, mask)
        total, outs = lax.optimization_barrier((total, outs))
    shaped = [x.reshape(batch_n, tok_n, chan_n) for x in outs]
    return (*shaped, total)


def solution(mesh):
    block = P("dp", "ctx", None)
    return jax.shard_map(
        body,
        mesh=mesh,
        in_specs=(block, block, block, block, P(), P()),
        out_specs=(block, block, block, P()),
        check_vma=False,
    )
```

time: 292 us -> 69.6 us (0.24)
  blocking collectives: 84.1 us -> 0 us
  waiting for transfers between devices: 88 us -> 7.01 us
  local copies, waits for them, and re-layouts: 81.8 us -> 1.11 us
  Pallas kernels: 0 us -> 30.8 us
  starting transfers between devices: 12.9 us -> 26.3 us
  other arithmetic: 13 us -> 2.76 us
  matrix products: 9.31 us -> 0 us
    psum x1 -> x0, blocking collectives: 84.1 us -> none  [body(): grad_filters = lax.psum(local_taps, ('dp', 'ctx')) * scale]
    ppermute x4 -> x12, waiting for transfers between devices: 88 us -> 7.01 us  [the longest x2 4.18 us: trade_dp(): return x + lax.ppermute(x, ('dp', 'ctx'), route)]
    pallas_call x0 -> x8, Pallas kernels: none -> 30.8 us  [the longest x4 12.4 us: grads_piece(): pl.pallas_call(kernel, out_shape=[shape] * 3, grid=(count // step,), in_s...]
    reshape x4 -> x0, local copies, waits for them, and re-layouts: 25.9 us -> none  [the longest x1 12.7 us: diagonal_sums(): flattened.reshape(leading + (block_size, 2 * block_size - 1)).sum(axis=-2)]
    rev x1 -> x0, local copies, waits for them, and re-layouts: 20.4 us -> none  [diagonal_sums(): flipped = jnp.flip(corr, -1)]
    ppermute x4 -> x12, starting transfers between devices: 12.9 us -> 26.3 us  [the longest x6 7.03 us: trade_ctx(): return x + lax.ppermute(x, 'ctx', [(i, i ^ mask) for i in range(ctx_n)])]
    slice x7 -> x0, local copies, waits for them, and re-layouts: 11.6 us -> none  [the longest x1 5.82 us: diagonal_sums(): padded.reshape(leading + (2 * block_size * block_size,))]
    dot_general x3 -> x0, matrix products: 9.31 us -> none  [the longest x1 4.04 us: body(): jnp.einsum('mgab,mnbgc->nagc', kernels, sig_blocks, preferred_element_typ...]
  transfers between devices with their start and end apart: 4 -> 12, of which waited for: 4 -> 7; matrix products, arithmetic and copies ran while one was open for 3% -> 3% of each run, Pallas kernels for 0% -> 36%
where the time goes in v1:
time: 69.6 us; the launch traced here: 68.7 us
  Pallas kernels  30.8 us (44%)
  starting transfers between devices  26.3 us (38%)
  waiting for transfers between devices  7.01 us (10%)
  other arithmetic  2.76 us (4%)
  local copies, waits for them, and re-layouts  1.11 us (2%)
  between operations  0.72 us (1%)
    pallas_call x4, Pallas kernels, grads_piece(): pl.pallas_call(kernel, out_shape=[shape] * 3, grid=(count // step,), in_s...  12.4 us
    pallas_call x2, Pallas kernels, gate_product(): pl.pallas_call(gate_product_kernel, out_shape=jax.ShapeDtypeStruct(a.shap...  11.5 us
    ppermute x6, starting transfers between devices, trade_ctx(): return x + lax.ppermute(x, 'ctx', [(i, i ^ mask) for i in range(ctx_n)])  7.03 us
    ppermute x1, starting transfers between devices, body(): got_x = lax.ppermute(mine_x, 'ctx', within)  6.56 us
    ppermute x1, starting transfers between devices, body(): got2_x = lax.ppermute(got_p, 'ctx', within)  6.3 us
    ppermute x2, waiting for transfers between devices, trade_dp(): return x + lax.ppermute(x, ('dp', 'ctx'), route)  4.18 us
    pallas_call x1, Pallas kernels, taps(): pl.pallas_call(kernel, out_shape=jax.ShapeDtypeStruct((group_n, 2 * TOK),...  3.89 us
    ppermute x2, starting transfers between devices, trade_dp(): return x + lax.ppermute(x, ('dp', 'ctx'), route)  3.76 us
  transfers between devices with their start and end apart: 12, of which 7 were waited for; matrix products, arithmetic and copies ran while one was open for 3% of the time, Pallas kernels for 36%

profile of v1, /device:TPU:1, one launch (start us, length us, event | category | flops | bytes accessed | tf_op | source)
XLA Modules:
  0.0 68.7 jit_solution(8797223398144938377)
XLA Ops:
  0.6 5.8 %shard_map.93.refs_2_.refs_0_ = bf16[128,4096]{1,0:T(8,128)(2,1)} custom-call(s32[1]{0:T(128)} %bitcast.side_ref, bf16[128,4096]{1,0:T(8,128)(2,1)} %bitcast.13, bf16[128,4096]{1,0:T(8,128)(2,1)} %bitcast.19, bf16[128,4096]{1,0:T(8,128)(2,1)} %bitcast.25, bf16[128,4096]{1,0:T(8,128)(2,1)} %bitcast.34), custom_call_target="tpu_custom_call" | custom-call | flops 524288 | bytes 3145728 | tf_op jit(solution)/shard_map/pallas_call | solution.py:31
  6.4 2.7 %collective-permute-start = (bf16[128,4096]{1,0:T(8,128)(2,1)}, bf16[128,4096]{1,0:T(8,128)(2,1)S(1)}, u32[]{:S(2)}, u32[]{:S(2)}) collective-permute-start(bf16[128,4096]{1,0:T(8,128)(2,1)} %shard_map.93.refs_2_.refs_0_), channel_id=1, source_target_pairs={{0,63},{1,2},{2,1},{3,4},{4,3},{5,6},{6,5},{7,8},{8,7},{9,10},{10,... | collective-permute-start | bytes 3145736 | tf_op jit(solution)/shard_map/ppermute | solution.py:224
  9.1 5.8 %shard_map.94.refs_3_.refs_1_ = bf16[128,4096]{1,0:T(8,128)(2,1)} custom-call(s32[1]{0:T(128)} %bitcast.side_ref, bf16[128,4096]{1,0:T(8,128)(2,1)} %bitcast.26, bf16[128,4096]{1,0:T(8,128)(2,1)} %bitcast.35, bf16[128,4096]{1,0:T(8,128)(2,1)} %bitcast.14, bf16[128,4096]{1,0:T(8,128)(2,1)} %bitcast.20), custom_call_target="tpu_custom_call" | custom-call | flops 524288 | bytes 3145728 | tf_op jit(solution)/shard_map/pallas_call | solution.py:31
  14.8 6.6 %collective-permute-start.1 = (bf16[128,4096]{1,0:T(8,128)(2,1)}, bf16[128,4096]{1,0:T(8,128)(2,1)S(1)}, u32[]{:S(2)}, u32[]{:S(2)}) collective-permute-start(bf16[128,4096]{1,0:T(8,128)(2,1)} %shard_map.94.refs_3_.refs_1_), channel_id=1, source_target_pairs={{0,1},{1,0},{2,3},{3,2},{4,5},{5,4},{6,7},{7,6},{8,9},{9,8},{10,11... | collective-permute-start | bytes 3145736 | tf_op jit(solution)/shard_map/ppermute | solution.py:226
  21.4 0.7 collective-permute-done.refs_4_.refs_2_
  22.1 0.0 copy-start
  22.1 6.3 %collective-permute-start.7 = (bf16[128,4096]{1,0:T(8,128)(2,1)S(1)}, bf16[128,4096]{1,0:T(8,128)(2,1)S(1)}, u32[]{:S(2)}, u32[]{:S(2)}) collective-permute-start(bf16[128,4096]{1,0:T(8,128)(2,1)S(1)} %collective-permute-done.refs_4_.refs_2_), channel_id=1, source_target_pairs={{0,1},{1,0},{2,3},{3,2},{4,5},{5,4},{6,7},{7,6},{8,9},{9,8},{10,11... | collective-permute-start | bytes 3145736 | tf_op jit(solution)/shard_map/ppermute | solution.py:230
  28.4 0.0 collective-permute-done.1.refs_5_.refs_3_
  28.4 0.0 copy-start.1
  28.4 0.0 collective-permute-start.6
  28.4 0.8 %pad_add_fusion.refs_0_.flag_ref = s32[3]{0:T(128)} fusion(s32[1]{0:T(128)} %bitcast.2, s32[1]{0:T(128)S(6)} %stack.33, s32[1]{0:T(128)} %bitcast.side_ref), kind=kLoop, calls=%fused_computation.1 | loop fusion | flops 6 | bytes 24 | tf_op jit(solution)/shard_map/stack | solution.py:217
  29.2 0.0 copy-done
  29.2 0.2 copy-done.1
  29.3 3.9 %shard_map.95 = f32[16,256]{1,0:T(8,128)} custom-call(s32[3]{0:T(128)} %pad_add_fusion.refs_0_.flag_ref, s32[16]{0:T(128)} %reach_ref.1, bf16[128,4096]{1,0:T(8,128)(2,1)} %shard_map.93.refs_2_.refs_0_, bf16[128,4096]{1,0:T(8,128)(2,1)} %shard_map.94.refs_3_.refs_1_, bf16[128,4096]{1,0:T(8,128)(2,1)} %copy-done, bf16[128,4096]{1,0:T(8,128)(2,1)} %copy-done.1), custom_call_target="tpu_custom_call" | custom-call | flops 402653184 | bytes 4194304 | tf_op jit(solution)/shard_map/pallas_call | solution.py:141
  33.2 4.9 %collective-permute-start.2 = (f32[16,256]{1,0:T(8,128)}, f32[16,256]{1,0:T(8,128)S(1)}, u32[]{:S(2)}, u32[]{:S(2)}) collective-permute-start(f32[16,256]{1,0:T(8,128)} %shard_map.95), channel_id=1, source_target_pairs={{0,1},{1,0},{2,3},{3,2},{4,5},{5,4},{6,7},{7,6},{8,9},{9,8},{10,11... | collective-permute-start | bytes 49160 | tf_op jit(solution)/shard_map/ppermute | solution.py:233
  38.1 1.0 %collective-permute-done.2 = f32[16,256]{1,0:T(8,128)S(1)} collective-permute-done((f32[16,256]{1,0:T(8,128)}, f32[16,256]{1,0:T(8,128)S(1)}, u32[]{:S(2)}, u32[]{:S(2)}) %collective-permute-start.2) | collective-permute-done | bytes 16416 | tf_op jit(solution)/shard_map/ppermute | solution.py:233
  39.2 0.7 %add.24 = f32[16,256]{1,0:T(8,128)S(1)} add(f32[16,256]{1,0:T(8,128)} %shard_map.95, f32[16,256]{1,0:T(8,128)S(1)} %collective-permute-done.2) | non-fusion elementwise | flops 4096 | bytes 49152 | tf_op jit(solution)/shard_map/add | solution.py:233
  39.9 1.4 %collective-permute-start.3 = (f32[16,256]{1,0:T(8,128)S(1)}, f32[16,256]{1,0:T(8,128)S(1)}, u32[]{:S(2)}, u32[]{:S(2)}) collective-permute-start(f32[16,256]{1,0:T(8,128)S(1)} %add.24), channel_id=1, source_target_pairs={{0,65},{1,64},{2,67},{3,66},{4,69},{5,68},{6,71},{7,70},{8,73},{9,... | collective-permute-start | bytes 49160 | tf_op jit(solution)/shard_map/ppermute | solution.py:239
  41.3 2.1 %collective-permute-done.3 = f32[16,256]{1,0:T(8,128)S(1)} collective-permute-done((f32[16,256]{1,0:T(8,128)S(1)}, f32[16,256]{1,0:T(8,128)S(1)}, u32[]{:S(2)}, u32[]{:S(2)}) %collective-permute-start.3) | collective-permute-done | bytes 16416 | tf_op jit(solution)/shard_map/ppermute | solution.py:239
  43.4 2.3 %collective-permute-start.4 = (f32[16,256]{1,0:T(8,128)S(1)}, f32[16,256]{1,0:T(8,128)S(1)}, u32[]{:S(2)}, u32[]{:S(2)}) collective-permute-start(f32[16,256]{1,0:T(8,128)S(1)} %add.25), channel_id=1, source_target_pairs={{0,193},{1,192},{2,195},{3,194},{4,197},{5,196},{6,199},{7,198},{8... | collective-permute-start | bytes 49160 | tf_op jit(solution)/shard_map/ppermute | solution.py:239
  45.8 2.1 %collective-permute-done.4 = f32[16,256]{1,0:T(8,128)S(1)} collective-permute-done((f32[16,256]{1,0:T(8,128)S(1)}, f32[16,256]{1,0:T(8,128)S(1)}, u32[]{:S(2)}, u32[]{:S(2)}) %collective-permute-start.4) | collective-permute-done | bytes 16416 | tf_op jit(solution)/shard_map/ppermute | solution.py:239
  47.8 0.0 collective-permute-start.5
  47.8 0.6 add_convert_fusion.edge_ref
  48.4 3.0 %shard_map.96 = (bf16[16,128,384]{2,1,0:T(8,128)(2,1)}, bf16[16,128,384]{2,1,0:T(8,128)(2,1)}) custom-call(s32[4]{0:T(128)} %add_convert_fusion.edge_ref, s32[16]{0:T(128)} %reach_ref.1, bf16[16,256]{1,0:T(8,128)(2,1)} %filt_ref.1), custom_call_target="tpu_custom_call" | custom-call | flops 2097152 | bytes 3145728 | tf_op jit(solution)/shard_map/pallas_call | solution.py:79
  51.4 0.0 collective-permute-done.5
  51.5 0.0 collective-permute-done.7.refs_5_
  51.5 0.0 copy-start.2
  51.5 0.0 collective-permute-done.6.refs_4_
  51.5 0.1 collective-permute-start.8
  51.6 0.9 %copy-done.2 = bf16[128,4096]{1,0:T(8,128)(2,1)} copy-done((bf16[128,4096]{1,0:T(8,128)(2,1)}, bf16[128,4096]{1,0:T(8,128)(2,1)S(1)}, u32[]{:S(2)}) %copy-start.2) | copy-done | bytes 1048600
  52.5 3.1 %shard_map.97 = (bf16[128,4096]{1,0:T(8,128)(2,1)}, bf16[128,4096]{1,0:T(8,128)(2,1)}, bf16[128,4096]{1,0:T(8,128)(2,1)}) custom-call(s32[3]{0:T(128)} %pad_add_fusion.refs_0_.flag_ref, bf16[16,128,384]{2,1,0:T(8,128)(2,1)} %get-tuple-element.63.ahead_ref, bf16[16,128,384]{2,1,0:T(8,128)(2,1)} %get-tuple-element.64.back_ref, ...), custom_call_target="tpu_custom_call" | custom-call | flops 201326592 | bytes 3538944 | tf_op jit(solution)/shard_map/pallas_call | solution.py:195
  55.6 0.0 collective-permute-done.8
  55.6 1.0 %collective-permute-start.9 = (f32[16,256]{1,0:T(8,128)S(1)}, f32[16,256]{1,0:T(8,128)S(1)}, u32[]{:S(2)}, u32[]{:S(2)}) collective-permute-start(f32[16,256]{1,0:T(8,128)S(1)} %add.28), channel_id=1, source_target_pairs={{0,57},{1,56},{2,59},{3,58},{4,61},{5,60},{6,63},{7,62},{8,49},{9,... | collective-permute-start | bytes 49160 | tf_op jit(solution)/shard_map/ppermute | solution.py:233
  56.6 3.1 %shard_map.98 = (bf16[128,4096]{1,0:T(8,128)(2,1)}, bf16[128,4096]{1,0:T(8,128)(2,1)}, bf16[128,4096]{1,0:T(8,128)(2,1)}) custom-call(s32[3]{0:T(128)} %pad_add_fusion.refs_0_.flag_ref, bf16[16,128,384]{2,1,0:T(8,128)(2,1)} %get-tuple-element.63.ahead_ref, ...), custom_call_target="tpu_custom_call", output_to_operand_aliasing={{0}: (12, {}), {1}: (13, {}), {2}: (14, {})} | custom-call | flops 201326592 | bytes 3538944 | tf_op jit(solution)/shard_map/pallas_call | solution.py:195
  59.7 0.4 collective-permute-done.9
  60.1 0.0 collective-permute-start.10
  60.1 3.1 %shard_map.99 = (bf16[128,4096]{1,0:T(8,128)(2,1)}, bf16[128,4096]{1,0:T(8,128)(2,1)}, bf16[128,4096]{1,0:T(8,128)(2,1)}) custom-call(s32[3]{0:T(128)} %pad_add_fusion.refs_0_.flag_ref, bf16[16,128,384]{2,1,0:T(8,128)(2,1)} %get-tuple-element.63.ahead_ref, ...), custom_call_target="tpu_custom_call", output_to_operand_aliasing={{0}: (12, {}), {1}: (13, {}), {2}: (14, {})} | custom-call | flops 201326592 | bytes 3538944 | tf_op jit(solution)/shard_map/pallas_call | solution.py:195
  63.2 0.5 collective-permute-done.10
  63.7 1.1 %collective-permute-start.11 = (f32[16,256]{1,0:T(8,128)S(1)}, f32[16,256]{1,0:T(8,128)S(1)}, u32[]{:S(2)}, u32[]{:S(2)}) collective-permute-start(f32[16,256]{1,0:T(8,128)S(1)} %add.30), channel_id=1, source_target_pairs={{0,7},{1,6},{2,5},{3,4},{4,3},{5,2},{6,1},{7,0},{8,15},{9,14},{10,... | collective-permute-start | bytes 49160 | tf_op jit(solution)/shard_map/ppermute | solution.py:233
  64.8 3.1 %shard_map.100 = (bf16[128,4096]{1,0:T(8,128)(2,1)}, bf16[128,4096]{1,0:T(8,128)(2,1)}, bf16[128,4096]{1,0:T(8,128)(2,1)}) custom-call(s32[3]{0:T(128)} %pad_add_fusion.refs_0_.flag_ref, bf16[16,128,384]{2,1,0:T(8,128)(2,1)} %get-tuple-element.63.ahead_ref, ...), custom_call_target="tpu_custom_call", output_to_operand_aliasing={{0}: (12, {}), {1}: (13, {}), {2}: (14, {})} | custom-call | flops 201326592 | bytes 3538944 | tf_op jit(solution)/shard_map/pallas_call | solution.py:195
  67.9 0.2 collective-permute-done.11
  68.1 0.6 add.31
  (6 shorter events, 0.0 us)
Async XLA Ops:
  6.4 15.6 %collective-permute-start = (bf16[128,4096]{1,0:T(8,128)(2,1)}, bf16[128,4096]{1,0:T(8,128)(2,1)S(1)}, u32[]{:S(2)}, u32[]{:S(2)}) collective-permute-start(bf16[128,4096]{1,0:T(8,128)(2,1)} %shard_map.93.refs_2_.refs_0_), channel_id=1, source_target_pairs={{0,63},{1,2},{2,1},{3,4},{4,3},{5,6},{6,5},{7,8},{8,7},{9,10},{10,... | collective-permute-start | bytes 3145736 | tf_op jit(solution)/shard_map/ppermute | solution.py:224
  14.8 13.5 %collective-permute-start.1 = (bf16[128,4096]{1,0:T(8,128)(2,1)}, bf16[128,4096]{1,0:T(8,128)(2,1)S(1)}, u32[]{:S(2)}, u32[]{:S(2)}) collective-permute-start(bf16[128,4096]{1,0:T(8,128)(2,1)} %shard_map.94.refs_3_.refs_1_), channel_id=1, source_target_pairs={{0,1},{1,0},{2,3},{3,2},{4,5},{5,4},{6,7},{7,6},{8,9},{9,8},{10,11... | collective-permute-start | bytes 3145736 | tf_op jit(solution)/shard_map/ppermute | solution.py:226
  22.1 7.1 %copy-start = (bf16[128,4096]{1,0:T(8,128)(2,1)}, bf16[128,4096]{1,0:T(8,128)(2,1)S(1)}, u32[]{:S(2)}) copy-start(bf16[128,4096]{1,0:T(8,128)(2,1)S(1)} %collective-permute-done.refs_4_.refs_2_) | copy-start | bytes 3145732
  22.1 29.4 %collective-permute-start.7 = (bf16[128,4096]{1,0:T(8,128)(2,1)S(1)}, bf16[128,4096]{1,0:T(8,128)(2,1)S(1)}, u32[]{:S(2)}, u32[]{:S(2)}) collective-permute-start(bf16[128,4096]{1,0:T(8,128)(2,1)S(1)} %collective-permute-done.refs_4_.refs_2_), channel_id=1, source_target_pairs={{0,1},{1,0},{2,3},{3,2},{4,5},{5,4},{6,7},{7,6},{8,9},{9,8},{10,11... | collective-permute-start | bytes 3145736 | tf_op jit(solution)/shard_map/ppermute | solution.py:230
  28.4 1.0 %copy-start.1 = (bf16[128,4096]{1,0:T(8,128)(2,1)}, bf16[128,4096]{1,0:T(8,128)(2,1)S(1)}, u32[]{:S(2)}) copy-start(bf16[128,4096]{1,0:T(8,128)(2,1)S(1)} %collective-permute-done.1.refs_5_.refs_3_) | copy-start | bytes 3145732
  28.4 23.1 %collective-permute-start.6 = (bf16[128,4096]{1,0:T(8,128)(2,1)S(1)}, bf16[128,4096]{1,0:T(8,128)(2,1)}, u32[]{:S(2)}, u32[]{:S(2)}) collective-permute-start(bf16[128,4096]{1,0:T(8,128)(2,1)S(1)} %collective-permute-done.1.refs_5_.refs_3_), channel_id=1, source_target_pairs={{0,63},{1,2},{2,1},{3,4},{4,3},{5,6},{6,5},{7,8},{8,7},{9,10},{10,... | collective-permute-start | bytes 3145736 | tf_op jit(solution)/shard_map/ppermute | solution.py:227
  33.2 5.9 %collective-permute-start.2 = (f32[16,256]{1,0:T(8,128)}, f32[16,256]{1,0:T(8,128)S(1)}, u32[]{:S(2)}, u32[]{:S(2)}) collective-permute-start(f32[16,256]{1,0:T(8,128)} %shard_map.95), channel_id=1, source_target_pairs={{0,1},{1,0},{2,3},{3,2},{4,5},{5,4},{6,7},{7,6},{8,9},{9,8},{10,11... | collective-permute-start | bytes 49160 | tf_op jit(solution)/shard_map/ppermute | solution.py:233
  39.9 3.6 %collective-permute-start.3 = (f32[16,256]{1,0:T(8,128)S(1)}, f32[16,256]{1,0:T(8,128)S(1)}, u32[]{:S(2)}, u32[]{:S(2)}) collective-permute-start(f32[16,256]{1,0:T(8,128)S(1)} %add.24), channel_id=1, source_target_pairs={{0,65},{1,64},{2,67},{3,66},{4,69},{5,68},{6,71},{7,70},{8,73},{9,... | collective-permute-start | bytes 49160 | tf_op jit(solution)/shard_map/ppermute | solution.py:239
  43.4 4.4 %collective-permute-start.4 = (f32[16,256]{1,0:T(8,128)S(1)}, f32[16,256]{1,0:T(8,128)S(1)}, u32[]{:S(2)}, u32[]{:S(2)}) collective-permute-start(f32[16,256]{1,0:T(8,128)S(1)} %add.25), channel_id=1, source_target_pairs={{0,193},{1,192},{2,195},{3,194},{4,197},{5,196},{6,199},{7,198},{8... | collective-permute-start | bytes 49160 | tf_op jit(solution)/shard_map/ppermute | solution.py:239
  47.8 3.6 %collective-permute-start.5 = (f32[16,256]{1,0:T(8,128)S(1)}, f32[16,256]{1,0:T(8,128)S(1)}, u32[]{:S(2)}, u32[]{:S(2)}) collective-permute-start(f32[16,256]{1,0:T(8,128)S(1)} %add.26), channel_id=1, source_target_pairs={{0,9},{1,8},{2,11},{3,10},{4,13},{5,12},{6,15},{7,14},{8,1},{9,0},... | collective-permute-start | bytes 49160 | tf_op jit(solution)/shard_map/ppermute | solution.py:233
  51.5 1.1 %copy-start.2 = (bf16[128,4096]{1,0:T(8,128)(2,1)}, bf16[128,4096]{1,0:T(8,128)(2,1)S(1)}, u32[]{:S(2)}) copy-start(bf16[128,4096]{1,0:T(8,128)(2,1)S(1)} %collective-permute-done.7.refs_5_) | copy-start | bytes 3145732
  51.5 4.2 %collective-permute-start.8 = (f32[16,256]{1,0:T(8,128)S(1)}, f32[16,256]{1,0:T(8,128)S(1)}, u32[]{:S(2)}, u32[]{:S(2)}) collective-permute-start(f32[16,256]{1,0:T(8,128)S(1)} %add.27), channel_id=1, source_target_pairs={{0,17},{1,16},{2,19},{3,18},{4,21},{5,20},{6,23},{7,22},{8,25},{9,... | collective-permute-start | bytes 49160 | tf_op jit(solution)/shard_map/ppermute | solution.py:233
  55.6 4.5 %collective-permute-start.9 = (f32[16,256]{1,0:T(8,128)S(1)}, f32[16,256]{1,0:T(8,128)S(1)}, u32[]{:S(2)}, u32[]{:S(2)}) collective-permute-start(f32[16,256]{1,0:T(8,128)S(1)} %add.28), channel_id=1, source_target_pairs={{0,57},{1,56},{2,59},{3,58},{4,61},{5,60},{6,63},{7,62},{8,49},{9,... | collective-permute-start | bytes 49160 | tf_op jit(solution)/shard_map/ppermute | solution.py:233
  60.1 3.6 %collective-permute-start.10 = (f32[16,256]{1,0:T(8,128)S(1)}, f32[16,256]{1,0:T(8,128)S(1)}, u32[]{:S(2)}, u32[]{:S(2)}) collective-permute-start(f32[16,256]{1,0:T(8,128)S(1)} %add.29), channel_id=1, source_target_pairs={{0,3},{1,2},{2,1},{3,0},{4,7},{5,6},{6,5},{7,4},{8,11},{9,10},{10,... | collective-permute-start | bytes 49160 | tf_op jit(solution)/shard_map/ppermute | solution.py:233
  63.7 4.4 %collective-permute-start.11 = (f32[16,256]{1,0:T(8,128)S(1)}, f32[16,256]{1,0:T(8,128)S(1)}, u32[]{:S(2)}, u32[]{:S(2)}) collective-permute-start(f32[16,256]{1,0:T(8,128)S(1)} %add.30), channel_id=1, source_target_pairs={{0,7},{1,6},{2,5},{3,4},{4,3},{5,2},{6,1},{7,0},{8,15},{9,14},{10,... | collective-permute-start | bytes 49160 | tf_op jit(solution)/shard_map/ppermute | solution.py:233

commit v2 on v1

v2 whole, which is shorter than its diff:
```python
import math

import jax
import jax.numpy as jnp
from jax import lax
from jax.experimental import pallas as pl
from jax.experimental.pallas import tpu as pltpu
from jax.sharding import PartitionSpec as P

F32 = jnp.float32
BF16 = jnp.bfloat16
TOK = 128
GW = 256


def whole():
    return pl.BlockSpec(memory_space=pltpu.VMEM)


def smem():
    return pl.BlockSpec(memory_space=pltpu.SMEM)


def params(mib):
    return pltpu.CompilerParams(vmem_limit_bytes=mib * 2**20)


def gate_product(me, a, b, c, d, chunks, flops):
    tok_n, chan_n = a.shape
    parts = 4
    rows = tok_n // parts
    width = chan_n // chunks

    def kernel(me_ref, a_ref, b_ref, c_ref, d_ref, *refs):
        outs, (left, right, sems) = refs[:chunks], refs[chunks:]

        def run(x_ref, y_ref):
            copies = []
            for i in range(parts):
                at = pl.ds(i * rows, rows)
                pair = (
                    pltpu.make_async_copy(x_ref.at[at], left.at[at], sems.at[0, i]),
                    pltpu.make_async_copy(y_ref.at[at], right.at[at], sems.at[1, i]),
                )
                for copy in pair:
                    copy.start()
                copies.append(pair)
            for i, pair in enumerate(copies):
                for copy in pair:
                    copy.wait()
                at = pl.ds(i * rows, rows)
                for j, out in enumerate(outs):
                    cols = pl.ds(j * width, width)
                    prod = left[at, cols].astype(F32) * right[at, cols].astype(F32)
                    out[at, :] = prod.astype(BF16)

        odd = (me_ref[0] & 1) == 1

        @pl.when(odd)
        def _():
            run(a_ref, b_ref)

        @pl.when(jnp.logical_not(odd))
        def _():
            run(c_ref, d_ref)

    fixed = (pltpu.with_memory_space_constraint(x, pltpu.HBM) for x in (a, b, c, d))
    return pl.pallas_call(
        kernel,
        out_shape=[jax.ShapeDtypeStruct((tok_n, width), BF16)] * chunks,
        in_specs=[smem()] + [pl.BlockSpec(memory_space=pltpu.HBM)] * 4,
        out_specs=[whole()] * chunks,
        scratch_shapes=[
            pltpu.VMEM((tok_n, chan_n), BF16),
            pltpu.VMEM((tok_n, chan_n), BF16),
            pltpu.SemaphoreType.DMA((2, parts)),
        ],
        compiler_params=params(8),
        cost_estimate=pl.CostEstimate(flops=flops, bytes_accessed=6 * a.size, transcendentals=0),
    )(me, *fixed)


def columns(chunks, g, group_n):
    each = group_n // len(chunks)
    at = g % each
    return chunks[g // each][:, at * GW : (at + 1) * GW]


def toeplitz(me, last, reaches, filters):
    group_n = filters.shape[0]
    shape = jax.ShapeDtypeStruct((group_n, TOK, 3 * TOK), BF16)

    def kernel(me_ref, reach_ref, filt_ref, ahead_ref, back_ref):
        row = lax.broadcasted_iota(jnp.int32, (TOK, TOK), 0)
        col = lax.broadcasted_iota(jnp.int32, (TOK, TOK), 1)
        upper = col >= row
        lag = lax.broadcasted_iota(jnp.int32, (1, 2 * TOK), 1)
        here = me_ref[0]
        back1, back2 = (here > 0).astype(F32), (here > 1).astype(F32)
        ahead1, ahead2 = (here < last).astype(F32), (here < last - 1).astype(F32)
        zero = jnp.zeros((TOK, TOK), F32)
        lines = filt_ref[...].astype(F32)
        for g in range(group_n):
            line = jnp.where(lag < reach_ref[g], lines[g : g + 1, :], 0.0)
            near, far = (
                pltpu.roll(
                    jnp.broadcast_to(part, (TOK, TOK)), 0, axis=1, stride=1, stride_axis=0
                )
                for part in (line[:, :TOK], line[:, TOK:])
            )
            w0 = jnp.where(upper, near, zero)
            w1 = jnp.where(upper, far, near)
            w2 = jnp.where(upper, zero, far)
            ahead_ref[g, :, :TOK] = w0.astype(BF16)
            ahead_ref[g, :, TOK : 2 * TOK] = (w1 * ahead1).astype(BF16)
            ahead_ref[g, :, 2 * TOK :] = (w2 * ahead2).astype(BF16)
            back_ref[g, :, :TOK] = w0.T.astype(BF16)
            back_ref[g, :, TOK : 2 * TOK] = (w1 * back1).T.astype(BF16)
            back_ref[g, :, 2 * TOK :] = (w2 * back2).T.astype(BF16)

    return pl.pallas_call(
        kernel,
        out_shape=[shape, shape],
        in_specs=[smem(), smem(), whole()],
        out_specs=[whole(), whole()],
        compiler_params=params(8),
        cost_estimate=pl.CostEstimate(
            flops=group_n * TOK, bytes_accessed=group_n * TOK, transcendentals=0
        ),
    )(me, reaches, filters)


def taps(scale, last, me, reaches, mine_p, mine_x, got_p, got_x, first, count):
    group_n = reaches.shape[0]
    fields = (mine_p, mine_x, got_p, got_x)
    sizes = [len(x) for x in fields]

    def kernel(me_ref, reach_ref, *refs):
        out_ref = refs[-1]
        split, at = [], 0
        for size in sizes:
            split.append(refs[at : at + size])
            at += size
        mine_p, mine_x, got_p, got_x = split
        row = lax.broadcasted_iota(jnp.int32, (TOK, TOK), 0)
        col = lax.broadcasted_iota(jnp.int32, (TOK, TOK), 1)
        upper = col >= row
        sub = lax.broadcasted_iota(jnp.int32, (8, TOK), 0)
        lane = lax.broadcasted_iota(jnp.int32, (1, TOK), 1)
        here = me_ref[0]
        near_ok = (here > 0).astype(F32)
        far_ok = ((here > 0) & (here < last)).astype(F32)

        def diagonals(tile):
            acc = tile[0:8, :]
            for k in range(1, TOK // 8):
                acc = acc + pltpu.roll(tile[8 * k : 8 * k + 8, :], TOK - 8 * k, axis=1)
            for bit in (1, 2, 4):
                acc = jnp.where((sub & bit) != 0, pltpu.roll(acc, TOK - bit, axis=1), acc)
            return jnp.sum(acc, axis=0, keepdims=True)

        def pair(a, b):
            return lax.dot_general(a, b, (((1,), (1,)), ((), ())), preferred_element_type=F32)

        def work(sig, sig_back, dcv, dcv_ahead):
            for i in range(count):
                here_s, back_s, here_d, ahead_d = (
                    columns(x, i, count) for x in (sig, sig_back, dcv, dcv_ahead)
                )
                c0 = pair(here_s, here_d)
                c1 = pair(back_s, here_d) * near_ok
                c2 = pair(back_s, ahead_d) * far_ok
                low = diagonals(jnp.where(upper, c0, c1))
                high = diagonals(jnp.where(upper, c1, c2))
                reach = reach_ref[first + i]
                out_ref[i : i + 1, :TOK] = jnp.where(lane < reach, low * scale, 0.0)
                out_ref[i : i + 1, TOK:] = jnp.where(lane + TOK < reach, high * scale, 0.0)

        odd = (here & 1) == 1

        @pl.when(odd)
        def _():
            work(mine_p, got_x, mine_x, got_p)

        @pl.when(jnp.logical_not(odd))
        def _():
            work(mine_x, got_p, mine_p, got_x)

    flat = [x for field in fields for x in field]
    return pl.pallas_call(
        kernel,
        out_shape=jax.ShapeDtypeStruct((count, 2 * TOK), F32),
        in_specs=[smem(), smem()] + [whole()] * len(flat),
        out_specs=whole(),
        compiler_params=params(8),
        cost_estimate=pl.CostEstimate(
            flops=count * TOK, bytes_accessed=count * TOK, transcendentals=0
        ),
    )(me, reaches, *flat)


def grads_piece(me, ahead, back, fields, gates, outs, first, count, step):
    tok_n, chan_n = gates[0].shape
    group_n = chan_n // GW
    start = first // step
    each = [group_n // len(x) for x in fields]
    fields = [x[first // n] for x, n in zip(fields, each)]
    cols = pl.BlockSpec((tok_n, step * GW), lambda i: (0, i + start))

    def kernel(me_ref, ahead_ref, back_ref, *refs):
        grad, kpart, vpart = refs[6:9]
        gq, gk, gv = refs[-3:]
        base = first + pl.program_id(0) * step

        def dot(a, b):
            return jnp.dot(a, b, preferred_element_type=F32)

        def cols_of(ref, offset, g):
            return ref[:, pl.ds(pl.multiple_of((base - offset + g) * GW, GW), GW)]

        def work(*order):
            for g in range(step):
                at = slice(g * GW, (g + 1) * GW)
                src = pl.ds(pl.multiple_of((base + g) * GW, GW), GW)
                sig, sig1, sig2, dcv, dcv1, dcv2 = (
                    cols_of(refs[i], first - first % each[i], g) for i in order
                )
                back_mat = back_ref[base + g]
                conv = (
                    dot(back_mat[:, :TOK], sig)
                    + dot(back_mat[:, TOK : 2 * TOK], sig1)
                    + dot(back_mat[:, 2 * TOK :], sig2)
                )
                gq[:, at] = (grad[:, src].astype(F32) * conv).astype(BF16)
                ahead_mat = ahead_ref[base + g]
                dsig = (
                    dot(ahead_mat[:, :TOK], dcv)
                    + dot(ahead_mat[:, TOK : 2 * TOK], dcv1)
                    + dot(ahead_mat[:, 2 * TOK :], dcv2)
                )
                gk[:, at] = (dsig * vpart[:, src].astype(F32)).astype(BF16)
                gv[:, at] = (dsig * kpart[:, src].astype(F32)).astype(BF16)

        odd = (me_ref[0] & 1) == 1

        @pl.when(odd)
        def _():
            work(0, 3, 5, 1, 2, 4)

        @pl.when(jnp.logical_not(odd))
        def _():
            work(1, 2, 4, 0, 3, 5)

    shape = jax.ShapeDtypeStruct((tok_n, chan_n), BF16)
    earlier = [] if outs is None else list(outs)
    part = count * TOK * GW
    return pl.pallas_call(
        kernel,
        out_shape=[shape] * 3,
        grid=(count // step,),
        in_specs=[smem()] + [whole()] * 11 + [pl.BlockSpec(memory_space=pl.ANY)] * len(earlier),
        out_specs=[cols] * 3,
        input_output_aliases={12 + i: i for i in range(len(earlier))},
        compiler_params=params(8),
        cost_estimate=pl.CostEstimate(
            flops=12 * part * TOK, bytes_accessed=27 * part, transcendentals=0
        ),
    )(me, ahead, back, *fields, *gates, *earlier)


def body(q_proj, k_proj, v_proj, out_grad, filters, reaches):
    batch_n, tok_n, chan_n = q_proj.shape
    group_n = filters.shape[0]
    ctx_n, dp_n = lax.axis_size("ctx"), lax.axis_size("dp")
    scale = 1.0 / math.sqrt(batch_n * dp_n * tok_n * ctx_n * (chan_n // group_n))
    q, k, v, grad = (x.reshape(tok_n, chan_n) for x in (q_proj, k_proj, v_proj, out_grad))

    me = lax.axis_index("ctx").astype(jnp.int32)[None]
    last = ctx_n - 1

    across = [(i, (i + 1) % ctx_n if i & 1 else (i - 1) % ctx_n) for i in range(ctx_n)]
    within = [(i, i ^ 1) for i in range(ctx_n)]

    def trade(chunks, route):
        return [lax.ppermute(x, "ctx", route) for x in chunks]

    p_n, x_n = 1, 2
    mine_p = gate_product(me, k, v, grad, q, p_n, 1)
    got_p = trade(mine_p, across)
    mine_p, me = lax.optimization_barrier((mine_p, me))
    mine_x = gate_product(me, grad, q, k, v, x_n, 10**9)
    got_x = [jnp.concatenate(trade(mine_x, within), axis=1)]
    got_x, me = lax.optimization_barrier((got_x, me))
    got2_p = trade(got_x, across)
    ahead, back = toeplitz(me, last, reaches, filters)
    ahead, me = lax.optimization_barrier((ahead, me))
    local, got2_x = [], []
    each = group_n // p_n
    for i in range(p_n):
        here = slice(i * x_n // p_n, (i + 1) * x_n // p_n)
        term = taps(
            scale, last, me, reaches, mine_p[i : i + 1], mine_x[here], got_p[i : i + 1], got_x,
            i * each, each,
        )
        term, got_p[i], me = lax.optimization_barrier((term, got_p[i], me))
        got2_x.append(lax.ppermute(got_p[i], "ctx", within))
        local.append(term)
    local = jnp.concatenate(local)

    def trade_ctx(x, mask):
        return x + lax.ppermute(x, "ctx", [(i, i ^ mask) for i in range(ctx_n)])

    def trade_dp(x, mask):
        route = [
            (d * ctx_n + i, (d ^ mask) * ctx_n + (i ^ 1)) for d in range(dp_n) for i in range(ctx_n)
        ]
        return x + lax.ppermute(x, ("dp", "ctx"), route)

    total = trade_ctx(local, 1)
    total = trade_dp(total, 1)
    total = trade_dp(total, 3)
    total = trade_ctx(total, 8 | 1)
    outs = None
    fields = (mine_p, mine_x, got_p, got_x, got2_p, got2_x)
    pieces = 4
    for at, mask in enumerate((16 | 1, 56 | 1, 2 | 1, 6 | 1)):
        total, fields = lax.optimization_barrier((total, fields))
        outs = grads_piece(
            me, ahead, back, fields, (grad, k, v), outs,
            at * group_n // pieces, group_n // pieces, 2,
        )
        total = trade_ctx(total, mask)
        total, outs = lax.optimization_barrier((total, outs))
    shaped = [x.reshape(batch_n, tok_n, chan_n) for x in outs]
    return (*shaped, total)


def solution(mesh):
    block = P("dp", "ctx", None)
    return jax.shard_map(
        body,
        mesh=mesh,
        in_specs=(block, block, block, block, P(), P()),
        out_specs=(block, block, block, P()),
        check_vma=False,
    )
```

time: 69.6 us -> 56.4 us (0.81); the launches traced: 68.7 us -> 56.2 us
  Pallas kernels: 30.8 us -> 13 us
  waiting for transfers between devices: 7.01 us -> 17.4 us
  other arithmetic: 2.76 us -> 0.71 us
  starting transfers between devices: 26.3 us -> 24.3 us
  local copies, waits for them, and re-layouts: 1.11 us -> 0.03 us
    pallas_call x4, Pallas kernels: 18.4 us -> 6.82 us  [the longest x2 3.27 us: gate_product(): pl.pallas_call(kernel, out_shape=[jax.ShapeDtypeStruct((tok_n, width), BF...]
    ppermute x6, waiting for transfers between devices: 2.15 us -> 11 us  [trade_ctx(): return x + lax.ppermute(x, 'ctx', [(i, i ^ mask) for i in range(ctx_n)])]
    pallas_call x4, Pallas kernels: 12.4 us -> 6.2 us  [grads_piece(): pl.pallas_call(kernel, out_shape=[shape] * 3, grid=(count // step,), in_s...]
    ppermute x6, starting transfers between devices: 7.03 us -> 4.48 us  [trade_ctx(): return x + lax.ppermute(x, 'ctx', [(i, i ^ mask) for i in range(ctx_n)])]
    ppermute x4 -> x5, waiting for transfers between devices: 0.67 us -> 2.42 us  [the longest x4 2.41 us: trade(): return [lax.ppermute(x, 'ctx', route) for x in chunks]]
    unnamed x6 -> x10, local copies, waits for them, and re-layouts: 1.11 us -> 0.03 us
    another operation x1 -> x0, other arithmetic: 0.79 us -> none  [body(): jnp.stack([odd, me > 0, (me > 0) & (me < ctx_n - 1)]).astype(jnp.int32)]
    add x6, other arithmetic: 1.35 us -> 0.63 us  [trade_ctx(): return x + lax.ppermute(x, 'ctx', [(i, i ^ mask) for i in range(ctx_n)])]
  transfers between devices with their start and end apart: 12 -> 13, of which waited for: 7 -> 11; matrix products, arithmetic and copies ran while one was open for 3% -> 0% of each run, Pallas kernels for 36% -> 20%
where the time goes in v2:
time: 56.4 us; the launch traced here: 56.2 us
  starting transfers between devices  24.3 us (43%)
  waiting for transfers between devices  17.4 us (31%)
  Pallas kernels  13 us (23%)
  between operations  0.79 us (1%)
  other arithmetic  0.71 us (1%)
    ppermute x6, waiting for transfers between devices, trade_ctx(): return x + lax.ppermute(x, 'ctx', [(i, i ^ mask) for i in range(ctx_n)])  11 us
    ppermute x4, starting transfers between devices, trade(): return [lax.ppermute(x, 'ctx', route) for x in chunks]  9.62 us
    ppermute x1, starting transfers between devices, body(): got2_x.append(lax.ppermute(got_p[i], 'ctx', within))  6.34 us
    pallas_call x4, Pallas kernels, grads_piece(): pl.pallas_call(kernel, out_shape=[shape] * 3, grid=(count // step,), in_s...  6.2 us
    ppermute x6, starting transfers between devices, trade_ctx(): return x + lax.ppermute(x, 'ctx', [(i, i ^ mask) for i in range(ctx_n)])  4.48 us
    ppermute x2, waiting for transfers between devices, trade_dp(): return x + lax.ppermute(x, ('dp', 'ctx'), route)  3.95 us
    ppermute x2, starting transfers between devices, trade_dp(): return x + lax.ppermute(x, ('dp', 'ctx'), route)  3.9 us
    pallas_call x2, Pallas kernels, gate_product(): pl.pallas_call(kernel, out_shape=[jax.ShapeDtypeStruct((tok_n, width), BF...  3.27 us
  transfers between devices with their start and end apart: 13, of which 11 were waited for; matrix products, arithmetic and copies ran while one was open for 0% of the time, Pallas kernels for 20%

profile of v2, /device:TPU:1, one launch (start us, length us, event | category | flops | bytes accessed | tf_op | source)
XLA Modules:
  0.0 56.2 jit_solution(15429889296934957326)
XLA Ops:
  0.6 1.6 %shard_map.93.refs_0_ = bf16[128,4096]{1,0:T(8,128)(2,1)S(1)} custom-call(s32[1]{0:T(128)} %bitcast.me_ref, bf16[128,4096]{1,0:T(8,128)(2,1)} %bitcast.8, bf16[128,4096]{1,0:T(8,128)(2,1)} %bitcast.14, bf16[128,4096]{1,0:T(8,128)(2,1)} %bitcast.20, bf16[128,4096]{1,0:T(8,128)(2,1)} %bitcast.29), custom_call_target="tpu_custom_call" | custom-call | flops 1 | bytes 3145728 | tf_op jit(solution)/shard_map/pallas_call | solution.py:68
  2.3 2.8 %collective-permute-start.2 = (bf16[128,4096]{1,0:T(8,128)(2,1)S(1)}, bf16[128,4096]{1,0:T(8,128)(2,1)S(1)}, u32[]{:S(2)}, u32[]{:S(2)}) collective-permute-start(bf16[128,4096]{1,0:T(8,128)(2,1)S(1)} %shard_map.93.refs_0_), channel_id=1, source_target_pairs={{0,63},{1,2},{2,1},{3,4},{4,3},{5,6},{6,5},{7,8},{8,7},{9,10},{10,... | collective-permute-start | bytes 3145736 | tf_op jit(solution)/shard_map/ppermute | solution.py:285
  5.1 1.6 %shard_map.94 = (bf16[128,2048]{1,0:T(8,128)(2,1)S(1)}, bf16[128,2048]{1,0:T(8,128)(2,1)S(1)}) custom-call(s32[1]{0:T(128)} %bitcast.me_ref, bf16[128,4096]{1,0:T(8,128)(2,1)} %bitcast.21, bf16[128,4096]{1,0:T(8,128)(2,1)} %bitcast.30, bf16[128,4096]{1,0:T(8,128)(2,1)} %bitcast.9, bf16[128,4096]{1,0:T(8,128)(2,1)} %bitcast.15), custom_call_target="tpu_custom_call" | custom-call | flops 1000000000 | bytes 3145728 | tf_op jit(solution)/shard_map/pallas_call | solution.py:68
  6.7 0.0 copy-start.3
  6.7 0.0 copy-start.4
  6.7 6.6 %collective-permute-start = (bf16[128,2048]{1,0:T(8,128)(2,1)S(1)}, bf16[128,2048]{1,0:T(8,128)(2,1)S(1)}, u32[]{:S(2)}, u32[]{:S(2)}) collective-permute-start(bf16[128,2048]{1,0:T(8,128)(2,1)S(1)} %get-tuple-element.102.refs_1_), channel_id=1, source_target_pairs={{0,1},{1,0},{2,3},{3,2},{4,5},{5,4},{6,7},{7,6},{8,9},{9,8},{10,11... | collective-permute-start | bytes 1572872 | tf_op jit(solution)/shard_map/ppermute | solution.py:285
  13.4 0.1 collective-permute-start.1
  13.5 1.4 %collective-permute-done = bf16[128,2048]{1,0:T(8,128)(2,1)S(1)} collective-permute-done((bf16[128,2048]{1,0:T(8,128)(2,1)S(1)}, bf16[128,2048]{1,0:T(8,128)(2,1)S(1)}, u32[]{:S(2)}, u32[]{:S(2)}) %collective-permute-start) | collective-permute-done | bytes 524320 | tf_op jit(solution)/shard_map/ppermute | solution.py:285
  14.9 0.7 %collective-permute-done.1 = bf16[128,2048]{1,0:T(8,128)(2,1)S(1)} collective-permute-done((bf16[128,2048]{1,0:T(8,128)(2,1)S(1)}, bf16[128,2048]{1,0:T(8,128)(2,1)S(1)}, u32[]{:S(2)}, u32[]{:S(2)}) %collective-permute-start.1) | collective-permute-done | bytes 524320 | tf_op jit(solution)/shard_map/ppermute | solution.py:285
  15.7 0.1 pad_maximum_fusion.refs_4_.refs_3_
  15.7 0.1 collective-permute-start.7
  15.8 0.0 copy-done.3
  15.8 0.0 copy-done.4
  15.9 1.7 %shard_map.95 = (bf16[16,128,384]{2,1,0:T(8,128)(2,1)S(1)}, bf16[16,128,384]{2,1,0:T(8,128)(2,1)S(1)}) custom-call(s32[1]{0:T(128)} %bitcast.me_ref, s32[16]{0:T(128)S(1)} %copy-done.4, bf16[16,256]{1,0:T(8,128)(2,1)S(1)} %copy-done.3), custom_call_target="tpu_custom_call" | custom-call | flops 2048 | bytes 2048 | tf_op jit(solution)/shard_map/pallas_call | solution.py:121
  17.6 0.0 copy-start
  17.6 0.0 copy-start.1
  17.6 0.0 copy-start.2
  17.6 0.2 collective-permute-done.2.refs_3_.refs_2_
  17.8 1.8 %shard_map.96 = f32[16,256]{1,0:T(8,128)S(1)} custom-call(s32[1]{0:T(128)} %bitcast.me_ref, s32[16]{0:T(128)S(1)} %copy-done.4, bf16[128,4096]{1,0:T(8,128)(2,1)S(1)} %shard_map.93.refs_0_, bf16[128,2048]{1,0:T(8,128)(2,1)S(1)} %get-tuple-element.102.refs_1_, bf16[128,2048]{1,0:T(8,128)(2,1)S(1)} %get-tuple-element.131.refs_2_.refs_1_, ...), custom_call_target="tpu_custom_call" | custom-call | flops 2048 | bytes 2048 | tf_op jit(solution)/shard_map/pallas_call | solution.py:190
  19.7 6.3 %collective-permute-start.8 = (bf16[128,4096]{1,0:T(8,128)(2,1)S(1)}, bf16[128,4096]{1,0:T(8,128)(2,1)S(1)}, u32[]{:S(2)}, u32[]{:S(2)}) collective-permute-start(bf16[128,4096]{1,0:T(8,128)(2,1)S(1)} %collective-permute-done.2.refs_3_.refs_2_), channel_id=1, source_target_pairs={{0,1},{1,0},{2,3},{3,2},{4,5},{5,4},{6,7},{7,6},{8,9},{9,8},{10,11... | collective-permute-start | bytes 3145736 | tf_op jit(solution)/shard_map/ppermute | solution.py:306
  26.0 0.1 collective-permute-start.3
  26.1 2.2 %collective-permute-done.3 = f32[16,256]{1,0:T(8,128)S(1)} collective-permute-done((f32[16,256]{1,0:T(8,128)S(1)}, f32[16,256]{1,0:T(8,128)S(1)}, u32[]{:S(2)}, u32[]{:S(2)}) %collective-permute-start.3) | collective-permute-done | bytes 16416 | tf_op jit(solution)/shard_map/ppermute | solution.py:311
  28.3 1.5 %collective-permute-start.4 = (f32[16,256]{1,0:T(8,128)S(1)}, f32[16,256]{1,0:T(8,128)S(1)}, u32[]{:S(2)}, u32[]{:S(2)}) collective-permute-start(f32[16,256]{1,0:T(8,128)S(1)} %add.24), channel_id=1, source_target_pairs={{0,65},{1,64},{2,67},{3,66},{4,69},{5,68},{6,71},{7,70},{8,73},{9,... | collective-permute-start | bytes 49160 | tf_op jit(solution)/shard_map/ppermute | solution.py:317
  29.8 2.0 %collective-permute-done.4 = f32[16,256]{1,0:T(8,128)S(1)} collective-permute-done((f32[16,256]{1,0:T(8,128)S(1)}, f32[16,256]{1,0:T(8,128)S(1)}, u32[]{:S(2)}, u32[]{:S(2)}) %collective-permute-start.4) | collective-permute-done | bytes 16416 | tf_op jit(solution)/shard_map/ppermute | solution.py:317
  31.8 2.4 %collective-permute-start.5 = (f32[16,256]{1,0:T(8,128)S(1)}, f32[16,256]{1,0:T(8,128)S(1)}, u32[]{:S(2)}, u32[]{:S(2)}) collective-permute-start(f32[16,256]{1,0:T(8,128)S(1)} %add.25), channel_id=1, source_target_pairs={{0,193},{1,192},{2,195},{3,194},{4,197},{5,196},{6,199},{7,198},{8... | collective-permute-start | bytes 49160 | tf_op jit(solution)/shard_map/ppermute | solution.py:317
  34.2 1.9 %collective-permute-done.5 = f32[16,256]{1,0:T(8,128)S(1)} collective-permute-done((f32[16,256]{1,0:T(8,128)S(1)}, f32[16,256]{1,0:T(8,128)S(1)}, u32[]{:S(2)}, u32[]{:S(2)}) %collective-permute-start.5) | collective-permute-done | bytes 16416 | tf_op jit(solution)/shard_map/ppermute | solution.py:317
  36.2 0.0 collective-permute-start.6
  36.2 3.2 %collective-permute-done.6 = f32[16,256]{1,0:T(8,128)S(1)} collective-permute-done((f32[16,256]{1,0:T(8,128)S(1)}, f32[16,256]{1,0:T(8,128)S(1)}, u32[]{:S(2)}, u32[]{:S(2)}) %collective-permute-start.6) | collective-permute-done | bytes 16416 | tf_op jit(solution)/shard_map/ppermute | solution.py:311
  39.4 0.0 collective-permute-done.7.refs_4_
  39.4 0.0 collective-permute-done.8.refs_5_
  39.4 0.1 collective-permute-start.9
  39.5 0.0 copy-done
  39.5 0.0 copy-done.1
  39.5 0.0 copy-done.2
  39.5 1.6 %shard_map.97 = (bf16[128,4096]{1,0:T(8,128)(2,1)}, bf16[128,4096]{1,0:T(8,128)(2,1)}, bf16[128,4096]{1,0:T(8,128)(2,1)}) custom-call(s32[1]{0:T(128)} %bitcast.me_ref, bf16[16,128,384]{2,1,0:T(8,128)(2,1)S(1)} %get-tuple-element.87.ahead_ref, bf16[16,128,384]{2,1,0:T(8,128)(2,1)S(1)} %get-tuple-element.88.back_ref, ...), custom_call_target="tpu_custom_call" | custom-call | flops 201326592 | bytes 3538944 | tf_op jit(solution)/shard_map/pallas_call | solution.py:257
  41.1 2.5 %collective-permute-done.9 = f32[16,256]{1,0:T(8,128)S(1)} collective-permute-done((f32[16,256]{1,0:T(8,128)S(1)}, f32[16,256]{1,0:T(8,128)S(1)}, u32[]{:S(2)}, u32[]{:S(2)}) %collective-permute-start.9) | collective-permute-done | bytes 16416 | tf_op jit(solution)/shard_map/ppermute | solution.py:311
  43.5 1.6 %collective-permute-start.10 = (f32[16,256]{1,0:T(8,128)S(1)}, f32[16,256]{1,0:T(8,128)S(1)}, u32[]{:S(2)}, u32[]{:S(2)}) collective-permute-start(f32[16,256]{1,0:T(8,128)S(1)} %add.28), channel_id=1, source_target_pairs={{0,57},{1,56},{2,59},{3,58},{4,61},{5,60},{6,63},{7,62},{8,49},{9,... | collective-permute-start | bytes 49160 | tf_op jit(solution)/shard_map/ppermute | solution.py:311
  45.2 1.5 %shard_map.98 = (bf16[128,4096]{1,0:T(8,128)(2,1)}, bf16[128,4096]{1,0:T(8,128)(2,1)}, bf16[128,4096]{1,0:T(8,128)(2,1)}) custom-call(s32[1]{0:T(128)} %bitcast.me_ref, bf16[16,128,384]{2,1,0:T(8,128)(2,1)S(1)} %get-tuple-element.87.ahead_ref, ...), custom_call_target="tpu_custom_call", output_to_operand_aliasing={{0}: (12, {}), {1}: (13, {}), {2}: (14, {})} | custom-call | flops 201326592 | bytes 3538944 | tf_op jit(solution)/shard_map/pallas_call | solution.py:257
  46.7 1.4 %collective-permute-done.10 = f32[16,256]{1,0:T(8,128)S(1)} collective-permute-done((f32[16,256]{1,0:T(8,128)S(1)}, f32[16,256]{1,0:T(8,128)S(1)}, u32[]{:S(2)}, u32[]{:S(2)}) %collective-permute-start.10) | collective-permute-done | bytes 16416 | tf_op jit(solution)/shard_map/ppermute | solution.py:311
  48.1 0.0 collective-permute-start.11
  48.1 1.6 %shard_map.99 = (bf16[128,4096]{1,0:T(8,128)(2,1)}, bf16[128,4096]{1,0:T(8,128)(2,1)}, bf16[128,4096]{1,0:T(8,128)(2,1)}) custom-call(s32[1]{0:T(128)} %bitcast.me_ref, bf16[16,128,384]{2,1,0:T(8,128)(2,1)S(1)} %get-tuple-element.87.ahead_ref, ...), custom_call_target="tpu_custom_call", output_to_operand_aliasing={{0}: (12, {}), {1}: (13, {}), {2}: (14, {})} | custom-call | flops 201326592 | bytes 3538944 | tf_op jit(solution)/shard_map/pallas_call | solution.py:257
  49.7 1.6 %collective-permute-done.11 = f32[16,256]{1,0:T(8,128)S(1)} collective-permute-done((f32[16,256]{1,0:T(8,128)S(1)}, f32[16,256]{1,0:T(8,128)S(1)}, u32[]{:S(2)}, u32[]{:S(2)}) %collective-permute-start.11) | collective-permute-done | bytes 16416 | tf_op jit(solution)/shard_map/ppermute | solution.py:311
  51.3 2.6 %collective-permute-start.12 = (f32[16,256]{1,0:T(8,128)S(1)}, f32[16,256]{1,0:T(8,128)S(1)}, u32[]{:S(2)}, u32[]{:S(2)}) collective-permute-start(f32[16,256]{1,0:T(8,128)S(1)} %add.30), channel_id=1, source_target_pairs={{0,7},{1,6},{2,5},{3,4},{4,3},{5,2},{6,1},{7,0},{8,15},{9,14},{10,... | collective-permute-start | bytes 49160 | tf_op jit(solution)/shard_map/ppermute | solution.py:311
  53.9 1.5 %shard_map.100 = (bf16[128,4096]{1,0:T(8,128)(2,1)}, bf16[128,4096]{1,0:T(8,128)(2,1)}, bf16[128,4096]{1,0:T(8,128)(2,1)}) custom-call(s32[1]{0:T(128)} %bitcast.me_ref, bf16[16,128,384]{2,1,0:T(8,128)(2,1)S(1)} %get-tuple-element.87.ahead_ref, ...), custom_call_target="tpu_custom_call", output_to_operand_aliasing={{0}: (12, {}), {1}: (13, {}), {2}: (14, {})} | custom-call | flops 201326592 | bytes 3538944 | tf_op jit(solution)/shard_map/pallas_call | solution.py:257
  55.4 0.2 collective-permute-done.12
  55.6 0.6 %add.31 = f32[16,256]{1,0:T(8,128)} add(f32[16,256]{1,0:T(8,128)S(1)} %add.30, f32[16,256]{1,0:T(8,128)S(1)} %collective-permute-done.12) | non-fusion elementwise | flops 4096 | bytes 49152 | tf_op jit(solution)/shard_map/add | solution.py:311
  (7 shorter events, 0.0 us)
Async XLA Ops:
  2.3 15.6 %collective-permute-start.2 = (bf16[128,4096]{1,0:T(8,128)(2,1)S(1)}, bf16[128,4096]{1,0:T(8,128)(2,1)S(1)}, u32[]{:S(2)}, u32[]{:S(2)}) collective-permute-start(bf16[128,4096]{1,0:T(8,128)(2,1)S(1)} %shard_map.93.refs_0_), channel_id=1, source_target_pairs={{0,63},{1,2},{2,1},{3,4},{4,3},{5,6},{6,5},{7,8},{8,7},{9,10},{10,... | collective-permute-start | bytes 3145736 | tf_op jit(solution)/shard_map/ppermute | solution.py:285
  6.7 9.1 %copy-start.3 = (bf16[16,256]{1,0:T(8,128)(2,1)S(1)}, bf16[16,256]{1,0:T(8,128)(2,1)}, u32[]{:S(2)}) copy-start(bf16[16,256]{1,0:T(8,128)(2,1)} %filt_ref.1) | copy-start | bytes 24580
  6.7 9.1 %copy-start.4 = (s32[16]{0:T(128)S(1)}, s32[16]{0:T(128)}, u32[]{:S(2)}) copy-start(s32[16]{0:T(128)} %reach_ref.3) | copy-start | bytes 196
  6.7 8.2 %collective-permute-start = (bf16[128,2048]{1,0:T(8,128)(2,1)S(1)}, bf16[128,2048]{1,0:T(8,128)(2,1)S(1)}, u32[]{:S(2)}, u32[]{:S(2)}) collective-permute-start(bf16[128,2048]{1,0:T(8,128)(2,1)S(1)} %get-tuple-element.102.refs_1_), channel_id=1, source_target_pairs={{0,1},{1,0},{2,3},{3,2},{4,5},{5,4},{6,7},{7,6},{8,9},{9,8},{10,11... | collective-permute-start | bytes 1572872 | tf_op jit(solution)/shard_map/ppermute | solution.py:285
  13.4 2.3 %collective-permute-start.1 = (bf16[128,2048]{1,0:T(8,128)(2,1)S(1)}, bf16[128,2048]{1,0:T(8,128)(2,1)S(1)}, u32[]{:S(2)}, u32[]{:S(2)}) collective-permute-start(bf16[128,2048]{1,0:T(8,128)(2,1)S(1)} %get-tuple-element.131.refs_2_.refs_1_), channel_id=1, source_target_pairs={{0,1},{1,0},{2,3},{3,2},{4,5},{5,4},{6,7},{7,6},{8,9},{9,8},{10,11... | collective-permute-start | bytes 1572872 | tf_op jit(solution)/shard_map/ppermute | solution.py:285
  15.7 23.6 %collective-permute-start.7 = (bf16[128,4096]{1,0:T(8,128)(2,1)S(1)}, bf16[128,4096]{1,0:T(8,128)(2,1)S(1)}, u32[]{:S(2)}, u32[]{:S(2)}) collective-permute-start(bf16[128,4096]{1,0:T(8,128)(2,1)S(1)} %pad_maximum_fusion.refs_4_.refs_3_), channel_id=1, source_target_pairs={{0,63},{1,2},{2,1},{3,4},{4,3},{5,6},{6,5},{7,8},{8,7},{9,10},{10,... | collective-permute-start | bytes 3145736 | tf_op jit(solution)/shard_map/ppermute | solution.py:285
  17.6 21.9 %copy-start = (bf16[1,128,4096]{2,1,0:T(8,128)(2,1)S(1)}, bf16[1,128,4096]{2,1,0:T(8,128)(2,1)}, u32[]{:S(2)}) copy-start(bf16[1,128,4096]{2,1,0:T(8,128)(2,1)} %param.7) | copy-start | bytes 3145732
  17.6 21.9 %copy-start.1 = (bf16[1,128,4096]{2,1,0:T(8,128)(2,1)S(1)}, bf16[1,128,4096]{2,1,0:T(8,128)(2,1)}, u32[]{:S(2)}) copy-start(bf16[1,128,4096]{2,1,0:T(8,128)(2,1)} %param.8) | copy-start | bytes 3145732
  17.6 21.9 %copy-start.2 = (bf16[1,128,4096]{2,1,0:T(8,128)(2,1)S(1)}, bf16[1,128,4096]{2,1,0:T(8,128)(2,1)}, u32[]{:S(2)}) copy-start(bf16[1,128,4096]{2,1,0:T(8,128)(2,1)} %param.9) | copy-start | bytes 3145732
  19.7 19.7 %collective-permute-start.8 = (bf16[128,4096]{1,0:T(8,128)(2,1)S(1)}, bf16[128,4096]{1,0:T(8,128)(2,1)S(1)}, u32[]{:S(2)}, u32[]{:S(2)}) collective-permute-start(bf16[128,4096]{1,0:T(8,128)(2,1)S(1)} %collective-permute-done.2.refs_3_.refs_2_), channel_id=1, source_target_pairs={{0,1},{1,0},{2,3},{3,2},{4,5},{5,4},{6,7},{7,6},{8,9},{9,8},{10,11... | collective-permute-start | bytes 3145736 | tf_op jit(solution)/shard_map/ppermute | solution.py:306
  26.0 2.3 %collective-permute-start.3 = (f32[16,256]{1,0:T(8,128)S(1)}, f32[16,256]{1,0:T(8,128)S(1)}, u32[]{:S(2)}, u32[]{:S(2)}) collective-permute-start(f32[16,256]{1,0:T(8,128)S(1)} %shard_map.96), channel_id=1, source_target_pairs={{0,1},{1,0},{2,3},{3,2},{4,5},{5,4},{6,7},{7,6},{8,9},{9,8},{10,11... | collective-permute-start | bytes 49160 | tf_op jit(solution)/shard_map/ppermute | solution.py:311
  28.3 3.5 %collective-permute-start.4 = (f32[16,256]{1,0:T(8,128)S(1)}, f32[16,256]{1,0:T(8,128)S(1)}, u32[]{:S(2)}, u32[]{:S(2)}) collective-permute-start(f32[16,256]{1,0:T(8,128)S(1)} %add.24), channel_id=1, source_target_pairs={{0,65},{1,64},{2,67},{3,66},{4,69},{5,68},{6,71},{7,70},{8,73},{9,... | collective-permute-start | bytes 49160 | tf_op jit(solution)/shard_map/ppermute | solution.py:317
  31.8 4.4 %collective-permute-start.5 = (f32[16,256]{1,0:T(8,128)S(1)}, f32[16,256]{1,0:T(8,128)S(1)}, u32[]{:S(2)}, u32[]{:S(2)}) collective-permute-start(f32[16,256]{1,0:T(8,128)S(1)} %add.25), channel_id=1, source_target_pairs={{0,193},{1,192},{2,195},{3,194},{4,197},{5,196},{6,199},{7,198},{8... | collective-permute-start | bytes 49160 | tf_op jit(solution)/shard_map/ppermute | solution.py:317
  36.2 3.2 %collective-permute-start.6 = (f32[16,256]{1,0:T(8,128)S(1)}, f32[16,256]{1,0:T(8,128)S(1)}, u32[]{:S(2)}, u32[]{:S(2)}) collective-permute-start(f32[16,256]{1,0:T(8,128)S(1)} %add.26), channel_id=1, source_target_pairs={{0,9},{1,8},{2,11},{3,10},{4,13},{5,12},{6,15},{7,14},{8,1},{9,0},... | collective-permute-start | bytes 49160 | tf_op jit(solution)/shard_map/ppermute | solution.py:311
  39.4 4.2 %collective-permute-start.9 = (f32[16,256]{1,0:T(8,128)S(1)}, f32[16,256]{1,0:T(8,128)S(1)}, u32[]{:S(2)}, u32[]{:S(2)}) collective-permute-start(f32[16,256]{1,0:T(8,128)S(1)} %add.27), channel_id=1, source_target_pairs={{0,17},{1,16},{2,19},{3,18},{4,21},{5,20},{6,23},{7,22},{8,25},{9,... | collective-permute-start | bytes 49160 | tf_op jit(solution)/shard_map/ppermute | solution.py:311
  43.5 4.6 %collective-permute-start.10 = (f32[16,256]{1,0:T(8,128)S(1)}, f32[16,256]{1,0:T(8,128)S(1)}, u32[]{:S(2)}, u32[]{:S(2)}) collective-permute-start(f32[16,256]{1,0:T(8,128)S(1)} %add.28), channel_id=1, source_target_pairs={{0,57},{1,56},{2,59},{3,58},{4,61},{5,60},{6,63},{7,62},{8,49},{9,... | collective-permute-start | bytes 49160 | tf_op jit(solution)/shard_map/ppermute | solution.py:311
  48.1 3.2 %collective-permute-start.11 = (f32[16,256]{1,0:T(8,128)S(1)}, f32[16,256]{1,0:T(8,128)S(1)}, u32[]{:S(2)}, u32[]{:S(2)}) collective-permute-start(f32[16,256]{1,0:T(8,128)S(1)} %add.29), channel_id=1, source_target_pairs={{0,3},{1,2},{2,1},{3,0},{4,7},{5,6},{6,5},{7,4},{8,11},{9,10},{10,... | collective-permute-start | bytes 49160 | tf_op jit(solution)/shard_map/ppermute | solution.py:311
  51.3 4.4 %collective-permute-start.12 = (f32[16,256]{1,0:T(8,128)S(1)}, f32[16,256]{1,0:T(8,128)S(1)}, u32[]{:S(2)}, u32[]{:S(2)}) collective-permute-start(f32[16,256]{1,0:T(8,128)S(1)} %add.30), channel_id=1, source_target_pairs={{0,7},{1,6},{2,5},{3,4},{4,3},{5,2},{6,1},{7,0},{8,15},{9,14},{10,... | collective-permute-start | bytes 49160 | tf_op jit(solution)/shard_map/ppermute | solution.py:311

commit v3 on v2

--- a/solution.py
+++ b/solution.py
@@ -80,10 +80,12 @@
     )(me, *fixed)
 
 
-def columns(chunks, g, group_n):
-    each = group_n // len(chunks)
-    at = g % each
-    return chunks[g // each][:, at * GW : (at + 1) * GW]
+def columns(chunks, g):
+    at = g * GW
+    for chunk in chunks:
+        if at < chunk.shape[1]:
+            return chunk[:, at : at + GW]
+        at -= chunk.shape[1]
 
 
 def toeplitz(me, last, reaches, filters):
@@ -130,73 +132,118 @@
     )(me, reaches, filters)
 
 
-def taps(scale, last, me, reaches, mine_p, mine_x, got_p, got_x, first, count):
-    group_n = reaches.shape[0]
-    fields = (mine_p, mine_x, got_p, got_x)
-    sizes = [len(x) for x in fields]
-
-    def kernel(me_ref, reach_ref, *refs):
-        out_ref = refs[-1]
-        split, at = [], 0
-        for size in sizes:
-            split.append(refs[at : at + size])
-            at += size
-        mine_p, mine_x, got_p, got_x = split
-        row = lax.broadcasted_iota(jnp.int32, (TOK, TOK), 0)
-        col = lax.broadcasted_iota(jnp.int32, (TOK, TOK), 1)
-        upper = col >= row
-        sub = lax.broadcasted_iota(jnp.int32, (8, TOK), 0)
-        lane = lax.broadcasted_iota(jnp.int32, (1, TOK), 1)
+def tile_sums(upper, tile):
+    sub = lax.broadcasted_iota(jnp.int32, (8, TOK), 0)
+    acc = tile[0:8, :]
+    for k in range(1, TOK // 8):
+        acc = acc + pltpu.roll(tile[8 * k : 8 * k + 8, :], TOK - 8 * k, axis=1)
+    for bit in (1, 2, 4):
+        acc = jnp.where((sub & bit) != 0, pltpu.roll(acc, TOK - bit, axis=1), acc)
+    return jnp.sum(acc, axis=0, keepdims=True)
+
+
+def upper_mask():
+    row = lax.broadcasted_iota(jnp.int32, (TOK, TOK), 0)
+    col = lax.broadcasted_iota(jnp.int32, (TOK, TOK), 1)
+    return col >= row
+
+
+def cross(a, b):
+    return lax.dot_general(a, b, (((1,), (1,)), ((), ())), preferred_element_type=F32)
+
+
+def taps_inside(scale, me, reaches, mine_p, mine_x, got_x):
+    group_n = mine_p.shape[1] // GW
+    x_n = len(mine_x)
+
+    def kernel(me_ref, reach_ref, mine_p, got_x, *refs):
+        mine_x, out_ref, weight_ref = refs[:x_n], refs[x_n], refs[x_n + 1]
+        upper = upper_mask()
+        lag = lax.broadcasted_iota(jnp.int32, (1, 2 * TOK), 1)
+        for g in range(group_n):
+            weight_ref[g : g + 1, :] = jnp.where(lag < reach_ref[g], scale, 0.0).astype(F32)
+
+        @pl.when((me_ref[0] & 1) == 1)
+        def _():
+            for g in range(group_n):
+                dcv = columns(mine_x, g)
+                c0 = cross(columns([mine_p], g), dcv)
+                c1 = cross(columns([got_x], g), dcv)
+                out_ref[g : g + 1, :TOK] = tile_sums(upper, jnp.where(upper, c0, c1))
+                out_ref[g : g + 1, TOK:] = tile_sums(upper, jnp.where(upper, c1, 0.0))
+
+        @pl.when((me_ref[0] & 1) == 0)
+        def _():
+            for g in range(group_n):
+                c0 = cross(columns(mine_x, g), columns([mine_p], g))
+                out_ref[g : g + 1, :TOK] = tile_sums(upper, jnp.where(upper, c0, 0.0))
+            out_ref[:, TOK:] = jnp.zeros((group_n, TOK), F32)
+
+    return pl.pallas_call(
+        kernel,
+        out_shape=[jax.ShapeDtypeStruct((group_n, 2 * TOK), F32)] * 2,
+        in_specs=[smem(), smem()] + [whole()] * (2 + x_n),
+        out_specs=[whole(), whole()],
+        compiler_params=params(8),
+        cost_estimate=pl.CostEstimate(
+            flops=group_n * TOK, bytes_accessed=group_n * TOK, transcendentals=0
+        ),
+    )(me, reaches, mine_p, got_x, *mine_x)
+
+
+def taps(last, me, inside, weight, mine_p, got_p, got_x):
+    group_n = inside.shape[0]
+    half = group_n // 2
+
+    def kernel(me_ref, in_ref, weight_ref, mine_p, got_p, got_x, out_ref):
+        upper = upper_mask()
         here = me_ref[0]
-        near_ok = (here > 0).astype(F32)
-        far_ok = ((here > 0) & (here < last)).astype(F32)
-
-        def diagonals(tile):
-            acc = tile[0:8, :]
-            for k in range(1, TOK // 8):
-                acc = acc + pltpu.roll(tile[8 * k : 8 * k + 8, :], TOK - 8 * k, axis=1)
-            for bit in (1, 2, 4):
-                acc = jnp.where((sub & bit) != 0, pltpu.roll(acc, TOK - bit, axis=1), acc)
-            return jnp.sum(acc, axis=0, keepdims=True)
-
-        def pair(a, b):
-            return lax.dot_general(a, b, (((1,), (1,)), ((), ())), preferred_element_type=F32)
-
-        def work(sig, sig_back, dcv, dcv_ahead):
-            for i in range(count):
-                here_s, back_s, here_d, ahead_d = (
-                    columns(x, i, count) for x in (sig, sig_back, dcv, dcv_ahead)
-                )
-                c0 = pair(here_s, here_d)
-                c1 = pair(back_s, here_d) * near_ok
-                c2 = pair(back_s, ahead_d) * far_ok
-                low = diagonals(jnp.where(upper, c0, c1))
-                high = diagonals(jnp.where(upper, c1, c2))
-                reach = reach_ref[first + i]
-                out_ref[i : i + 1, :TOK] = jnp.where(lane < reach, low * scale, 0.0)
-                out_ref[i : i + 1, TOK:] = jnp.where(lane + TOK < reach, high * scale, 0.0)
-
         odd = (here & 1) == 1
 
+        def at(ref, g):
+            return columns([ref], g)
+
+        def work(near, far, near_groups, ok):
+            for g in range(group_n):
+                c2 = cross(*far(g))
+                if g in near_groups:
+                    c1 = cross(*near(g))
+                    out_ref[g : g + 1, :TOK] = tile_sums(upper, jnp.where(upper, 0.0, c1))
+                    out_ref[g : g + 1, TOK:] = tile_sums(upper, jnp.where(upper, c1, c2))
+                else:
+                    out_ref[g : g + 1, TOK:] = tile_sums(upper, jnp.where(upper, 0.0, c2))
+            none = slice(half, group_n) if 0 in near_groups else slice(0, half)
+            out_ref[none, :TOK] = jnp.zeros((half, TOK), F32)
+            out_ref[...] = (in_ref[...] + jnp.where(ok, out_ref[...], 0.0)) * weight_ref[...]
+
         @pl.when(odd)
         def _():
-            work(mine_p, got_x, mine_x, got_p)
+            work(
+                lambda g: (at(mine_p, g), at(got_p, g)),
+                lambda g: (at(got_x, g), at(got_p, g)),
+                range(half, group_n),
+                here < last,
+            )
 
         @pl.when(jnp.logical_not(odd))
         def _():
-            work(mine_x, got_p, mine_p, got_x)
-
-    flat = [x for field in fields for x in field]
-    return pl.pallas_call(
-        kernel,
-        out_shape=jax.ShapeDtypeStruct((count, 2 * TOK), F32),
-        in_specs=[smem(), smem()] + [whole()] * len(flat),
+            work(
+                lambda g: (at(got_p, g), at(mine_p, g)),
+                lambda g: (at(got_p, g), at(got_x, g)),
+                range(half),
+                here > 0,
+            )
+
+    return pl.pallas_call(
+        kernel,
+        out_shape=jax.ShapeDtypeStruct((group_n, 2 * TOK), F32),
+        in_specs=[smem()] + [whole()] * 5,
         out_specs=whole(),
         compiler_params=params(8),
         cost_estimate=pl.CostEstimate(
-            flops=count * TOK, bytes_accessed=count * TOK, transcendentals=0
+            flops=group_n * TOK, bytes_accessed=group_n * TOK, transcendentals=0
         ),
-    )(me, reaches, *flat)
+    )(me, inside, weight, mine_p, got_p, got_x)
 
 
 def grads_piece(me, ahead, back, fields, gates, outs, first, count, step):
@@ -225,19 +272,9 @@
                 sig, sig1, sig2, dcv, dcv1, dcv2 = (
                     cols_of(refs[i], first - first % each[i], g) for i in order
                 )
-                back_mat = back_ref[base + g]
-                conv = (
-                    dot(back_mat[:, :TOK], sig)
-                    + dot(back_mat[:, TOK : 2 * TOK], sig1)
-                    + dot(back_mat[:, 2 * TOK :], sig2)
-                )
+                conv = dot(back_ref[base + g], jnp.concatenate([sig, sig1, sig2], axis=0))
                 gq[:, at] = (grad[:, src].astype(F32) * conv).astype(BF16)
-                ahead_mat = ahead_ref[base + g]
-                dsig = (
-                    dot(ahead_mat[:, :TOK], dcv)
-                    + dot(ahead_mat[:, TOK : 2 * TOK], dcv1)
-                    + dot(ahead_mat[:, 2 * TOK :], dcv2)
-                )
+                dsig = dot(ahead_ref[base + g], jnp.concatenate([dcv, dcv1, dcv2], axis=0))
                 gk[:, at] = (dsig * vpart[:, src].astype(F32)).astype(BF16)
                 gv[:, at] = (dsig * kpart[:, src].astype(F32)).astype(BF16)
 
@@ -294,18 +331,10 @@
     got2_p = trade(got_x, across)
     ahead, back = toeplitz(me, last, reaches, filters)
     ahead, me = lax.optimization_barrier((ahead, me))
-    local, got2_x = [], []
-    each = group_n // p_n
-    for i in range(p_n):
-        here = slice(i * x_n // p_n, (i + 1) * x_n // p_n)
-        term = taps(
-            scale, last, me, reaches, mine_p[i : i + 1], mine_x[here], got_p[i : i + 1], got_x,
-            i * each, each,
-        )
-        term, got_p[i], me = lax.optimization_barrier((term, got_p[i], me))
-        got2_x.append(lax.ppermute(got_p[i], "ctx", within))
-        local.append(term)
-    local = jnp.concatenate(local)
+    inside, weight = taps_inside(scale, me, reaches, mine_p[0], mine_x, got_x[0])
+    local = taps(last, me, inside, weight, mine_p[0], got_p[0], got_x[0])
+    local, got_p = lax.optimization_barrier((local, got_p))
+    got2_x = trade(got_p, within)
 
     def trade_ctx(x, mask):
         return x + lax.ppermute(x, "ctx", [(i, i ^ mask) for i in range(ctx_n)])
@@ -316,9 +345,9 @@
         ]
         return x + lax.ppermute(x, ("dp", "ctx"), route)
 
-    total = trade_ctx(local, 1)
-    total = trade_dp(total, 1)
+    total = trade_dp(local, 1)
     total = trade_dp(total, 3)
+    total = trade_ctx(total, 1)
     total = trade_ctx(total, 8 | 1)
     outs = None
     fields = (mine_p, mine_x, got_p, got_x, got2_p, got2_x)

time: 56.4 us -> 54.6 us (0.968)
  starting transfers between devices: 24.3 us -> 21.7 us
    ppermute x1 -> x0, starting transfers between devices: 6.34 us -> none  [body(): got2_x.append(lax.ppermute(got_p[i], 'ctx', within))]
    ppermute x4 -> x5, starting transfers between devices: 9.62 us -> 14.6 us  [trade(): return [lax.ppermute(x, 'ctx', route) for x in chunks]]
    ppermute x2, waiting for transfers between devices: 3.95 us -> 4.8 us  [trade_dp(): return x + lax.ppermute(x, ('dp', 'ctx'), route)]
    pallas_call x1 -> x2, Pallas kernels: 1.83 us -> 2.5 us  [the longest x1 1.6 us: taps_inside(): pl.pallas_call(kernel, out_shape=[jax.ShapeDtypeStruct((group_n, 2 * TOK)...]
    ppermute x6, starting transfers between devices: 4.48 us -> 3.83 us  [trade_ctx(): return x + lax.ppermute(x, 'ctx', [(i, i ^ mask) for i in range(ctx_n)])]
    ppermute x4 -> x5, waiting for transfers between devices: 2.41 us -> 2.19 us  [trade(): return [lax.ppermute(x, 'ctx', route) for x in chunks]]
  transfers between devices with their start and end apart: 13 -> 13, of which waited for: 11 -> 10; matrix products, arithmetic and copies ran while one was open for 0% -> 0% of each run, Pallas kernels for 20% -> 21%
where the time goes in v3:
time: 54.6 us; the launch traced here: 54.5 us
  starting transfers between devices  21.7 us (40%)
  waiting for transfers between devices  17.9 us (33%)
  Pallas kernels  13.3 us (24%)
  between operations  0.8 us (1%)
  other arithmetic  0.71 us (1%)
    ppermute x5, starting transfers between devices, trade(): return [lax.ppermute(x, 'ctx', route) for x in chunks]  14.6 us
    ppermute x6, waiting for transfers between devices, trade_ctx(): return x + lax.ppermute(x, 'ctx', [(i, i ^ mask) for i in range(ctx_n)])  10.9 us
    pallas_call x4, Pallas kernels, grads_piece(): pl.pallas_call(kernel, out_shape=[shape] * 3, grid=(count // step,), in_s...  5.85 us
    ppermute x2, waiting for transfers between devices, trade_dp(): return x + lax.ppermute(x, ('dp', 'ctx'), route)  4.8 us
    ppermute x6, starting transfers between devices, trade_ctx(): return x + lax.ppermute(x, 'ctx', [(i, i ^ mask) for i in range(ctx_n)])  3.83 us
    ppermute x2, starting transfers between devices, trade_dp(): return x + lax.ppermute(x, ('dp', 'ctx'), route)  3.34 us
    pallas_call x2, Pallas kernels, gate_product(): pl.pallas_call(kernel, out_shape=[jax.ShapeDtypeStruct((tok_n, width), BF...  3.27 us
    ppermute x5, waiting for transfers between devices, trade(): return [lax.ppermute(x, 'ctx', route) for x in chunks]  2.19 us
  transfers between devices with their start and end apart: 13, of which 10 were waited for; matrix products, arithmetic and copies ran while one was open for 0% of the time, Pallas kernels for 21%

profile of v3, /device:TPU:1, one launch (start us, length us, event | category | flops | bytes accessed | tf_op | source)
XLA Modules:
  0.0 54.5 jit_solution(12891492675402620773)
XLA Ops:
  0.6 1.6 %shard_map.93.mine_p.refs_0_ = bf16[128,4096]{1,0:T(8,128)(2,1)S(1)} custom-call(s32[1]{0:T(128)} %bitcast.me_ref, bf16[128,4096]{1,0:T(8,128)(2,1)} %bitcast.8, bf16[128,4096]{1,0:T(8,128)(2,1)} %bitcast.14, bf16[128,4096]{1,0:T(8,128)(2,1)} %bitcast.20, bf16[128,4096]{1,0:T(8,128)(2,1)} %bitcast.29), custom_call_target="tpu_custom_call" | custom-call | flops 1 | bytes 3145728 | tf_op jit(solution)/shard_map/pallas_call | solution.py:68
  2.3 2.8 %collective-permute-start.2 = (bf16[128,4096]{1,0:T(8,128)(2,1)S(1)}, bf16[128,4096]{1,0:T(8,128)(2,1)S(1)}, u32[]{:S(2)}, u32[]{:S(2)}) collective-permute-start(bf16[128,4096]{1,0:T(8,128)(2,1)S(1)} %shard_map.93.mine_p.refs_0_), channel_id=1, source_target_pairs={{0,63},{1,2},{2,1},{3,4},{4,3},{5,6},{6,5},{7,8},{8,7},{9,10},{10,... | collective-permute-start | bytes 3145736 | tf_op jit(solution)/shard_map/ppermute | solution.py:322
  5.1 1.6 %shard_map.94 = (bf16[128,2048]{1,0:T(8,128)(2,1)S(1)}, bf16[128,2048]{1,0:T(8,128)(2,1)S(1)}) custom-call(s32[1]{0:T(128)} %bitcast.me_ref, bf16[128,4096]{1,0:T(8,128)(2,1)} %bitcast.21, bf16[128,4096]{1,0:T(8,128)(2,1)} %bitcast.30, bf16[128,4096]{1,0:T(8,128)(2,1)} %bitcast.9, bf16[128,4096]{1,0:T(8,128)(2,1)} %bitcast.15), custom_call_target="tpu_custom_call" | custom-call | flops 1000000000 | bytes 3145728 | tf_op jit(solution)/shard_map/pallas_call | solution.py:68
  6.7 0.0 copy-start.3
  6.7 0.0 copy-start.4
  6.7 6.6 %collective-permute-start = (bf16[128,2048]{1,0:T(8,128)(2,1)S(1)}, bf16[128,2048]{1,0:T(8,128)(2,1)S(1)}, u32[]{:S(2)}, u32[]{:S(2)}) collective-permute-start(bf16[128,2048]{1,0:T(8,128)(2,1)S(1)} %get-tuple-element.104.refs_0_.refs_1_), channel_id=1, source_target_pairs={{0,1},{1,0},{2,3},{3,2},{4,5},{5,4},{6,7},{7,6},{8,9},{9,8},{10,11... | collective-permute-start | bytes 1572872 | tf_op jit(solution)/shard_map/ppermute | solution.py:322
  13.4 0.1 collective-permute-start.1
  13.5 1.4 %collective-permute-done = bf16[128,2048]{1,0:T(8,128)(2,1)S(1)} collective-permute-done((bf16[128,2048]{1,0:T(8,128)(2,1)S(1)}, bf16[128,2048]{1,0:T(8,128)(2,1)S(1)}, u32[]{:S(2)}, u32[]{:S(2)}) %collective-permute-start) | collective-permute-done | bytes 524320 | tf_op jit(solution)/shard_map/ppermute | solution.py:322
  14.9 0.7 %collective-permute-done.1 = bf16[128,2048]{1,0:T(8,128)(2,1)S(1)} collective-permute-done((bf16[128,2048]{1,0:T(8,128)(2,1)S(1)}, bf16[128,2048]{1,0:T(8,128)(2,1)S(1)}, u32[]{:S(2)}, u32[]{:S(2)}) %collective-permute-start.1) | collective-permute-done | bytes 524320 | tf_op jit(solution)/shard_map/ppermute | solution.py:322
  15.7 0.1 pad_maximum_fusion.got_x.refs_3_
  15.7 0.1 collective-permute-start.7
  15.8 0.0 copy-done.3
  15.9 0.0 copy-done.4
  15.9 1.7 %shard_map.95 = (bf16[16,128,384]{2,1,0:T(8,128)(2,1)S(1)}, bf16[16,128,384]{2,1,0:T(8,128)(2,1)S(1)}) custom-call(s32[1]{0:T(128)} %bitcast.me_ref, s32[16]{0:T(128)S(1)} %copy-done.4, bf16[16,256]{1,0:T(8,128)(2,1)S(1)} %copy-done.3), custom_call_target="tpu_custom_call" | custom-call | flops 2048 | bytes 2048 | tf_op jit(solution)/shard_map/pallas_call | solution.py:123
  17.6 1.6 %shard_map.96 = (f32[16,256]{1,0:T(8,128)S(1)}, f32[16,256]{1,0:T(8,128)S(1)}) custom-call(s32[1]{0:T(128)} %bitcast.me_ref, s32[16]{0:T(128)S(1)} %copy-done.4, bf16[128,4096]{1,0:T(8,128)(2,1)S(1)} %shard_map.93.mine_p.refs_0_, bf16[128,4096]{1,0:T(8,128)(2,1)S(1)} %pad_maximum_fusion.got_x.refs_3_, ...), custom_call_target="tpu_custom_call" | custom-call | flops 2048 | bytes 2048 | tf_op jit(solution)/shard_map/pallas_call | solution.py:182
  19.2 0.0 collective-permute-done.2.got_p.refs_2_
  19.2 0.0 copy-start
  19.2 0.0 copy-start.1
  19.2 0.0 copy-start.2
  19.2 0.9 %shard_map.97 = f32[16,256]{1,0:T(8,128)S(1)} custom-call(s32[1]{0:T(128)} %bitcast.me_ref, f32[16,256]{1,0:T(8,128)S(1)} %get-tuple-element.84.in_ref, f32[16,256]{1,0:T(8,128)S(1)} %get-tuple-element.85.weight_ref, bf16[128,4096]{1,0:T(8,128)(2,1)S(1)} %shard_map.93.mine_p.refs_0_, bf16[128,4096]{1,0:T(8,128)(2,1)S(1)} %collective-permute-done.2.got_p.refs_2_, ...), custom_call_target="tpu_custom_call" | custom-call | flops 2048 | bytes 2048 | tf_op jit(solution)/shard_map/pallas_call | solution.py:237
  20.1 4.9 %collective-permute-start.8 = (bf16[128,4096]{1,0:T(8,128)(2,1)S(1)}, bf16[128,4096]{1,0:T(8,128)(2,1)S(1)}, u32[]{:S(2)}, u32[]{:S(2)}) collective-permute-start(bf16[128,4096]{1,0:T(8,128)(2,1)S(1)} %collective-permute-done.2.got_p.refs_2_), channel_id=1, source_target_pairs={{0,1},{1,0},{2,3},{3,2},{4,5},{5,4},{6,7},{7,6},{8,9},{9,8},{10,11... | collective-permute-start | bytes 3145736 | tf_op jit(solution)/shard_map/ppermute | solution.py:322
  25.1 1.2 %collective-permute-start.3 = (f32[16,256]{1,0:T(8,128)S(1)}, f32[16,256]{1,0:T(8,128)S(1)}, u32[]{:S(2)}, u32[]{:S(2)}) collective-permute-start(f32[16,256]{1,0:T(8,128)S(1)} %shard_map.97), channel_id=1, source_target_pairs={{0,65},{1,64},{2,67},{3,66},{4,69},{5,68},{6,71},{7,70},{8,73},{9,... | collective-permute-start | bytes 49160 | tf_op jit(solution)/shard_map/ppermute | solution.py:346
  26.3 2.3 %collective-permute-done.3 = f32[16,256]{1,0:T(8,128)S(1)} collective-permute-done((f32[16,256]{1,0:T(8,128)S(1)}, f32[16,256]{1,0:T(8,128)S(1)}, u32[]{:S(2)}, u32[]{:S(2)}) %collective-permute-start.3) | collective-permute-done | bytes 16416 | tf_op jit(solution)/shard_map/ppermute | solution.py:346
  28.6 2.1 %collective-permute-start.4 = (f32[16,256]{1,0:T(8,128)S(1)}, f32[16,256]{1,0:T(8,128)S(1)}, u32[]{:S(2)}, u32[]{:S(2)}) collective-permute-start(f32[16,256]{1,0:T(8,128)S(1)} %add.24), channel_id=1, source_target_pairs={{0,193},{1,192},{2,195},{3,194},{4,197},{5,196},{6,199},{7,198},{8... | collective-permute-start | bytes 49160 | tf_op jit(solution)/shard_map/ppermute | solution.py:346
  30.7 2.5 %collective-permute-done.4 = f32[16,256]{1,0:T(8,128)S(1)} collective-permute-done((f32[16,256]{1,0:T(8,128)S(1)}, f32[16,256]{1,0:T(8,128)S(1)}, u32[]{:S(2)}, u32[]{:S(2)}) %collective-permute-start.4) | collective-permute-done | bytes 16416 | tf_op jit(solution)/shard_map/ppermute | solution.py:346
  33.2 0.0 collective-permute-start.5
  33.2 1.2 %collective-permute-done.5 = f32[16,256]{1,0:T(8,128)S(1)} collective-permute-done((f32[16,256]{1,0:T(8,128)S(1)}, f32[16,256]{1,0:T(8,128)S(1)}, u32[]{:S(2)}, u32[]{:S(2)}) %collective-permute-start.5) | collective-permute-done | bytes 16416 | tf_op jit(solution)/shard_map/ppermute | solution.py:340
  34.4 0.0 collective-permute-start.6
  34.4 3.2 %collective-permute-done.6 = f32[16,256]{1,0:T(8,128)S(1)} collective-permute-done((f32[16,256]{1,0:T(8,128)S(1)}, f32[16,256]{1,0:T(8,128)S(1)}, u32[]{:S(2)}, u32[]{:S(2)}) %collective-permute-start.6) | collective-permute-done | bytes 16416 | tf_op jit(solution)/shard_map/ppermute | solution.py:340
  37.6 0.0 collective-permute-done.7.refs_4_
  37.6 0.0 collective-permute-done.8.refs_5_
  37.6 0.1 collective-permute-start.9
  37.7 0.0 copy-done
  37.7 0.0 copy-done.1
  37.7 0.0 copy-done.2
  37.7 1.5 %shard_map.98 = (bf16[128,4096]{1,0:T(8,128)(2,1)}, bf16[128,4096]{1,0:T(8,128)(2,1)}, bf16[128,4096]{1,0:T(8,128)(2,1)}) custom-call(s32[1]{0:T(128)} %bitcast.me_ref, bf16[16,128,384]{2,1,0:T(8,128)(2,1)S(1)} %get-tuple-element.89.ahead_ref, bf16[16,128,384]{2,1,0:T(8,128)(2,1)S(1)} %get-tuple-element.90.back_ref, ...), custom_call_target="tpu_custom_call" | custom-call | flops 201326592 | bytes 3538944 | tf_op jit(solution)/shard_map/pallas_call | solution.py:294
  39.2 2.5 %collective-permute-done.9 = f32[16,256]{1,0:T(8,128)S(1)} collective-permute-done((f32[16,256]{1,0:T(8,128)S(1)}, f32[16,256]{1,0:T(8,128)S(1)}, u32[]{:S(2)}, u32[]{:S(2)}) %collective-permute-start.9) | collective-permute-done | bytes 16416 | tf_op jit(solution)/shard_map/ppermute | solution.py:340
  41.8 1.7 %collective-permute-start.10 = (f32[16,256]{1,0:T(8,128)S(1)}, f32[16,256]{1,0:T(8,128)S(1)}, u32[]{:S(2)}, u32[]{:S(2)}) collective-permute-start(f32[16,256]{1,0:T(8,128)S(1)} %add.28), channel_id=1, source_target_pairs={{0,57},{1,56},{2,59},{3,58},{4,61},{5,60},{6,63},{7,62},{8,49},{9,... | collective-permute-start | bytes 49160 | tf_op jit(solution)/shard_map/ppermute | solution.py:340
  43.5 1.4 %shard_map.99 = (bf16[128,4096]{1,0:T(8,128)(2,1)}, bf16[128,4096]{1,0:T(8,128)(2,1)}, bf16[128,4096]{1,0:T(8,128)(2,1)}) custom-call(s32[1]{0:T(128)} %bitcast.me_ref, bf16[16,128,384]{2,1,0:T(8,128)(2,1)S(1)} %get-tuple-element.89.ahead_ref, ...), custom_call_target="tpu_custom_call", output_to_operand_aliasing={{0}: (12, {}), {1}: (13, {}), {2}: (14, {})} | custom-call | flops 201326592 | bytes 3538944 | tf_op jit(solution)/shard_map/pallas_call | solution.py:294
  44.9 1.4 %collective-permute-done.10 = f32[16,256]{1,0:T(8,128)S(1)} collective-permute-done((f32[16,256]{1,0:T(8,128)S(1)}, f32[16,256]{1,0:T(8,128)S(1)}, u32[]{:S(2)}, u32[]{:S(2)}) %collective-permute-start.10) | collective-permute-done | bytes 16416 | tf_op jit(solution)/shard_map/ppermute | solution.py:340
  46.3 0.0 collective-permute-start.11
  46.3 1.5 %shard_map.100 = (bf16[128,4096]{1,0:T(8,128)(2,1)}, bf16[128,4096]{1,0:T(8,128)(2,1)}, bf16[128,4096]{1,0:T(8,128)(2,1)}) custom-call(s32[1]{0:T(128)} %bitcast.me_ref, bf16[16,128,384]{2,1,0:T(8,128)(2,1)S(1)} %get-tuple-element.89.ahead_ref, ...), custom_call_target="tpu_custom_call", output_to_operand_aliasing={{0}: (12, {}), {1}: (13, {}), {2}: (14, {})} | custom-call | flops 201326592 | bytes 3538944 | tf_op jit(solution)/shard_map/pallas_call | solution.py:294
  47.8 1.7 %collective-permute-done.11 = f32[16,256]{1,0:T(8,128)S(1)} collective-permute-done((f32[16,256]{1,0:T(8,128)S(1)}, f32[16,256]{1,0:T(8,128)S(1)}, u32[]{:S(2)}, u32[]{:S(2)}) %collective-permute-start.11) | collective-permute-done | bytes 16416 | tf_op jit(solution)/shard_map/ppermute | solution.py:340
  49.5 2.0 %collective-permute-start.12 = (f32[16,256]{1,0:T(8,128)S(1)}, f32[16,256]{1,0:T(8,128)S(1)}, u32[]{:S(2)}, u32[]{:S(2)}) collective-permute-start(f32[16,256]{1,0:T(8,128)S(1)} %add.30), channel_id=1, source_target_pairs={{0,7},{1,6},{2,5},{3,4},{4,3},{5,2},{6,1},{7,0},{8,15},{9,14},{10,... | collective-permute-start | bytes 49160 | tf_op jit(solution)/shard_map/ppermute | solution.py:340
  51.5 1.4 %shard_map.101 = (bf16[128,4096]{1,0:T(8,128)(2,1)}, bf16[128,4096]{1,0:T(8,128)(2,1)}, bf16[128,4096]{1,0:T(8,128)(2,1)}) custom-call(s32[1]{0:T(128)} %bitcast.me_ref, bf16[16,128,384]{2,1,0:T(8,128)(2,1)S(1)} %get-tuple-element.89.ahead_ref, ...), custom_call_target="tpu_custom_call", output_to_operand_aliasing={{0}: (12, {}), {1}: (13, {}), {2}: (14, {})} | custom-call | flops 201326592 | bytes 3538944 | tf_op jit(solution)/shard_map/pallas_call | solution.py:294
  52.9 0.9 %collective-permute-done.12 = f32[16,256]{1,0:T(8,128)S(1)} collective-permute-done((f32[16,256]{1,0:T(8,128)S(1)}, f32[16,256]{1,0:T(8,128)S(1)}, u32[]{:S(2)}, u32[]{:S(2)}) %collective-permute-start.12) | collective-permute-done | bytes 16416 | tf_op jit(solution)/shard_map/ppermute | solution.py:340
  53.9 0.6 %add.31 = f32[16,256]{1,0:T(8,128)} add(f32[16,256]{1,0:T(8,128)S(1)} %add.30, f32[16,256]{1,0:T(8,128)S(1)} %collective-permute-done.12) | non-fusion elementwise | flops 4096 | bytes 49152 | tf_op jit(solution)/shard_map/add | solution.py:340
  (7 shorter events, 0.0 us)
Async XLA Ops:
  2.3 16.9 %collective-permute-start.2 = (bf16[128,4096]{1,0:T(8,128)(2,1)S(1)}, bf16[128,4096]{1,0:T(8,128)(2,1)S(1)}, u32[]{:S(2)}, u32[]{:S(2)}) collective-permute-start(bf16[128,4096]{1,0:T(8,128)(2,1)S(1)} %shard_map.93.mine_p.refs_0_), channel_id=1, source_target_pairs={{0,63},{1,2},{2,1},{3,4},{4,3},{5,6},{6,5},{7,8},{8,7},{9,10},{10,... | collective-permute-start | bytes 3145736 | tf_op jit(solution)/shard_map/ppermute | solution.py:322
  6.7 9.1 %copy-start.3 = (bf16[16,256]{1,0:T(8,128)(2,1)S(1)}, bf16[16,256]{1,0:T(8,128)(2,1)}, u32[]{:S(2)}) copy-start(bf16[16,256]{1,0:T(8,128)(2,1)} %filt_ref.1) | copy-start | bytes 24580
  6.7 9.1 %copy-start.4 = (s32[16]{0:T(128)S(1)}, s32[16]{0:T(128)}, u32[]{:S(2)}) copy-start(s32[16]{0:T(128)} %reach_ref.3) | copy-start | bytes 196
  6.7 8.2 %collective-permute-start = (bf16[128,2048]{1,0:T(8,128)(2,1)S(1)}, bf16[128,2048]{1,0:T(8,128)(2,1)S(1)}, u32[]{:S(2)}, u32[]{:S(2)}) collective-permute-start(bf16[128,2048]{1,0:T(8,128)(2,1)S(1)} %get-tuple-element.104.refs_0_.refs_1_), channel_id=1, source_target_pairs={{0,1},{1,0},{2,3},{3,2},{4,5},{5,4},{6,7},{7,6},{8,9},{9,8},{10,11... | collective-permute-start | bytes 1572872 | tf_op jit(solution)/shard_map/ppermute | solution.py:322
  13.4 2.3 %collective-permute-start.1 = (bf16[128,2048]{1,0:T(8,128)(2,1)S(1)}, bf16[128,2048]{1,0:T(8,128)(2,1)S(1)}, u32[]{:S(2)}, u32[]{:S(2)}) collective-permute-start(bf16[128,2048]{1,0:T(8,128)(2,1)S(1)} %get-tuple-element.133.refs_1_), channel_id=1, source_target_pairs={{0,1},{1,0},{2,3},{3,2},{4,5},{5,4},{6,7},{7,6},{8,9},{9,8},{10,11... | collective-permute-start | bytes 1572872 | tf_op jit(solution)/shard_map/ppermute | solution.py:322
  15.7 21.8 %collective-permute-start.7 = (bf16[128,4096]{1,0:T(8,128)(2,1)S(1)}, bf16[128,4096]{1,0:T(8,128)(2,1)S(1)}, u32[]{:S(2)}, u32[]{:S(2)}) collective-permute-start(bf16[128,4096]{1,0:T(8,128)(2,1)S(1)} %pad_maximum_fusion.got_x.refs_3_), channel_id=1, source_target_pairs={{0,63},{1,2},{2,1},{3,4},{4,3},{5,6},{6,5},{7,8},{8,7},{9,10},{10,... | collective-permute-start | bytes 3145736 | tf_op jit(solution)/shard_map/ppermute | solution.py:322
  19.2 18.5 %copy-start = (bf16[1,128,4096]{2,1,0:T(8,128)(2,1)S(1)}, bf16[1,128,4096]{2,1,0:T(8,128)(2,1)}, u32[]{:S(2)}) copy-start(bf16[1,128,4096]{2,1,0:T(8,128)(2,1)} %param.7) | copy-start | bytes 3145732
  19.2 18.5 %copy-start.1 = (bf16[1,128,4096]{2,1,0:T(8,128)(2,1)S(1)}, bf16[1,128,4096]{2,1,0:T(8,128)(2,1)}, u32[]{:S(2)}) copy-start(bf16[1,128,4096]{2,1,0:T(8,128)(2,1)} %param.8) | copy-start | bytes 3145732
  19.2 18.5 %copy-start.2 = (bf16[1,128,4096]{2,1,0:T(8,128)(2,1)S(1)}, bf16[1,128,4096]{2,1,0:T(8,128)(2,1)}, u32[]{:S(2)}) copy-start(bf16[1,128,4096]{2,1,0:T(8,128)(2,1)} %param.9) | copy-start | bytes 3145732
  20.1 17.5 %collective-permute-start.8 = (bf16[128,4096]{1,0:T(8,128)(2,1)S(1)}, bf16[128,4096]{1,0:T(8,128)(2,1)S(1)}, u32[]{:S(2)}, u32[]{:S(2)}) collective-permute-start(bf16[128,4096]{1,0:T(8,128)(2,1)S(1)} %collective-permute-done.2.got_p.refs_2_), channel_id=1, source_target_pairs={{0,1},{1,0},{2,3},{3,2},{4,5},{5,4},{6,7},{7,6},{8,9},{9,8},{10,11... | collective-permute-start | bytes 3145736 | tf_op jit(solution)/shard_map/ppermute | solution.py:322
  25.1 3.5 %collective-permute-start.3 = (f32[16,256]{1,0:T(8,128)S(1)}, f32[16,256]{1,0:T(8,128)S(1)}, u32[]{:S(2)}, u32[]{:S(2)}) collective-permute-start(f32[16,256]{1,0:T(8,128)S(1)} %shard_map.97), channel_id=1, source_target_pairs={{0,65},{1,64},{2,67},{3,66},{4,69},{5,68},{6,71},{7,70},{8,73},{9,... | collective-permute-start | bytes 49160 | tf_op jit(solution)/shard_map/ppermute | solution.py:346
  28.6 4.7 %collective-permute-start.4 = (f32[16,256]{1,0:T(8,128)S(1)}, f32[16,256]{1,0:T(8,128)S(1)}, u32[]{:S(2)}, u32[]{:S(2)}) collective-permute-start(f32[16,256]{1,0:T(8,128)S(1)} %add.24), channel_id=1, source_target_pairs={{0,193},{1,192},{2,195},{3,194},{4,197},{5,196},{6,199},{7,198},{8... | collective-permute-start | bytes 49160 | tf_op jit(solution)/shard_map/ppermute | solution.py:346
  33.2 1.2 %collective-permute-start.5 = (f32[16,256]{1,0:T(8,128)S(1)}, f32[16,256]{1,0:T(8,128)S(1)}, u32[]{:S(2)}, u32[]{:S(2)}) collective-permute-start(f32[16,256]{1,0:T(8,128)S(1)} %add.25), channel_id=1, source_target_pairs={{0,1},{1,0},{2,3},{3,2},{4,5},{5,4},{6,7},{7,6},{8,9},{9,8},{10,11... | collective-permute-start | bytes 49160 | tf_op jit(solution)/shard_map/ppermute | solution.py:340
  34.4 3.2 %collective-permute-start.6 = (f32[16,256]{1,0:T(8,128)S(1)}, f32[16,256]{1,0:T(8,128)S(1)}, u32[]{:S(2)}, u32[]{:S(2)}) collective-permute-start(f32[16,256]{1,0:T(8,128)S(1)} %add.26), channel_id=1, source_target_pairs={{0,9},{1,8},{2,11},{3,10},{4,13},{5,12},{6,15},{7,14},{8,1},{9,0},... | collective-permute-start | bytes 49160 | tf_op jit(solution)/shard_map/ppermute | solution.py:340
  37.6 4.2 %collective-permute-start.9 = (f32[16,256]{1,0:T(8,128)S(1)}, f32[16,256]{1,0:T(8,128)S(1)}, u32[]{:S(2)}, u32[]{:S(2)}) collective-permute-start(f32[16,256]{1,0:T(8,128)S(1)} %add.27), channel_id=1, source_target_pairs={{0,17},{1,16},{2,19},{3,18},{4,21},{5,20},{6,23},{7,22},{8,25},{9,... | collective-permute-start | bytes 49160 | tf_op jit(solution)/shard_map/ppermute | solution.py:340
  41.8 4.6 %collective-permute-start.10 = (f32[16,256]{1,0:T(8,128)S(1)}, f32[16,256]{1,0:T(8,128)S(1)}, u32[]{:S(2)}, u32[]{:S(2)}) collective-permute-start(f32[16,256]{1,0:T(8,128)S(1)} %add.28), channel_id=1, source_target_pairs={{0,57},{1,56},{2,59},{3,58},{4,61},{5,60},{6,63},{7,62},{8,49},{9,... | collective-permute-start | bytes 49160 | tf_op jit(solution)/shard_map/ppermute | solution.py:340
  46.3 3.2 %collective-permute-start.11 = (f32[16,256]{1,0:T(8,128)S(1)}, f32[16,256]{1,0:T(8,128)S(1)}, u32[]{:S(2)}, u32[]{:S(2)}) collective-permute-start(f32[16,256]{1,0:T(8,128)S(1)} %add.29), channel_id=1, source_target_pairs={{0,3},{1,2},{2,1},{3,0},{4,7},{5,6},{6,5},{7,4},{8,11},{9,10},{10,... | collective-permute-start | bytes 49160 | tf_op jit(solution)/shard_map/ppermute | solution.py:340
  49.5 4.4 %collective-permute-start.12 = (f32[16,256]{1,0:T(8,128)S(1)}, f32[16,256]{1,0:T(8,128)S(1)}, u32[]{:S(2)}, u32[]{:S(2)}) collective-permute-start(f32[16,256]{1,0:T(8,128)S(1)} %add.30), channel_id=1, source_target_pairs={{0,7},{1,6},{2,5},{3,4},{4,3},{5,2},{6,1},{7,0},{8,15},{9,14},{10,... | collective-permute-start | bytes 49160 | tf_op jit(solution)/shard_map/ppermute | solution.py:340

commit v4 on v3

--- a/solution.py
+++ b/solution.py
@@ -315,11 +315,23 @@
     me = lax.axis_index("ctx").astype(jnp.int32)[None]
     last = ctx_n - 1
 
-    across = [(i, (i + 1) % ctx_n if i & 1 else (i - 1) % ctx_n) for i in range(ctx_n)]
-    within = [(i, i ^ 1) for i in range(ctx_n)]
+    def partner(d, i):
+        if i in (0, last):
+            return (d ^ 1) * ctx_n + i
+        return d * ctx_n + (i + 1 if i & 1 else i - 1)
+
+    across = [(d * ctx_n + i, partner(d, i)) for d in range(dp_n) for i in range(ctx_n)]
+    relay = [
+        (d * ctx_n + i, d * ctx_n + (i + (1 if i & 1 else -1)) % ctx_n)
+        for d in range(dp_n)
+        for i in range(ctx_n)
+    ]
+    within = [
+        (d * ctx_n + i, d * ctx_n + (i ^ 1)) for d in range(dp_n) for i in range(ctx_n)
+    ]
 
     def trade(chunks, route):
-        return [lax.ppermute(x, "ctx", route) for x in chunks]
+        return [lax.ppermute(x, ("dp", "ctx"), route) for x in chunks]
 
     p_n, x_n = 1, 2
     mine_p = gate_product(me, k, v, grad, q, p_n, 1)
@@ -328,7 +340,7 @@
     mine_x = gate_product(me, grad, q, k, v, x_n, 10**9)
     got_x = [jnp.concatenate(trade(mine_x, within), axis=1)]
     got_x, me = lax.optimization_barrier((got_x, me))
-    got2_p = trade(got_x, across)
+    got2_p = trade(got_x, relay)
     ahead, back = toeplitz(me, last, reaches, filters)
     ahead, me = lax.optimization_barrier((ahead, me))
     inside, weight = taps_inside(scale, me, reaches, mine_p[0], mine_x, got_x[0])

time: 54.6 us -> 53.4 us (0.978)
  starting transfers between devices: 21.7 us -> 20.3 us
    ppermute x5, starting transfers between devices: 14.6 us -> 7.47 us  [trade(): return [lax.ppermute(x, ('dp', 'ctx'), route) for x in chunks]]
    ppermute x6, starting transfers between devices: 3.83 us -> 10.9 us  [trade_ctx(): return x + lax.ppermute(x, 'ctx', [(i, i ^ mask) for i in range(ctx_n)])]
    ppermute x6, waiting for transfers between devices: 10.9 us -> 6.33 us  [trade_ctx(): return x + lax.ppermute(x, 'ctx', [(i, i ^ mask) for i in range(ctx_n)])]
    ppermute x5, waiting for transfers between devices: 2.19 us -> 5.74 us  [trade(): return [lax.ppermute(x, ('dp', 'ctx'), route) for x in chunks]]
    ppermute x2, starting transfers between devices: 3.34 us -> 1.99 us  [trade_dp(): return x + lax.ppermute(x, ('dp', 'ctx'), route)]
    ppermute x2, waiting for transfers between devices: 4.8 us -> 6.05 us  [trade_dp(): return x + lax.ppermute(x, ('dp', 'ctx'), route)]
  transfers between devices with their start and end apart: 13 -> 13, of which waited for: 10 -> 9; matrix products, arithmetic and copies ran while one was open for 0% -> 0% of each run, Pallas kernels for 21% -> 22%
where the time goes in v4:
time: 53.4 us; the launch traced here: 53.2 us
  starting transfers between devices  20.3 us (38%)
  waiting for transfers between devices  18.1 us (34%)
  Pallas kernels  13.3 us (25%)
  between operations  0.73 us (1%)
  other arithmetic  0.71 us (1%)
    ppermute x6, starting transfers between devices, trade_ctx(): return x + lax.ppermute(x, 'ctx', [(i, i ^ mask) for i in range(ctx_n)])  10.9 us
    ppermute x5, starting transfers between devices, trade(): return [lax.ppermute(x, ('dp', 'ctx'), route) for x in chunks]  7.47 us
    ppermute x6, waiting for transfers between devices, trade_ctx(): return x + lax.ppermute(x, 'ctx', [(i, i ^ mask) for i in range(ctx_n)])  6.33 us
    ppermute x2, waiting for transfers between devices, trade_dp(): return x + lax.ppermute(x, ('dp', 'ctx'), route)  6.05 us
    pallas_call x4, Pallas kernels, grads_piece(): pl.pallas_call(kernel, out_shape=[shape] * 3, grid=(count // step,), in_s...  5.84 us
    ppermute x5, waiting for transfers between devices, trade(): return [lax.ppermute(x, ('dp', 'ctx'), route) for x in chunks]  5.74 us
    pallas_call x2, Pallas kernels, gate_product(): pl.pallas_call(kernel, out_shape=[jax.ShapeDtypeStruct((tok_n, width), BF...  3.27 us
    ppermute x2, starting transfers between devices, trade_dp(): return x + lax.ppermute(x, ('dp', 'ctx'), route)  1.99 us
  transfers between devices with their start and end apart: 13, of which 9 were waited for; matrix products, arithmetic and copies ran while one was open for 0% of the time, Pallas kernels for 22%

profile of v4, /device:TPU:1, one launch (start us, length us, event | category | flops | bytes accessed | tf_op | source)
XLA Modules:
  0.0 53.2 jit_solution(622190352770596469)
XLA Ops:
  0.6 1.6 %shard_map.93.mine_p.refs_0_ = bf16[128,4096]{1,0:T(8,128)(2,1)S(1)} custom-call(s32[1]{0:T(128)} %bitcast.me_ref, bf16[128,4096]{1,0:T(8,128)(2,1)} %bitcast.8, bf16[128,4096]{1,0:T(8,128)(2,1)} %bitcast.14, bf16[128,4096]{1,0:T(8,128)(2,1)} %bitcast.20, bf16[128,4096]{1,0:T(8,128)(2,1)} %bitcast.29), custom_call_target="tpu_custom_call" | custom-call | flops 1 | bytes 3145728 | tf_op jit(solution)/shard_map/pallas_call | solution.py:68
  2.3 2.8 %collective-permute-start.2 = (bf16[128,4096]{1,0:T(8,128)(2,1)S(1)}, bf16[128,4096]{1,0:T(8,128)(2,1)S(1)}, u32[]{:S(2)}, u32[]{:S(2)}) collective-permute-start(bf16[128,4096]{1,0:T(8,128)(2,1)S(1)} %shard_map.93.mine_p.refs_0_), channel_id=1, source_target_pairs={{0,64},{1,2},{2,1},{3,4},{4,3},{5,6},{6,5},{7,8},{8,7},{9,10},{10,... | collective-permute-start | bytes 3145736 | tf_op jit(solution)/shard_map/ppermute | solution.py:334
  5.1 1.6 %shard_map.94 = (bf16[128,2048]{1,0:T(8,128)(2,1)S(1)}, bf16[128,2048]{1,0:T(8,128)(2,1)S(1)}) custom-call(s32[1]{0:T(128)} %bitcast.me_ref, bf16[128,4096]{1,0:T(8,128)(2,1)} %bitcast.21, bf16[128,4096]{1,0:T(8,128)(2,1)} %bitcast.30, bf16[128,4096]{1,0:T(8,128)(2,1)} %bitcast.9, bf16[128,4096]{1,0:T(8,128)(2,1)} %bitcast.15), custom_call_target="tpu_custom_call" | custom-call | flops 1000000000 | bytes 3145728 | tf_op jit(solution)/shard_map/pallas_call | solution.py:68
  6.7 0.0 copy-start.3
  6.7 0.0 copy-start.4
  6.7 0.7 %collective-permute-start = (bf16[128,2048]{1,0:T(8,128)(2,1)S(1)}, bf16[128,2048]{1,0:T(8,128)(2,1)S(1)}, u32[]{:S(2)}, u32[]{:S(2)}) collective-permute-start(bf16[128,2048]{1,0:T(8,128)(2,1)S(1)} %get-tuple-element.104.refs_0_.refs_1_), channel_id=1, source_target_pairs={{0,1},{1,0},{2,3},{3,2},{4,5},{5,4},{6,7},{7,6},{8,9},{9,8},{10,11... | collective-permute-start | bytes 1572872 | tf_op jit(solution)/shard_map/ppermute | solution.py:334
  7.4 0.1 collective-permute-start.1
  7.5 1.4 %collective-permute-done = bf16[128,2048]{1,0:T(8,128)(2,1)S(1)} collective-permute-done((bf16[128,2048]{1,0:T(8,128)(2,1)S(1)}, bf16[128,2048]{1,0:T(8,128)(2,1)S(1)}, u32[]{:S(2)}, u32[]{:S(2)}) %collective-permute-start) | collective-permute-done | bytes 524320 | tf_op jit(solution)/shard_map/ppermute | solution.py:334
  8.9 0.7 %collective-permute-done.1 = bf16[128,2048]{1,0:T(8,128)(2,1)S(1)} collective-permute-done((bf16[128,2048]{1,0:T(8,128)(2,1)S(1)}, bf16[128,2048]{1,0:T(8,128)(2,1)S(1)}, u32[]{:S(2)}, u32[]{:S(2)}) %collective-permute-start.1) | collective-permute-done | bytes 524320 | tf_op jit(solution)/shard_map/ppermute | solution.py:334
  9.7 0.1 pad_maximum_fusion.got_x.refs_3_
  9.8 1.2 %collective-permute-start.7 = (bf16[128,4096]{1,0:T(8,128)(2,1)S(1)}, bf16[128,4096]{1,0:T(8,128)(2,1)S(1)}, u32[]{:S(2)}, u32[]{:S(2)}) collective-permute-start(bf16[128,4096]{1,0:T(8,128)(2,1)S(1)} %pad_maximum_fusion.got_x.refs_3_), channel_id=1, source_target_pairs={{0,63},{1,2},{2,1},{3,4},{4,3},{5,6},{6,5},{7,8},{8,7},{9,10},{10,... | collective-permute-start | bytes 3145736 | tf_op jit(solution)/shard_map/ppermute | solution.py:334
  11.0 0.0 copy-done.3
  11.0 0.0 copy-done.4
  11.0 1.7 %shard_map.95 = (bf16[16,128,384]{2,1,0:T(8,128)(2,1)S(1)}, bf16[16,128,384]{2,1,0:T(8,128)(2,1)S(1)}) custom-call(s32[1]{0:T(128)} %bitcast.me_ref, s32[16]{0:T(128)S(1)} %copy-done.4, bf16[16,256]{1,0:T(8,128)(2,1)S(1)} %copy-done.3), custom_call_target="tpu_custom_call" | custom-call | flops 2048 | bytes 2048 | tf_op jit(solution)/shard_map/pallas_call | solution.py:123
  12.7 1.6 %shard_map.96 = (f32[16,256]{1,0:T(8,128)S(1)}, f32[16,256]{1,0:T(8,128)S(1)}) custom-call(s32[1]{0:T(128)} %bitcast.me_ref, s32[16]{0:T(128)S(1)} %copy-done.4, bf16[128,4096]{1,0:T(8,128)(2,1)S(1)} %shard_map.93.mine_p.refs_0_, bf16[128,4096]{1,0:T(8,128)(2,1)S(1)} %pad_maximum_fusion.got_x.refs_3_, ...), custom_call_target="tpu_custom_call" | custom-call | flops 2048 | bytes 2048 | tf_op jit(solution)/shard_map/pallas_call | solution.py:182
  14.3 3.5 %collective-permute-done.2.got_p.refs_2_ = bf16[128,4096]{1,0:T(8,128)(2,1)S(1)} collective-permute-done((bf16[128,4096]{1,0:T(8,128)(2,1)S(1)}, bf16[128,4096]{1,0:T(8,128)(2,1)S(1)}, u32[]{:S(2)}, u32[]{:S(2)}) %collective-permute-start.2) | collective-permute-done | bytes 1048608 | tf_op jit(solution)/shard_map/ppermute | solution.py:334
  17.8 0.0 copy-start
  17.8 0.0 copy-start.1
  17.8 0.0 copy-start.2
  17.8 0.9 %shard_map.97 = f32[16,256]{1,0:T(8,128)S(1)} custom-call(s32[1]{0:T(128)} %bitcast.me_ref, f32[16,256]{1,0:T(8,128)S(1)} %get-tuple-element.84.in_ref, f32[16,256]{1,0:T(8,128)S(1)} %get-tuple-element.85.weight_ref, bf16[128,4096]{1,0:T(8,128)(2,1)S(1)} %shard_map.93.mine_p.refs_0_, bf16[128,4096]{1,0:T(8,128)(2,1)S(1)} %collective-permute-done.2.got_p.refs_2_, ...), custom_call_target="tpu_custom_call" | custom-call | flops 2048 | bytes 2048 | tf_op jit(solution)/shard_map/pallas_call | solution.py:237
  18.7 2.7 %collective-permute-start.8 = (bf16[128,4096]{1,0:T(8,128)(2,1)S(1)}, bf16[128,4096]{1,0:T(8,128)(2,1)S(1)}, u32[]{:S(2)}, u32[]{:S(2)}) collective-permute-start(bf16[128,4096]{1,0:T(8,128)(2,1)S(1)} %collective-permute-done.2.got_p.refs_2_), channel_id=1, source_target_pairs={{0,1},{1,0},{2,3},{3,2},{4,5},{5,4},{6,7},{7,6},{8,9},{9,8},{10,11... | collective-permute-start | bytes 3145736 | tf_op jit(solution)/shard_map/ppermute | solution.py:334
  21.5 0.5 collective-permute-start.3
  22.0 3.0 %collective-permute-done.3 = f32[16,256]{1,0:T(8,128)S(1)} collective-permute-done((f32[16,256]{1,0:T(8,128)S(1)}, f32[16,256]{1,0:T(8,128)S(1)}, u32[]{:S(2)}, u32[]{:S(2)}) %collective-permute-start.3) | collective-permute-done | bytes 16416 | tf_op jit(solution)/shard_map/ppermute | solution.py:358
  24.9 1.5 %collective-permute-start.4 = (f32[16,256]{1,0:T(8,128)S(1)}, f32[16,256]{1,0:T(8,128)S(1)}, u32[]{:S(2)}, u32[]{:S(2)}) collective-permute-start(f32[16,256]{1,0:T(8,128)S(1)} %add.24), channel_id=1, source_target_pairs={{0,193},{1,192},{2,195},{3,194},{4,197},{5,196},{6,199},{7,198},{8... | collective-permute-start | bytes 49160 | tf_op jit(solution)/shard_map/ppermute | solution.py:358
  26.4 3.1 %collective-permute-done.4 = f32[16,256]{1,0:T(8,128)S(1)} collective-permute-done((f32[16,256]{1,0:T(8,128)S(1)}, f32[16,256]{1,0:T(8,128)S(1)}, u32[]{:S(2)}, u32[]{:S(2)}) %collective-permute-start.4) | collective-permute-done | bytes 16416 | tf_op jit(solution)/shard_map/ppermute | solution.py:358
  29.5 0.0 collective-permute-start.5
  29.5 1.2 %collective-permute-done.5 = f32[16,256]{1,0:T(8,128)S(1)} collective-permute-done((f32[16,256]{1,0:T(8,128)S(1)}, f32[16,256]{1,0:T(8,128)S(1)}, u32[]{:S(2)}, u32[]{:S(2)}) %collective-permute-start.5) | collective-permute-done | bytes 16416 | tf_op jit(solution)/shard_map/ppermute | solution.py:352
  30.7 1.5 %collective-permute-start.6 = (f32[16,256]{1,0:T(8,128)S(1)}, f32[16,256]{1,0:T(8,128)S(1)}, u32[]{:S(2)}, u32[]{:S(2)}) collective-permute-start(f32[16,256]{1,0:T(8,128)S(1)} %add.26), channel_id=1, source_target_pairs={{0,9},{1,8},{2,11},{3,10},{4,13},{5,12},{6,15},{7,14},{8,1},{9,0},... | collective-permute-start | bytes 49160 | tf_op jit(solution)/shard_map/ppermute | solution.py:352
  32.2 1.6 %collective-permute-done.6 = f32[16,256]{1,0:T(8,128)S(1)} collective-permute-done((f32[16,256]{1,0:T(8,128)S(1)}, f32[16,256]{1,0:T(8,128)S(1)}, u32[]{:S(2)}, u32[]{:S(2)}) %collective-permute-start.6) | collective-permute-done | bytes 16416 | tf_op jit(solution)/shard_map/ppermute | solution.py:352
  33.9 0.0 collective-permute-done.7.refs_4_
  33.9 0.0 collective-permute-done.8.refs_5_
  33.9 3.1 %collective-permute-start.9 = (f32[16,256]{1,0:T(8,128)S(1)}, f32[16,256]{1,0:T(8,128)S(1)}, u32[]{:S(2)}, u32[]{:S(2)}) collective-permute-start(f32[16,256]{1,0:T(8,128)S(1)} %add.27), channel_id=1, source_target_pairs={{0,17},{1,16},{2,19},{3,18},{4,21},{5,20},{6,23},{7,22},{8,25},{9,... | collective-permute-start | bytes 49160 | tf_op jit(solution)/shard_map/ppermute | solution.py:352
  37.0 0.0 copy-done
  37.0 0.0 copy-done.1
  37.0 0.0 copy-done.2
  37.0 1.5 %shard_map.98 = (bf16[128,4096]{1,0:T(8,128)(2,1)}, bf16[128,4096]{1,0:T(8,128)(2,1)}, bf16[128,4096]{1,0:T(8,128)(2,1)}) custom-call(s32[1]{0:T(128)} %bitcast.me_ref, bf16[16,128,384]{2,1,0:T(8,128)(2,1)S(1)} %get-tuple-element.89.ahead_ref, bf16[16,128,384]{2,1,0:T(8,128)(2,1)S(1)} %get-tuple-element.90.back_ref, ...), custom_call_target="tpu_custom_call" | custom-call | flops 201326592 | bytes 3538944 | tf_op jit(solution)/shard_map/pallas_call | solution.py:294
  38.5 0.0 collective-permute-done.9
  38.5 5.0 %collective-permute-start.10 = (f32[16,256]{1,0:T(8,128)S(1)}, f32[16,256]{1,0:T(8,128)S(1)}, u32[]{:S(2)}, u32[]{:S(2)}) collective-permute-start(f32[16,256]{1,0:T(8,128)S(1)} %add.28), channel_id=1, source_target_pairs={{0,57},{1,56},{2,59},{3,58},{4,61},{5,60},{6,63},{7,62},{8,49},{9,... | collective-permute-start | bytes 49160 | tf_op jit(solution)/shard_map/ppermute | solution.py:352
  43.5 1.4 %shard_map.99 = (bf16[128,4096]{1,0:T(8,128)(2,1)}, bf16[128,4096]{1,0:T(8,128)(2,1)}, bf16[128,4096]{1,0:T(8,128)(2,1)}) custom-call(s32[1]{0:T(128)} %bitcast.me_ref, bf16[16,128,384]{2,1,0:T(8,128)(2,1)S(1)} %get-tuple-element.89.ahead_ref, ...), custom_call_target="tpu_custom_call", output_to_operand_aliasing={{0}: (12, {}), {1}: (13, {}), {2}: (14, {})} | custom-call | flops 201326592 | bytes 3538944 | tf_op jit(solution)/shard_map/pallas_call | solution.py:294
  44.9 0.0 collective-permute-done.10
  45.0 0.1 collective-permute-start.11
  45.0 1.5 %shard_map.100 = (bf16[128,4096]{1,0:T(8,128)(2,1)}, bf16[128,4096]{1,0:T(8,128)(2,1)}, bf16[128,4096]{1,0:T(8,128)(2,1)}) custom-call(s32[1]{0:T(128)} %bitcast.me_ref, bf16[16,128,384]{2,1,0:T(8,128)(2,1)S(1)} %get-tuple-element.89.ahead_ref, ...), custom_call_target="tpu_custom_call", output_to_operand_aliasing={{0}: (12, {}), {1}: (13, {}), {2}: (14, {})} | custom-call | flops 201326592 | bytes 3538944 | tf_op jit(solution)/shard_map/pallas_call | solution.py:294
  46.5 1.7 %collective-permute-done.11 = f32[16,256]{1,0:T(8,128)S(1)} collective-permute-done((f32[16,256]{1,0:T(8,128)S(1)}, f32[16,256]{1,0:T(8,128)S(1)}, u32[]{:S(2)}, u32[]{:S(2)}) %collective-permute-start.11) | collective-permute-done | bytes 16416 | tf_op jit(solution)/shard_map/ppermute | solution.py:352
  48.2 1.2 %collective-permute-start.12 = (f32[16,256]{1,0:T(8,128)S(1)}, f32[16,256]{1,0:T(8,128)S(1)}, u32[]{:S(2)}, u32[]{:S(2)}) collective-permute-start(f32[16,256]{1,0:T(8,128)S(1)} %add.30), channel_id=1, source_target_pairs={{0,7},{1,6},{2,5},{3,4},{4,3},{5,2},{6,1},{7,0},{8,15},{9,14},{10,... | collective-permute-start | bytes 49160 | tf_op jit(solution)/shard_map/ppermute | solution.py:352
  49.4 1.4 %shard_map.101 = (bf16[128,4096]{1,0:T(8,128)(2,1)}, bf16[128,4096]{1,0:T(8,128)(2,1)}, bf16[128,4096]{1,0:T(8,128)(2,1)}) custom-call(s32[1]{0:T(128)} %bitcast.me_ref, bf16[16,128,384]{2,1,0:T(8,128)(2,1)S(1)} %get-tuple-element.89.ahead_ref, ...), custom_call_target="tpu_custom_call", output_to_operand_aliasing={{0}: (12, {}), {1}: (13, {}), {2}: (14, {})} | custom-call | flops 201326592 | bytes 3538944 | tf_op jit(solution)/shard_map/pallas_call | solution.py:294
  50.8 1.8 %collective-permute-done.12 = f32[16,256]{1,0:T(8,128)S(1)} collective-permute-done((f32[16,256]{1,0:T(8,128)S(1)}, f32[16,256]{1,0:T(8,128)S(1)}, u32[]{:S(2)}, u32[]{:S(2)}) %collective-permute-start.12) | collective-permute-done | bytes 16416 | tf_op jit(solution)/shard_map/ppermute | solution.py:352
  52.6 0.6 %add.31 = f32[16,256]{1,0:T(8,128)} add(f32[16,256]{1,0:T(8,128)S(1)} %add.30, f32[16,256]{1,0:T(8,128)S(1)} %collective-permute-done.12) | non-fusion elementwise | flops 4096 | bytes 49152 | tf_op jit(solution)/shard_map/add | solution.py:352
  (7 shorter events, 0.0 us)
Async XLA Ops:
  2.3 15.6 %collective-permute-start.2 = (bf16[128,4096]{1,0:T(8,128)(2,1)S(1)}, bf16[128,4096]{1,0:T(8,128)(2,1)S(1)}, u32[]{:S(2)}, u32[]{:S(2)}) collective-permute-start(bf16[128,4096]{1,0:T(8,128)(2,1)S(1)} %shard_map.93.mine_p.refs_0_), channel_id=1, source_target_pairs={{0,64},{1,2},{2,1},{3,4},{4,3},{5,6},{6,5},{7,8},{8,7},{9,10},{10,... | collective-permute-start | bytes 3145736 | tf_op jit(solution)/shard_map/ppermute | solution.py:334
  6.7 4.3 %copy-start.3 = (bf16[16,256]{1,0:T(8,128)(2,1)S(1)}, bf16[16,256]{1,0:T(8,128)(2,1)}, u32[]{:S(2)}) copy-start(bf16[16,256]{1,0:T(8,128)(2,1)} %filt_ref.1) | copy-start | bytes 24580
  6.7 4.3 %copy-start.4 = (s32[16]{0:T(128)S(1)}, s32[16]{0:T(128)}, u32[]{:S(2)}) copy-start(s32[16]{0:T(128)} %reach_ref.3) | copy-start | bytes 196
  6.7 2.2 %collective-permute-start = (bf16[128,2048]{1,0:T(8,128)(2,1)S(1)}, bf16[128,2048]{1,0:T(8,128)(2,1)S(1)}, u32[]{:S(2)}, u32[]{:S(2)}) collective-permute-start(bf16[128,2048]{1,0:T(8,128)(2,1)S(1)} %get-tuple-element.104.refs_0_.refs_1_), channel_id=1, source_target_pairs={{0,1},{1,0},{2,3},{3,2},{4,5},{5,4},{6,7},{7,6},{8,9},{9,8},{10,11... | collective-permute-start | bytes 1572872 | tf_op jit(solution)/shard_map/ppermute | solution.py:334
  7.4 2.3 %collective-permute-start.1 = (bf16[128,2048]{1,0:T(8,128)(2,1)S(1)}, bf16[128,2048]{1,0:T(8,128)(2,1)S(1)}, u32[]{:S(2)}, u32[]{:S(2)}) collective-permute-start(bf16[128,2048]{1,0:T(8,128)(2,1)S(1)} %get-tuple-element.133.refs_1_), channel_id=1, source_target_pairs={{0,1},{1,0},{2,3},{3,2},{4,5},{5,4},{6,7},{7,6},{8,9},{9,8},{10,11... | collective-permute-start | bytes 1572872 | tf_op jit(solution)/shard_map/ppermute | solution.py:334
  9.8 24.1 %collective-permute-start.7 = (bf16[128,4096]{1,0:T(8,128)(2,1)S(1)}, bf16[128,4096]{1,0:T(8,128)(2,1)S(1)}, u32[]{:S(2)}, u32[]{:S(2)}) collective-permute-start(bf16[128,4096]{1,0:T(8,128)(2,1)S(1)} %pad_maximum_fusion.got_x.refs_3_), channel_id=1, source_target_pairs={{0,63},{1,2},{2,1},{3,4},{4,3},{5,6},{6,5},{7,8},{8,7},{9,10},{10,... | collective-permute-start | bytes 3145736 | tf_op jit(solution)/shard_map/ppermute | solution.py:334
  17.8 19.1 %copy-start = (bf16[1,128,4096]{2,1,0:T(8,128)(2,1)S(1)}, bf16[1,128,4096]{2,1,0:T(8,128)(2,1)}, u32[]{:S(2)}) copy-start(bf16[1,128,4096]{2,1,0:T(8,128)(2,1)} %param.7) | copy-start | bytes 3145732
  17.8 19.1 %copy-start.1 = (bf16[1,128,4096]{2,1,0:T(8,128)(2,1)S(1)}, bf16[1,128,4096]{2,1,0:T(8,128)(2,1)}, u32[]{:S(2)}) copy-start(bf16[1,128,4096]{2,1,0:T(8,128)(2,1)} %param.8) | copy-start | bytes 3145732
  17.8 19.1 %copy-start.2 = (bf16[1,128,4096]{2,1,0:T(8,128)(2,1)S(1)}, bf16[1,128,4096]{2,1,0:T(8,128)(2,1)}, u32[]{:S(2)}) copy-start(bf16[1,128,4096]{2,1,0:T(8,128)(2,1)} %param.9) | copy-start | bytes 3145732
  18.7 15.1 %collective-permute-start.8 = (bf16[128,4096]{1,0:T(8,128)(2,1)S(1)}, bf16[128,4096]{1,0:T(8,128)(2,1)S(1)}, u32[]{:S(2)}, u32[]{:S(2)}) collective-permute-start(bf16[128,4096]{1,0:T(8,128)(2,1)S(1)} %collective-permute-done.2.got_p.refs_2_), channel_id=1, source_target_pairs={{0,1},{1,0},{2,3},{3,2},{4,5},{5,4},{6,7},{7,6},{8,9},{9,8},{10,11... | collective-permute-start | bytes 3145736 | tf_op jit(solution)/shard_map/ppermute | solution.py:334
  21.5 3.5 %collective-permute-start.3 = (f32[16,256]{1,0:T(8,128)S(1)}, f32[16,256]{1,0:T(8,128)S(1)}, u32[]{:S(2)}, u32[]{:S(2)}) collective-permute-start(f32[16,256]{1,0:T(8,128)S(1)} %shard_map.97), channel_id=1, source_target_pairs={{0,65},{1,64},{2,67},{3,66},{4,69},{5,68},{6,71},{7,70},{8,73},{9,... | collective-permute-start | bytes 49160 | tf_op jit(solution)/shard_map/ppermute | solution.py:358
  24.9 4.6 %collective-permute-start.4 = (f32[16,256]{1,0:T(8,128)S(1)}, f32[16,256]{1,0:T(8,128)S(1)}, u32[]{:S(2)}, u32[]{:S(2)}) collective-permute-start(f32[16,256]{1,0:T(8,128)S(1)} %add.24), channel_id=1, source_target_pairs={{0,193},{1,192},{2,195},{3,194},{4,197},{5,196},{6,199},{7,198},{8... | collective-permute-start | bytes 49160 | tf_op jit(solution)/shard_map/ppermute | solution.py:358
  29.5 1.2 %collective-permute-start.5 = (f32[16,256]{1,0:T(8,128)S(1)}, f32[16,256]{1,0:T(8,128)S(1)}, u32[]{:S(2)}, u32[]{:S(2)}) collective-permute-start(f32[16,256]{1,0:T(8,128)S(1)} %add.25), channel_id=1, source_target_pairs={{0,1},{1,0},{2,3},{3,2},{4,5},{5,4},{6,7},{7,6},{8,9},{9,8},{10,11... | collective-permute-start | bytes 49160 | tf_op jit(solution)/shard_map/ppermute | solution.py:352
  30.7 3.2 %collective-permute-start.6 = (f32[16,256]{1,0:T(8,128)S(1)}, f32[16,256]{1,0:T(8,128)S(1)}, u32[]{:S(2)}, u32[]{:S(2)}) collective-permute-start(f32[16,256]{1,0:T(8,128)S(1)} %add.26), channel_id=1, source_target_pairs={{0,9},{1,8},{2,11},{3,10},{4,13},{5,12},{6,15},{7,14},{8,1},{9,0},... | collective-permute-start | bytes 49160 | tf_op jit(solution)/shard_map/ppermute | solution.py:352
  33.9 4.6 %collective-permute-start.9 = (f32[16,256]{1,0:T(8,128)S(1)}, f32[16,256]{1,0:T(8,128)S(1)}, u32[]{:S(2)}, u32[]{:S(2)}) collective-permute-start(f32[16,256]{1,0:T(8,128)S(1)} %add.27), channel_id=1, source_target_pairs={{0,17},{1,16},{2,19},{3,18},{4,21},{5,20},{6,23},{7,22},{8,25},{9,... | collective-permute-start | bytes 49160 | tf_op jit(solution)/shard_map/ppermute | solution.py:352
  38.5 6.5 %collective-permute-start.10 = (f32[16,256]{1,0:T(8,128)S(1)}, f32[16,256]{1,0:T(8,128)S(1)}, u32[]{:S(2)}, u32[]{:S(2)}) collective-permute-start(f32[16,256]{1,0:T(8,128)S(1)} %add.28), channel_id=1, source_target_pairs={{0,57},{1,56},{2,59},{3,58},{4,61},{5,60},{6,63},{7,62},{8,49},{9,... | collective-permute-start | bytes 49160 | tf_op jit(solution)/shard_map/ppermute | solution.py:352
  45.0 3.3 %collective-permute-start.11 = (f32[16,256]{1,0:T(8,128)S(1)}, f32[16,256]{1,0:T(8,128)S(1)}, u32[]{:S(2)}, u32[]{:S(2)}) collective-permute-start(f32[16,256]{1,0:T(8,128)S(1)} %add.29), channel_id=1, source_target_pairs={{0,3},{1,2},{2,1},{3,0},{4,7},{5,6},{6,5},{7,4},{8,11},{9,10},{10,... | collective-permute-start | bytes 49160 | tf_op jit(solution)/shard_map/ppermute | solution.py:352
  48.2 4.4 %collective-permute-start.12 = (f32[16,256]{1,0:T(8,128)S(1)}, f32[16,256]{1,0:T(8,128)S(1)}, u32[]{:S(2)}, u32[]{:S(2)}) collective-permute-start(f32[16,256]{1,0:T(8,128)S(1)} %add.30), channel_id=1, source_target_pairs={{0,7},{1,6},{2,5},{3,4},{4,3},{5,2},{6,1},{7,0},{8,15},{9,14},{10,... | collective-permute-start | bytes 49160 | tf_op jit(solution)/shard_map/ppermute | solution.py:352

commit v5 on v4

--- a/solution.py
+++ b/solution.py
@@ -364,7 +364,7 @@
     outs = None
     fields = (mine_p, mine_x, got_p, got_x, got2_p, got2_x)
     pieces = 4
-    for at, mask in enumerate((16 | 1, 56 | 1, 2 | 1, 6 | 1)):
+    for at, mask in enumerate((16 | 1, 56 | 1, 2 | 1, 6)):
         total, fields = lax.optimization_barrier((total, fields))
         outs = grads_piece(
             me, ahead, back, fields, (grad, k, v), outs,

time: 53.4 us -> 52.9 us (level)
  no operation moved by 1% of the time
where the time goes in v5:
time: 52.9 us; the launch traced here: 52.6 us
  starting transfers between devices  20.3 us (38%)
  waiting for transfers between devices  17.6 us (33%)
  Pallas kernels  13.3 us (25%)
  between operations  0.73 us (1%)
  other arithmetic  0.71 us (1%)
    ppermute x6, starting transfers between devices, trade_ctx(): return x + lax.ppermute(x, 'ctx', [(i, i ^ mask) for i in range(ctx_n)])  10.8 us
    ppermute x5, starting transfers between devices, trade(): return [lax.ppermute(x, ('dp', 'ctx'), route) for x in chunks]  7.47 us
    ppermute x2, waiting for transfers between devices, trade_dp(): return x + lax.ppermute(x, ('dp', 'ctx'), route)  6.05 us
    pallas_call x4, Pallas kernels, grads_piece(): pl.pallas_call(kernel, out_shape=[shape] * 3, grid=(count // step,), in_s...  5.84 us
    ppermute x6, waiting for transfers between devices, trade_ctx(): return x + lax.ppermute(x, 'ctx', [(i, i ^ mask) for i in range(ctx_n)])  5.81 us
    ppermute x5, waiting for transfers between devices, trade(): return [lax.ppermute(x, ('dp', 'ctx'), route) for x in chunks]  5.74 us
    pallas_call x2, Pallas kernels, gate_product(): pl.pallas_call(kernel, out_shape=[jax.ShapeDtypeStruct((tok_n, width), BF...  3.27 us
    ppermute x2, starting transfers between devices, trade_dp(): return x + lax.ppermute(x, ('dp', 'ctx'), route)  1.99 us
  transfers between devices with their start and end apart: 13, of which 9 were waited for; matrix products, arithmetic and copies ran while one was open for 0% of the time, Pallas kernels for 22%

profile of v5, /device:TPU:1, one launch (start us, length us, event | category | flops | bytes accessed | tf_op | source)
XLA Modules:
  0.0 52.6 jit_solution(13970795399375609010)
XLA Ops:
  0.6 1.6 %shard_map.93.mine_p.refs_0_ = bf16[128,4096]{1,0:T(8,128)(2,1)S(1)} custom-call(s32[1]{0:T(128)} %bitcast.me_ref, bf16[128,4096]{1,0:T(8,128)(2,1)} %bitcast.8, bf16[128,4096]{1,0:T(8,128)(2,1)} %bitcast.14, bf16[128,4096]{1,0:T(8,128)(2,1)} %bitcast.20, bf16[128,4096]{1,0:T(8,128)(2,1)} %bitcast.29), custom_call_target="tpu_custom_call" | custom-call | flops 1 | bytes 3145728 | tf_op jit(solution)/shard_map/pallas_call | solution.py:68
  2.3 2.8 %collective-permute-start.2 = (bf16[128,4096]{1,0:T(8,128)(2,1)S(1)}, bf16[128,4096]{1,0:T(8,128)(2,1)S(1)}, u32[]{:S(2)}, u32[]{:S(2)}) collective-permute-start(bf16[128,4096]{1,0:T(8,128)(2,1)S(1)} %shard_map.93.mine_p.refs_0_), channel_id=1, source_target_pairs={{0,64},{1,2},{2,1},{3,4},{4,3},{5,6},{6,5},{7,8},{8,7},{9,10},{10,... | collective-permute-start | bytes 3145736 | tf_op jit(solution)/shard_map/ppermute | solution.py:334
  5.1 1.6 %shard_map.94 = (bf16[128,2048]{1,0:T(8,128)(2,1)S(1)}, bf16[128,2048]{1,0:T(8,128)(2,1)S(1)}) custom-call(s32[1]{0:T(128)} %bitcast.me_ref, bf16[128,4096]{1,0:T(8,128)(2,1)} %bitcast.21, bf16[128,4096]{1,0:T(8,128)(2,1)} %bitcast.30, bf16[128,4096]{1,0:T(8,128)(2,1)} %bitcast.9, bf16[128,4096]{1,0:T(8,128)(2,1)} %bitcast.15), custom_call_target="tpu_custom_call" | custom-call | flops 1000000000 | bytes 3145728 | tf_op jit(solution)/shard_map/pallas_call | solution.py:68
  6.7 0.0 copy-start.3
  6.7 0.0 copy-start.4
  6.7 0.7 %collective-permute-start = (bf16[128,2048]{1,0:T(8,128)(2,1)S(1)}, bf16[128,2048]{1,0:T(8,128)(2,1)S(1)}, u32[]{:S(2)}, u32[]{:S(2)}) collective-permute-start(bf16[128,2048]{1,0:T(8,128)(2,1)S(1)} %get-tuple-element.104.refs_0_.refs_1_), channel_id=1, source_target_pairs={{0,1},{1,0},{2,3},{3,2},{4,5},{5,4},{6,7},{7,6},{8,9},{9,8},{10,11... | collective-permute-start | bytes 1572872 | tf_op jit(solution)/shard_map/ppermute | solution.py:334
  7.4 0.1 collective-permute-start.1
  7.5 1.4 %collective-permute-done = bf16[128,2048]{1,0:T(8,128)(2,1)S(1)} collective-permute-done((bf16[128,2048]{1,0:T(8,128)(2,1)S(1)}, bf16[128,2048]{1,0:T(8,128)(2,1)S(1)}, u32[]{:S(2)}, u32[]{:S(2)}) %collective-permute-start) | collective-permute-done | bytes 524320 | tf_op jit(solution)/shard_map/ppermute | solution.py:334
  8.9 0.7 %collective-permute-done.1 = bf16[128,2048]{1,0:T(8,128)(2,1)S(1)} collective-permute-done((bf16[128,2048]{1,0:T(8,128)(2,1)S(1)}, bf16[128,2048]{1,0:T(8,128)(2,1)S(1)}, u32[]{:S(2)}, u32[]{:S(2)}) %collective-permute-start.1) | collective-permute-done | bytes 524320 | tf_op jit(solution)/shard_map/ppermute | solution.py:334
  9.7 0.1 pad_maximum_fusion.got_x.refs_3_
  9.8 1.2 %collective-permute-start.7 = (bf16[128,4096]{1,0:T(8,128)(2,1)S(1)}, bf16[128,4096]{1,0:T(8,128)(2,1)S(1)}, u32[]{:S(2)}, u32[]{:S(2)}) collective-permute-start(bf16[128,4096]{1,0:T(8,128)(2,1)S(1)} %pad_maximum_fusion.got_x.refs_3_), channel_id=1, source_target_pairs={{0,63},{1,2},{2,1},{3,4},{4,3},{5,6},{6,5},{7,8},{8,7},{9,10},{10,... | collective-permute-start | bytes 3145736 | tf_op jit(solution)/shard_map/ppermute | solution.py:334
  11.0 0.0 copy-done.3
  11.0 0.0 copy-done.4
  11.0 1.7 %shard_map.95 = (bf16[16,128,384]{2,1,0:T(8,128)(2,1)S(1)}, bf16[16,128,384]{2,1,0:T(8,128)(2,1)S(1)}) custom-call(s32[1]{0:T(128)} %bitcast.me_ref, s32[16]{0:T(128)S(1)} %copy-done.4, bf16[16,256]{1,0:T(8,128)(2,1)S(1)} %copy-done.3), custom_call_target="tpu_custom_call" | custom-call | flops 2048 | bytes 2048 | tf_op jit(solution)/shard_map/pallas_call | solution.py:123
  12.7 1.6 %shard_map.96 = (f32[16,256]{1,0:T(8,128)S(1)}, f32[16,256]{1,0:T(8,128)S(1)}) custom-call(s32[1]{0:T(128)} %bitcast.me_ref, s32[16]{0:T(128)S(1)} %copy-done.4, bf16[128,4096]{1,0:T(8,128)(2,1)S(1)} %shard_map.93.mine_p.refs_0_, bf16[128,4096]{1,0:T(8,128)(2,1)S(1)} %pad_maximum_fusion.got_x.refs_3_, ...), custom_call_target="tpu_custom_call" | custom-call | flops 2048 | bytes 2048 | tf_op jit(solution)/shard_map/pallas_call | solution.py:182
  14.3 3.5 %collective-permute-done.2.got_p.refs_2_ = bf16[128,4096]{1,0:T(8,128)(2,1)S(1)} collective-permute-done((bf16[128,4096]{1,0:T(8,128)(2,1)S(1)}, bf16[128,4096]{1,0:T(8,128)(2,1)S(1)}, u32[]{:S(2)}, u32[]{:S(2)}) %collective-permute-start.2) | collective-permute-done | bytes 1048608 | tf_op jit(solution)/shard_map/ppermute | solution.py:334
  17.8 0.0 copy-start
  17.8 0.0 copy-start.1
  17.8 0.0 copy-start.2
  17.8 0.9 %shard_map.97 = f32[16,256]{1,0:T(8,128)S(1)} custom-call(s32[1]{0:T(128)} %bitcast.me_ref, f32[16,256]{1,0:T(8,128)S(1)} %get-tuple-element.84.in_ref, f32[16,256]{1,0:T(8,128)S(1)} %get-tuple-element.85.weight_ref, bf16[128,4096]{1,0:T(8,128)(2,1)S(1)} %shard_map.93.mine_p.refs_0_, bf16[128,4096]{1,0:T(8,128)(2,1)S(1)} %collective-permute-done.2.got_p.refs_2_, ...), custom_call_target="tpu_custom_call" | custom-call | flops 2048 | bytes 2048 | tf_op jit(solution)/shard_map/pallas_call | solution.py:237
  18.7 2.7 %collective-permute-start.8 = (bf16[128,4096]{1,0:T(8,128)(2,1)S(1)}, bf16[128,4096]{1,0:T(8,128)(2,1)S(1)}, u32[]{:S(2)}, u32[]{:S(2)}) collective-permute-start(bf16[128,4096]{1,0:T(8,128)(2,1)S(1)} %collective-permute-done.2.got_p.refs_2_), channel_id=1, source_target_pairs={{0,1},{1,0},{2,3},{3,2},{4,5},{5,4},{6,7},{7,6},{8,9},{9,8},{10,11... | collective-permute-start | bytes 3145736 | tf_op jit(solution)/shard_map/ppermute | solution.py:334
  21.5 0.5 collective-permute-start.3
  22.0 3.0 %collective-permute-done.3 = f32[16,256]{1,0:T(8,128)S(1)} collective-permute-done((f32[16,256]{1,0:T(8,128)S(1)}, f32[16,256]{1,0:T(8,128)S(1)}, u32[]{:S(2)}, u32[]{:S(2)}) %collective-permute-start.3) | collective-permute-done | bytes 16416 | tf_op jit(solution)/shard_map/ppermute | solution.py:358
  24.9 1.5 %collective-permute-start.4 = (f32[16,256]{1,0:T(8,128)S(1)}, f32[16,256]{1,0:T(8,128)S(1)}, u32[]{:S(2)}, u32[]{:S(2)}) collective-permute-start(f32[16,256]{1,0:T(8,128)S(1)} %add.24), channel_id=1, source_target_pairs={{0,193},{1,192},{2,195},{3,194},{4,197},{5,196},{6,199},{7,198},{8... | collective-permute-start | bytes 49160 | tf_op jit(solution)/shard_map/ppermute | solution.py:358
  26.4 3.1 %collective-permute-done.4 = f32[16,256]{1,0:T(8,128)S(1)} collective-permute-done((f32[16,256]{1,0:T(8,128)S(1)}, f32[16,256]{1,0:T(8,128)S(1)}, u32[]{:S(2)}, u32[]{:S(2)}) %collective-permute-start.4) | collective-permute-done | bytes 16416 | tf_op jit(solution)/shard_map/ppermute | solution.py:358
  29.5 0.0 collective-permute-start.5
  29.5 1.2 %collective-permute-done.5 = f32[16,256]{1,0:T(8,128)S(1)} collective-permute-done((f32[16,256]{1,0:T(8,128)S(1)}, f32[16,256]{1,0:T(8,128)S(1)}, u32[]{:S(2)}, u32[]{:S(2)}) %collective-permute-start.5) | collective-permute-done | bytes 16416 | tf_op jit(solution)/shard_map/ppermute | solution.py:352
  30.7 1.5 %collective-permute-start.6 = (f32[16,256]{1,0:T(8,128)S(1)}, f32[16,256]{1,0:T(8,128)S(1)}, u32[]{:S(2)}, u32[]{:S(2)}) collective-permute-start(f32[16,256]{1,0:T(8,128)S(1)} %add.26), channel_id=1, source_target_pairs={{0,9},{1,8},{2,11},{3,10},{4,13},{5,12},{6,15},{7,14},{8,1},{9,0},... | collective-permute-start | bytes 49160 | tf_op jit(solution)/shard_map/ppermute | solution.py:352
  32.2 1.6 %collective-permute-done.6 = f32[16,256]{1,0:T(8,128)S(1)} collective-permute-done((f32[16,256]{1,0:T(8,128)S(1)}, f32[16,256]{1,0:T(8,128)S(1)}, u32[]{:S(2)}, u32[]{:S(2)}) %collective-permute-start.6) | collective-permute-done | bytes 16416 | tf_op jit(solution)/shard_map/ppermute | solution.py:352
  33.9 0.0 collective-permute-done.7.refs_4_
  33.9 0.0 collective-permute-done.8.refs_5_
  33.9 3.1 %collective-permute-start.9 = (f32[16,256]{1,0:T(8,128)S(1)}, f32[16,256]{1,0:T(8,128)S(1)}, u32[]{:S(2)}, u32[]{:S(2)}) collective-permute-start(f32[16,256]{1,0:T(8,128)S(1)} %add.27), channel_id=1, source_target_pairs={{0,17},{1,16},{2,19},{3,18},{4,21},{5,20},{6,23},{7,22},{8,25},{9,... | collective-permute-start | bytes 49160 | tf_op jit(solution)/shard_map/ppermute | solution.py:352
  37.0 0.0 copy-done
  37.0 0.0 copy-done.1
  37.0 0.0 copy-done.2
  37.0 1.5 %shard_map.98 = (bf16[128,4096]{1,0:T(8,128)(2,1)}, bf16[128,4096]{1,0:T(8,128)(2,1)}, bf16[128,4096]{1,0:T(8,128)(2,1)}) custom-call(s32[1]{0:T(128)} %bitcast.me_ref, bf16[16,128,384]{2,1,0:T(8,128)(2,1)S(1)} %get-tuple-element.89.ahead_ref, bf16[16,128,384]{2,1,0:T(8,128)(2,1)S(1)} %get-tuple-element.90.back_ref, ...), custom_call_target="tpu_custom_call" | custom-call | flops 201326592 | bytes 3538944 | tf_op jit(solution)/shard_map/pallas_call | solution.py:294
  38.5 0.0 collective-permute-done.9
  38.5 5.0 %collective-permute-start.10 = (f32[16,256]{1,0:T(8,128)S(1)}, f32[16,256]{1,0:T(8,128)S(1)}, u32[]{:S(2)}, u32[]{:S(2)}) collective-permute-start(f32[16,256]{1,0:T(8,128)S(1)} %add.28), channel_id=1, source_target_pairs={{0,57},{1,56},{2,59},{3,58},{4,61},{5,60},{6,63},{7,62},{8,49},{9,... | collective-permute-start | bytes 49160 | tf_op jit(solution)/shard_map/ppermute | solution.py:352
  43.5 1.4 %shard_map.99 = (bf16[128,4096]{1,0:T(8,128)(2,1)}, bf16[128,4096]{1,0:T(8,128)(2,1)}, bf16[128,4096]{1,0:T(8,128)(2,1)}) custom-call(s32[1]{0:T(128)} %bitcast.me_ref, bf16[16,128,384]{2,1,0:T(8,128)(2,1)S(1)} %get-tuple-element.89.ahead_ref, ...), custom_call_target="tpu_custom_call", output_to_operand_aliasing={{0}: (12, {}), {1}: (13, {}), {2}: (14, {})} | custom-call | flops 201326592 | bytes 3538944 | tf_op jit(solution)/shard_map/pallas_call | solution.py:294
  44.9 0.0 collective-permute-done.10
  45.0 0.1 collective-permute-start.11
  45.0 1.5 %shard_map.100 = (bf16[128,4096]{1,0:T(8,128)(2,1)}, bf16[128,4096]{1,0:T(8,128)(2,1)}, bf16[128,4096]{1,0:T(8,128)(2,1)}) custom-call(s32[1]{0:T(128)} %bitcast.me_ref, bf16[16,128,384]{2,1,0:T(8,128)(2,1)S(1)} %get-tuple-element.89.ahead_ref, ...), custom_call_target="tpu_custom_call", output_to_operand_aliasing={{0}: (12, {}), {1}: (13, {}), {2}: (14, {})} | custom-call | flops 201326592 | bytes 3538944 | tf_op jit(solution)/shard_map/pallas_call | solution.py:294
  46.5 1.7 %collective-permute-done.11 = f32[16,256]{1,0:T(8,128)S(1)} collective-permute-done((f32[16,256]{1,0:T(8,128)S(1)}, f32[16,256]{1,0:T(8,128)S(1)}, u32[]{:S(2)}, u32[]{:S(2)}) %collective-permute-start.11) | collective-permute-done | bytes 16416 | tf_op jit(solution)/shard_map/ppermute | solution.py:352
  48.2 1.1 %collective-permute-start.12 = (f32[16,256]{1,0:T(8,128)S(1)}, f32[16,256]{1,0:T(8,128)S(1)}, u32[]{:S(2)}, u32[]{:S(2)}) collective-permute-start(f32[16,256]{1,0:T(8,128)S(1)} %add.30), channel_id=1, source_target_pairs={{0,6},{1,7},{2,4},{3,5},{4,2},{5,3},{6,0},{7,1},{8,14},{9,15},{10,... | collective-permute-start | bytes 49160 | tf_op jit(solution)/shard_map/ppermute | solution.py:352
  49.4 1.4 %shard_map.101 = (bf16[128,4096]{1,0:T(8,128)(2,1)}, bf16[128,4096]{1,0:T(8,128)(2,1)}, bf16[128,4096]{1,0:T(8,128)(2,1)}) custom-call(s32[1]{0:T(128)} %bitcast.me_ref, bf16[16,128,384]{2,1,0:T(8,128)(2,1)S(1)} %get-tuple-element.89.ahead_ref, ...), custom_call_target="tpu_custom_call", output_to_operand_aliasing={{0}: (12, {}), {1}: (13, {}), {2}: (14, {})} | custom-call | flops 201326592 | bytes 3538944 | tf_op jit(solution)/shard_map/pallas_call | solution.py:294
  50.8 1.2 %collective-permute-done.12 = f32[16,256]{1,0:T(8,128)S(1)} collective-permute-done((f32[16,256]{1,0:T(8,128)S(1)}, f32[16,256]{1,0:T(8,128)S(1)}, u32[]{:S(2)}, u32[]{:S(2)}) %collective-permute-start.12) | collective-permute-done | bytes 16416 | tf_op jit(solution)/shard_map/ppermute | solution.py:352
  52.0 0.6 %add.31 = f32[16,256]{1,0:T(8,128)} add(f32[16,256]{1,0:T(8,128)S(1)} %add.30, f32[16,256]{1,0:T(8,128)S(1)} %collective-permute-done.12) | non-fusion elementwise | flops 4096 | bytes 49152 | tf_op jit(solution)/shard_map/add | solution.py:352
  (7 shorter events, 0.0 us)
Async XLA Ops:
  2.3 15.6 %collective-permute-start.2 = (bf16[128,4096]{1,0:T(8,128)(2,1)S(1)}, bf16[128,4096]{1,0:T(8,128)(2,1)S(1)}, u32[]{:S(2)}, u32[]{:S(2)}) collective-permute-start(bf16[128,4096]{1,0:T(8,128)(2,1)S(1)} %shard_map.93.mine_p.refs_0_), channel_id=1, source_target_pairs={{0,64},{1,2},{2,1},{3,4},{4,3},{5,6},{6,5},{7,8},{8,7},{9,10},{10,... | collective-permute-start | bytes 3145736 | tf_op jit(solution)/shard_map/ppermute | solution.py:334
  6.7 4.3 %copy-start.3 = (bf16[16,256]{1,0:T(8,128)(2,1)S(1)}, bf16[16,256]{1,0:T(8,128)(2,1)}, u32[]{:S(2)}) copy-start(bf16[16,256]{1,0:T(8,128)(2,1)} %filt_ref.1) | copy-start | bytes 24580
  6.7 4.3 %copy-start.4 = (s32[16]{0:T(128)S(1)}, s32[16]{0:T(128)}, u32[]{:S(2)}) copy-start(s32[16]{0:T(128)} %reach_ref.3) | copy-start | bytes 196
  6.7 2.2 %collective-permute-start = (bf16[128,2048]{1,0:T(8,128)(2,1)S(1)}, bf16[128,2048]{1,0:T(8,128)(2,1)S(1)}, u32[]{:S(2)}, u32[]{:S(2)}) collective-permute-start(bf16[128,2048]{1,0:T(8,128)(2,1)S(1)} %get-tuple-element.104.refs_0_.refs_1_), channel_id=1, source_target_pairs={{0,1},{1,0},{2,3},{3,2},{4,5},{5,4},{6,7},{7,6},{8,9},{9,8},{10,11... | collective-permute-start | bytes 1572872 | tf_op jit(solution)/shard_map/ppermute | solution.py:334
  7.4 2.3 %collective-permute-start.1 = (bf16[128,2048]{1,0:T(8,128)(2,1)S(1)}, bf16[128,2048]{1,0:T(8,128)(2,1)S(1)}, u32[]{:S(2)}, u32[]{:S(2)}) collective-permute-start(bf16[128,2048]{1,0:T(8,128)(2,1)S(1)} %get-tuple-element.133.refs_1_), channel_id=1, source_target_pairs={{0,1},{1,0},{2,3},{3,2},{4,5},{5,4},{6,7},{7,6},{8,9},{9,8},{10,11... | collective-permute-start | bytes 1572872 | tf_op jit(solution)/shard_map/ppermute | solution.py:334
  9.8 24.1 %collective-permute-start.7 = (bf16[128,4096]{1,0:T(8,128)(2,1)S(1)}, bf16[128,4096]{1,0:T(8,128)(2,1)S(1)}, u32[]{:S(2)}, u32[]{:S(2)}) collective-permute-start(bf16[128,4096]{1,0:T(8,128)(2,1)S(1)} %pad_maximum_fusion.got_x.refs_3_), channel_id=1, source_target_pairs={{0,63},{1,2},{2,1},{3,4},{4,3},{5,6},{6,5},{7,8},{8,7},{9,10},{10,... | collective-permute-start | bytes 3145736 | tf_op jit(solution)/shard_map/ppermute | solution.py:334
  17.8 19.1 %copy-start = (bf16[1,128,4096]{2,1,0:T(8,128)(2,1)S(1)}, bf16[1,128,4096]{2,1,0:T(8,128)(2,1)}, u32[]{:S(2)}) copy-start(bf16[1,128,4096]{2,1,0:T(8,128)(2,1)} %param.7) | copy-start | bytes 3145732
  17.8 19.1 %copy-start.1 = (bf16[1,128,4096]{2,1,0:T(8,128)(2,1)S(1)}, bf16[1,128,4096]{2,1,0:T(8,128)(2,1)}, u32[]{:S(2)}) copy-start(bf16[1,128,4096]{2,1,0:T(8,128)(2,1)} %param.8) | copy-start | bytes 3145732
  17.8 19.1 %copy-start.2 = (bf16[1,128,4096]{2,1,0:T(8,128)(2,1)S(1)}, bf16[1,128,4096]{2,1,0:T(8,128)(2,1)}, u32[]{:S(2)}) copy-start(bf16[1,128,4096]{2,1,0:T(8,128)(2,1)} %param.9) | copy-start | bytes 3145732
  18.7 15.1 %collective-permute-start.8 = (bf16[128,4096]{1,0:T(8,128)(2,1)S(1)}, bf16[128,4096]{1,0:T(8,128)(2,1)S(1)}, u32[]{:S(2)}, u32[]{:S(2)}) collective-permute-start(bf16[128,4096]{1,0:T(8,128)(2,1)S(1)} %collective-permute-done.2.got_p.refs_2_), channel_id=1, source_target_pairs={{0,1},{1,0},{2,3},{3,2},{4,5},{5,4},{6,7},{7,6},{8,9},{9,8},{10,11... | collective-permute-start | bytes 3145736 | tf_op jit(solution)/shard_map/ppermute | solution.py:334
  21.5 3.5 %collective-permute-start.3 = (f32[16,256]{1,0:T(8,128)S(1)}, f32[16,256]{1,0:T(8,128)S(1)}, u32[]{:S(2)}, u32[]{:S(2)}) collective-permute-start(f32[16,256]{1,0:T(8,128)S(1)} %shard_map.97), channel_id=1, source_target_pairs={{0,65},{1,64},{2,67},{3,66},{4,69},{5,68},{6,71},{7,70},{8,73},{9,... | collective-permute-start | bytes 49160 | tf_op jit(solution)/shard_map/ppermute | solution.py:358
  24.9 4.6 %collective-permute-start.4 = (f32[16,256]{1,0:T(8,128)S(1)}, f32[16,256]{1,0:T(8,128)S(1)}, u32[]{:S(2)}, u32[]{:S(2)}) collective-permute-start(f32[16,256]{1,0:T(8,128)S(1)} %add.24), channel_id=1, source_target_pairs={{0,193},{1,192},{2,195},{3,194},{4,197},{5,196},{6,199},{7,198},{8... | collective-permute-start | bytes 49160 | tf_op jit(solution)/shard_map/ppermute | solution.py:358
  29.5 1.2 %collective-permute-start.5 = (f32[16,256]{1,0:T(8,128)S(1)}, f32[16,256]{1,0:T(8,128)S(1)}, u32[]{:S(2)}, u32[]{:S(2)}) collective-permute-start(f32[16,256]{1,0:T(8,128)S(1)} %add.25), channel_id=1, source_target_pairs={{0,1},{1,0},{2,3},{3,2},{4,5},{5,4},{6,7},{7,6},{8,9},{9,8},{10,11... | collective-permute-start | bytes 49160 | tf_op jit(solution)/shard_map/ppermute | solution.py:352
  30.7 3.2 %collective-permute-start.6 = (f32[16,256]{1,0:T(8,128)S(1)}, f32[16,256]{1,0:T(8,128)S(1)}, u32[]{:S(2)}, u32[]{:S(2)}) collective-permute-start(f32[16,256]{1,0:T(8,128)S(1)} %add.26), channel_id=1, source_target_pairs={{0,9},{1,8},{2,11},{3,10},{4,13},{5,12},{6,15},{7,14},{8,1},{9,0},... | collective-permute-start | bytes 49160 | tf_op jit(solution)/shard_map/ppermute | solution.py:352
  33.9 4.6 %collective-permute-start.9 = (f32[16,256]{1,0:T(8,128)S(1)}, f32[16,256]{1,0:T(8,128)S(1)}, u32[]{:S(2)}, u32[]{:S(2)}) collective-permute-start(f32[16,256]{1,0:T(8,128)S(1)} %add.27), channel_id=1, source_target_pairs={{0,17},{1,16},{2,19},{3,18},{4,21},{5,20},{6,23},{7,22},{8,25},{9,... | collective-permute-start | bytes 49160 | tf_op jit(solution)/shard_map/ppermute | solution.py:352
  38.5 6.5 %collective-permute-start.10 = (f32[16,256]{1,0:T(8,128)S(1)}, f32[16,256]{1,0:T(8,128)S(1)}, u32[]{:S(2)}, u32[]{:S(2)}) collective-permute-start(f32[16,256]{1,0:T(8,128)S(1)} %add.28), channel_id=1, source_target_pairs={{0,57},{1,56},{2,59},{3,58},{4,61},{5,60},{6,63},{7,62},{8,49},{9,... | collective-permute-start | bytes 49160 | tf_op jit(solution)/shard_map/ppermute | solution.py:352
  45.0 3.3 %collective-permute-start.11 = (f32[16,256]{1,0:T(8,128)S(1)}, f32[16,256]{1,0:T(8,128)S(1)}, u32[]{:S(2)}, u32[]{:S(2)}) collective-permute-start(f32[16,256]{1,0:T(8,128)S(1)} %add.29), channel_id=1, source_target_pairs={{0,3},{1,2},{2,1},{3,0},{4,7},{5,6},{6,5},{7,4},{8,11},{9,10},{10,... | collective-permute-start | bytes 49160 | tf_op jit(solution)/shard_map/ppermute | solution.py:352
  48.2 3.8 %collective-permute-start.12 = (f32[16,256]{1,0:T(8,128)S(1)}, f32[16,256]{1,0:T(8,128)S(1)}, u32[]{:S(2)}, u32[]{:S(2)}) collective-permute-start(f32[16,256]{1,0:T(8,128)S(1)} %add.30), channel_id=1, source_target_pairs={{0,6},{1,7},{2,4},{3,5},{4,2},{5,3},{6,0},{7,1},{8,14},{9,15},{10,... | collective-permute-start | bytes 49160 | tf_op jit(solution)/shard_map/ppermute | solution.py:352

commit v6 on v5

--- a/solution.py
+++ b/solution.py
@@ -357,14 +357,14 @@
         ]
         return x + lax.ppermute(x, ("dp", "ctx"), route)
 
-    total = trade_dp(local, 1)
-    total = trade_dp(total, 3)
+    total = trade_dp(local, 3)
+    total = trade_dp(total, 1)
     total = trade_ctx(total, 1)
     total = trade_ctx(total, 8 | 1)
     outs = None
     fields = (mine_p, mine_x, got_p, got_x, got2_p, got2_x)
     pieces = 4
-    for at, mask in enumerate((16 | 1, 56 | 1, 2 | 1, 6)):
+    for at, mask in enumerate((16 | 1, 56 | 1, 6, 2 | 1)):
         total, fields = lax.optimization_barrier((total, fields))
         outs = grads_piece(
             me, ahead, back, fields, (grad, k, v), outs,

time: 52.9 us -> 52.9 us (level)
  no operation moved by 1% of the time
where the time goes in v6:
time: 52.9 us; the launch traced here: 52.6 us
  starting transfers between devices  20.1 us (38%)
  waiting for transfers between devices  17.8 us (34%)
  Pallas kernels  13.3 us (25%)
  between operations  0.73 us (1%)
  other arithmetic  0.71 us (1%)
    ppermute x6, starting transfers between devices, trade_ctx(): return x + lax.ppermute(x, 'ctx', [(i, i ^ mask) for i in range(ctx_n)])  10.8 us
    ppermute x5, starting transfers between devices, trade(): return [lax.ppermute(x, ('dp', 'ctx'), route) for x in chunks]  7.47 us
    ppermute x2, waiting for transfers between devices, trade_dp(): return x + lax.ppermute(x, ('dp', 'ctx'), route)  6.24 us
    pallas_call x4, Pallas kernels, grads_piece(): pl.pallas_call(kernel, out_shape=[shape] * 3, grid=(count // step,), in_s...  5.85 us
    ppermute x6, waiting for transfers between devices, trade_ctx(): return x + lax.ppermute(x, 'ctx', [(i, i ^ mask) for i in range(ctx_n)])  5.79 us
    ppermute x5, waiting for transfers between devices, trade(): return [lax.ppermute(x, ('dp', 'ctx'), route) for x in chunks]  5.74 us
    pallas_call x2, Pallas kernels, gate_product(): pl.pallas_call(kernel, out_shape=[jax.ShapeDtypeStruct((tok_n, width), BF...  3.27 us
    ppermute x2, starting transfers between devices, trade_dp(): return x + lax.ppermute(x, ('dp', 'ctx'), route)  1.8 us
  transfers between devices with their start and end apart: 13, of which 9 were waited for; matrix products, arithmetic and copies ran while one was open for 0% of the time, Pallas kernels for 22%

profile of v6, /device:TPU:1, one launch (start us, length us, event | category | flops | bytes accessed | tf_op | source)
XLA Modules:
  0.0 52.6 jit_solution(9604682051109908574)
XLA Ops:
  0.6 1.6 %shard_map.93.mine_p.refs_0_ = bf16[128,4096]{1,0:T(8,128)(2,1)S(1)} custom-call(s32[1]{0:T(128)} %bitcast.me_ref, bf16[128,4096]{1,0:T(8,128)(2,1)} %bitcast.8, bf16[128,4096]{1,0:T(8,128)(2,1)} %bitcast.14, bf16[128,4096]{1,0:T(8,128)(2,1)} %bitcast.20, bf16[128,4096]{1,0:T(8,128)(2,1)} %bitcast.29), custom_call_target="tpu_custom_call" | custom-call | flops 1 | bytes 3145728 | tf_op jit(solution)/shard_map/pallas_call | solution.py:68
  2.3 2.8 %collective-permute-start.2 = (bf16[128,4096]{1,0:T(8,128)(2,1)S(1)}, bf16[128,4096]{1,0:T(8,128)(2,1)S(1)}, u32[]{:S(2)}, u32[]{:S(2)}) collective-permute-start(bf16[128,4096]{1,0:T(8,128)(2,1)S(1)} %shard_map.93.mine_p.refs_0_), channel_id=1, source_target_pairs={{0,64},{1,2},{2,1},{3,4},{4,3},{5,6},{6,5},{7,8},{8,7},{9,10},{10,... | collective-permute-start | bytes 3145736 | tf_op jit(solution)/shard_map/ppermute | solution.py:334
  5.1 1.6 %shard_map.94 = (bf16[128,2048]{1,0:T(8,128)(2,1)S(1)}, bf16[128,2048]{1,0:T(8,128)(2,1)S(1)}) custom-call(s32[1]{0:T(128)} %bitcast.me_ref, bf16[128,4096]{1,0:T(8,128)(2,1)} %bitcast.21, bf16[128,4096]{1,0:T(8,128)(2,1)} %bitcast.30, bf16[128,4096]{1,0:T(8,128)(2,1)} %bitcast.9, bf16[128,4096]{1,0:T(8,128)(2,1)} %bitcast.15), custom_call_target="tpu_custom_call" | custom-call | flops 1000000000 | bytes 3145728 | tf_op jit(solution)/shard_map/pallas_call | solution.py:68
  6.7 0.0 copy-start.3
  6.7 0.0 copy-start.4
  6.7 0.7 %collective-permute-start = (bf16[128,2048]{1,0:T(8,128)(2,1)S(1)}, bf16[128,2048]{1,0:T(8,128)(2,1)S(1)}, u32[]{:S(2)}, u32[]{:S(2)}) collective-permute-start(bf16[128,2048]{1,0:T(8,128)(2,1)S(1)} %get-tuple-element.104.refs_0_.refs_1_), channel_id=1, source_target_pairs={{0,1},{1,0},{2,3},{3,2},{4,5},{5,4},{6,7},{7,6},{8,9},{9,8},{10,11... | collective-permute-start | bytes 1572872 | tf_op jit(solution)/shard_map/ppermute | solution.py:334
  7.4 0.1 collective-permute-start.1
  7.5 1.4 %collective-permute-done = bf16[128,2048]{1,0:T(8,128)(2,1)S(1)} collective-permute-done((bf16[128,2048]{1,0:T(8,128)(2,1)S(1)}, bf16[128,2048]{1,0:T(8,128)(2,1)S(1)}, u32[]{:S(2)}, u32[]{:S(2)}) %collective-permute-start) | collective-permute-done | bytes 524320 | tf_op jit(solution)/shard_map/ppermute | solution.py:334
  8.9 0.7 %collective-permute-done.1 = bf16[128,2048]{1,0:T(8,128)(2,1)S(1)} collective-permute-done((bf16[128,2048]{1,0:T(8,128)(2,1)S(1)}, bf16[128,2048]{1,0:T(8,128)(2,1)S(1)}, u32[]{:S(2)}, u32[]{:S(2)}) %collective-permute-start.1) | collective-permute-done | bytes 524320 | tf_op jit(solution)/shard_map/ppermute | solution.py:334
  9.7 0.1 pad_maximum_fusion.got_x.refs_3_
  9.8 1.2 %collective-permute-start.7 = (bf16[128,4096]{1,0:T(8,128)(2,1)S(1)}, bf16[128,4096]{1,0:T(8,128)(2,1)S(1)}, u32[]{:S(2)}, u32[]{:S(2)}) collective-permute-start(bf16[128,4096]{1,0:T(8,128)(2,1)S(1)} %pad_maximum_fusion.got_x.refs_3_), channel_id=1, source_target_pairs={{0,63},{1,2},{2,1},{3,4},{4,3},{5,6},{6,5},{7,8},{8,7},{9,10},{10,... | collective-permute-start | bytes 3145736 | tf_op jit(solution)/shard_map/ppermute | solution.py:334
  11.0 0.0 copy-done.3
  11.0 0.0 copy-done.4
  11.0 1.7 %shard_map.95 = (bf16[16,128,384]{2,1,0:T(8,128)(2,1)S(1)}, bf16[16,128,384]{2,1,0:T(8,128)(2,1)S(1)}) custom-call(s32[1]{0:T(128)} %bitcast.me_ref, s32[16]{0:T(128)S(1)} %copy-done.4, bf16[16,256]{1,0:T(8,128)(2,1)S(1)} %copy-done.3), custom_call_target="tpu_custom_call" | custom-call | flops 2048 | bytes 2048 | tf_op jit(solution)/shard_map/pallas_call | solution.py:123
  12.7 1.6 %shard_map.96 = (f32[16,256]{1,0:T(8,128)S(1)}, f32[16,256]{1,0:T(8,128)S(1)}) custom-call(s32[1]{0:T(128)} %bitcast.me_ref, s32[16]{0:T(128)S(1)} %copy-done.4, bf16[128,4096]{1,0:T(8,128)(2,1)S(1)} %shard_map.93.mine_p.refs_0_, bf16[128,4096]{1,0:T(8,128)(2,1)S(1)} %pad_maximum_fusion.got_x.refs_3_, ...), custom_call_target="tpu_custom_call" | custom-call | flops 2048 | bytes 2048 | tf_op jit(solution)/shard_map/pallas_call | solution.py:182
  14.3 3.5 %collective-permute-done.2.got_p.refs_2_ = bf16[128,4096]{1,0:T(8,128)(2,1)S(1)} collective-permute-done((bf16[128,4096]{1,0:T(8,128)(2,1)S(1)}, bf16[128,4096]{1,0:T(8,128)(2,1)S(1)}, u32[]{:S(2)}, u32[]{:S(2)}) %collective-permute-start.2) | collective-permute-done | bytes 1048608 | tf_op jit(solution)/shard_map/ppermute | solution.py:334
  17.8 0.0 copy-start
  17.8 0.0 copy-start.1
  17.8 0.0 copy-start.2
  17.8 0.9 %shard_map.97 = f32[16,256]{1,0:T(8,128)S(1)} custom-call(s32[1]{0:T(128)} %bitcast.me_ref, f32[16,256]{1,0:T(8,128)S(1)} %get-tuple-element.84.in_ref, f32[16,256]{1,0:T(8,128)S(1)} %get-tuple-element.85.weight_ref, bf16[128,4096]{1,0:T(8,128)(2,1)S(1)} %shard_map.93.mine_p.refs_0_, bf16[128,4096]{1,0:T(8,128)(2,1)S(1)} %collective-permute-done.2.got_p.refs_2_, ...), custom_call_target="tpu_custom_call" | custom-call | flops 2048 | bytes 2048 | tf_op jit(solution)/shard_map/pallas_call | solution.py:237
  18.7 2.7 %collective-permute-start.8 = (bf16[128,4096]{1,0:T(8,128)(2,1)S(1)}, bf16[128,4096]{1,0:T(8,128)(2,1)S(1)}, u32[]{:S(2)}, u32[]{:S(2)}) collective-permute-start(bf16[128,4096]{1,0:T(8,128)(2,1)S(1)} %collective-permute-done.2.got_p.refs_2_), channel_id=1, source_target_pairs={{0,1},{1,0},{2,3},{3,2},{4,5},{5,4},{6,7},{7,6},{8,9},{9,8},{10,11... | collective-permute-start | bytes 3145736 | tf_op jit(solution)/shard_map/ppermute | solution.py:334
  21.5 1.8 %collective-permute-start.3 = (f32[16,256]{1,0:T(8,128)S(1)}, f32[16,256]{1,0:T(8,128)S(1)}, u32[]{:S(2)}, u32[]{:S(2)}) collective-permute-start(f32[16,256]{1,0:T(8,128)S(1)} %shard_map.97), channel_id=1, source_target_pairs={{0,193},{1,192},{2,195},{3,194},{4,197},{5,196},{6,199},{7,198},{8... | collective-permute-start | bytes 49160 | tf_op jit(solution)/shard_map/ppermute | solution.py:358
  23.3 2.9 %collective-permute-done.3 = f32[16,256]{1,0:T(8,128)S(1)} collective-permute-done((f32[16,256]{1,0:T(8,128)S(1)}, f32[16,256]{1,0:T(8,128)S(1)}, u32[]{:S(2)}, u32[]{:S(2)}) %collective-permute-start.3) | collective-permute-done | bytes 16416 | tf_op jit(solution)/shard_map/ppermute | solution.py:358
  26.1 0.0 collective-permute-start.4
  26.2 3.3 %collective-permute-done.4 = f32[16,256]{1,0:T(8,128)S(1)} collective-permute-done((f32[16,256]{1,0:T(8,128)S(1)}, f32[16,256]{1,0:T(8,128)S(1)}, u32[]{:S(2)}, u32[]{:S(2)}) %collective-permute-start.4) | collective-permute-done | bytes 16416 | tf_op jit(solution)/shard_map/ppermute | solution.py:358
  29.5 0.0 collective-permute-start.5
  29.5 1.2 %collective-permute-done.5 = f32[16,256]{1,0:T(8,128)S(1)} collective-permute-done((f32[16,256]{1,0:T(8,128)S(1)}, f32[16,256]{1,0:T(8,128)S(1)}, u32[]{:S(2)}, u32[]{:S(2)}) %collective-permute-start.5) | collective-permute-done | bytes 16416 | tf_op jit(solution)/shard_map/ppermute | solution.py:352
  30.7 1.5 %collective-permute-start.6 = (f32[16,256]{1,0:T(8,128)S(1)}, f32[16,256]{1,0:T(8,128)S(1)}, u32[]{:S(2)}, u32[]{:S(2)}) collective-permute-start(f32[16,256]{1,0:T(8,128)S(1)} %add.26), channel_id=1, source_target_pairs={{0,9},{1,8},{2,11},{3,10},{4,13},{5,12},{6,15},{7,14},{8,1},{9,0},... | collective-permute-start | bytes 49160 | tf_op jit(solution)/shard_map/ppermute | solution.py:352
  32.2 1.6 %collective-permute-done.6 = f32[16,256]{1,0:T(8,128)S(1)} collective-permute-done((f32[16,256]{1,0:T(8,128)S(1)}, f32[16,256]{1,0:T(8,128)S(1)}, u32[]{:S(2)}, u32[]{:S(2)}) %collective-permute-start.6) | collective-permute-done | bytes 16416 | tf_op jit(solution)/shard_map/ppermute | solution.py:352
  33.9 0.0 collective-permute-done.7.refs_4_
  33.9 0.0 collective-permute-done.8.refs_5_
  33.9 3.1 %collective-permute-start.9 = (f32[16,256]{1,0:T(8,128)S(1)}, f32[16,256]{1,0:T(8,128)S(1)}, u32[]{:S(2)}, u32[]{:S(2)}) collective-permute-start(f32[16,256]{1,0:T(8,128)S(1)} %add.27), channel_id=1, source_target_pairs={{0,17},{1,16},{2,19},{3,18},{4,21},{5,20},{6,23},{7,22},{8,25},{9,... | collective-permute-start | bytes 49160 | tf_op jit(solution)/shard_map/ppermute | solution.py:352
  37.0 0.0 copy-done
  37.0 0.0 copy-done.1
  37.0 0.0 copy-done.2
  37.0 1.5 %shard_map.98 = (bf16[128,4096]{1,0:T(8,128)(2,1)}, bf16[128,4096]{1,0:T(8,128)(2,1)}, bf16[128,4096]{1,0:T(8,128)(2,1)}) custom-call(s32[1]{0:T(128)} %bitcast.me_ref, bf16[16,128,384]{2,1,0:T(8,128)(2,1)S(1)} %get-tuple-element.89.ahead_ref, bf16[16,128,384]{2,1,0:T(8,128)(2,1)S(1)} %get-tuple-element.90.back_ref, ...), custom_call_target="tpu_custom_call" | custom-call | flops 201326592 | bytes 3538944 | tf_op jit(solution)/shard_map/pallas_call | solution.py:294
  38.5 0.0 collective-permute-done.9
  38.5 5.0 %collective-permute-start.10 = (f32[16,256]{1,0:T(8,128)S(1)}, f32[16,256]{1,0:T(8,128)S(1)}, u32[]{:S(2)}, u32[]{:S(2)}) collective-permute-start(f32[16,256]{1,0:T(8,128)S(1)} %add.28), channel_id=1, source_target_pairs={{0,57},{1,56},{2,59},{3,58},{4,61},{5,60},{6,63},{7,62},{8,49},{9,... | collective-permute-start | bytes 49160 | tf_op jit(solution)/shard_map/ppermute | solution.py:352
  43.5 1.4 %shard_map.99 = (bf16[128,4096]{1,0:T(8,128)(2,1)}, bf16[128,4096]{1,0:T(8,128)(2,1)}, bf16[128,4096]{1,0:T(8,128)(2,1)}) custom-call(s32[1]{0:T(128)} %bitcast.me_ref, bf16[16,128,384]{2,1,0:T(8,128)(2,1)S(1)} %get-tuple-element.89.ahead_ref, ...), custom_call_target="tpu_custom_call", output_to_operand_aliasing={{0}: (12, {}), {1}: (13, {}), {2}: (14, {})} | custom-call | flops 201326592 | bytes 3538944 | tf_op jit(solution)/shard_map/pallas_call | solution.py:294
  44.9 0.0 collective-permute-done.10
  45.0 1.2 %collective-permute-start.11 = (f32[16,256]{1,0:T(8,128)S(1)}, f32[16,256]{1,0:T(8,128)S(1)}, u32[]{:S(2)}, u32[]{:S(2)}) collective-permute-start(f32[16,256]{1,0:T(8,128)S(1)} %add.29), channel_id=1, source_target_pairs={{0,6},{1,7},{2,4},{3,5},{4,2},{5,3},{6,0},{7,1},{8,14},{9,15},{10,... | collective-permute-start | bytes 49160 | tf_op jit(solution)/shard_map/ppermute | solution.py:352
  46.1 1.4 %shard_map.100 = (bf16[128,4096]{1,0:T(8,128)(2,1)}, bf16[128,4096]{1,0:T(8,128)(2,1)}, bf16[128,4096]{1,0:T(8,128)(2,1)}) custom-call(s32[1]{0:T(128)} %bitcast.me_ref, bf16[16,128,384]{2,1,0:T(8,128)(2,1)S(1)} %get-tuple-element.89.ahead_ref, ...), custom_call_target="tpu_custom_call", output_to_operand_aliasing={{0}: (12, {}), {1}: (13, {}), {2}: (14, {})} | custom-call | flops 201326592 | bytes 3538944 | tf_op jit(solution)/shard_map/pallas_call | solution.py:294
  47.6 1.3 %collective-permute-done.11 = f32[16,256]{1,0:T(8,128)S(1)} collective-permute-done((f32[16,256]{1,0:T(8,128)S(1)}, f32[16,256]{1,0:T(8,128)S(1)}, u32[]{:S(2)}, u32[]{:S(2)}) %collective-permute-start.11) | collective-permute-done | bytes 16416 | tf_op jit(solution)/shard_map/ppermute | solution.py:352
  48.8 0.0 collective-permute-start.12
  48.8 1.5 %shard_map.101 = (bf16[128,4096]{1,0:T(8,128)(2,1)}, bf16[128,4096]{1,0:T(8,128)(2,1)}, bf16[128,4096]{1,0:T(8,128)(2,1)}) custom-call(s32[1]{0:T(128)} %bitcast.me_ref, bf16[16,128,384]{2,1,0:T(8,128)(2,1)S(1)} %get-tuple-element.89.ahead_ref, ...), custom_call_target="tpu_custom_call", output_to_operand_aliasing={{0}: (12, {}), {1}: (13, {}), {2}: (14, {})} | custom-call | flops 201326592 | bytes 3538944 | tf_op jit(solution)/shard_map/pallas_call | solution.py:294
  50.3 1.7 %collective-permute-done.12 = f32[16,256]{1,0:T(8,128)S(1)} collective-permute-done((f32[16,256]{1,0:T(8,128)S(1)}, f32[16,256]{1,0:T(8,128)S(1)}, u32[]{:S(2)}, u32[]{:S(2)}) %collective-permute-start.12) | collective-permute-done | bytes 16416 | tf_op jit(solution)/shard_map/ppermute | solution.py:352
  52.0 0.6 %add.31 = f32[16,256]{1,0:T(8,128)} add(f32[16,256]{1,0:T(8,128)S(1)} %add.30, f32[16,256]{1,0:T(8,128)S(1)} %collective-permute-done.12) | non-fusion elementwise | flops 4096 | bytes 49152 | tf_op jit(solution)/shard_map/add | solution.py:352
  (7 shorter events, 0.0 us)
Async XLA Ops:
  2.3 15.6 %collective-permute-start.2 = (bf16[128,4096]{1,0:T(8,128)(2,1)S(1)}, bf16[128,4096]{1,0:T(8,128)(2,1)S(1)}, u32[]{:S(2)}, u32[]{:S(2)}) collective-permute-start(bf16[128,4096]{1,0:T(8,128)(2,1)S(1)} %shard_map.93.mine_p.refs_0_), channel_id=1, source_target_pairs={{0,64},{1,2},{2,1},{3,4},{4,3},{5,6},{6,5},{7,8},{8,7},{9,10},{10,... | collective-permute-start | bytes 3145736 | tf_op jit(solution)/shard_map/ppermute | solution.py:334
  6.7 4.3 %copy-start.3 = (bf16[16,256]{1,0:T(8,128)(2,1)S(1)}, bf16[16,256]{1,0:T(8,128)(2,1)}, u32[]{:S(2)}) copy-start(bf16[16,256]{1,0:T(8,128)(2,1)} %filt_ref.1) | copy-start | bytes 24580
  6.7 4.3 %copy-start.4 = (s32[16]{0:T(128)S(1)}, s32[16]{0:T(128)}, u32[]{:S(2)}) copy-start(s32[16]{0:T(128)} %reach_ref.3) | copy-start | bytes 196
  6.7 2.2 %collective-permute-start = (bf16[128,2048]{1,0:T(8,128)(2,1)S(1)}, bf16[128,2048]{1,0:T(8,128)(2,1)S(1)}, u32[]{:S(2)}, u32[]{:S(2)}) collective-permute-start(bf16[128,2048]{1,0:T(8,128)(2,1)S(1)} %get-tuple-element.104.refs_0_.refs_1_), channel_id=1, source_target_pairs={{0,1},{1,0},{2,3},{3,2},{4,5},{5,4},{6,7},{7,6},{8,9},{9,8},{10,11... | collective-permute-start | bytes 1572872 | tf_op jit(solution)/shard_map/ppermute | solution.py:334
  7.4 2.3 %collective-permute-start.1 = (bf16[128,2048]{1,0:T(8,128)(2,1)S(1)}, bf16[128,2048]{1,0:T(8,128)(2,1)S(1)}, u32[]{:S(2)}, u32[]{:S(2)}) collective-permute-start(bf16[128,2048]{1,0:T(8,128)(2,1)S(1)} %get-tuple-element.133.refs_1_), channel_id=1, source_target_pairs={{0,1},{1,0},{2,3},{3,2},{4,5},{5,4},{6,7},{7,6},{8,9},{9,8},{10,11... | collective-permute-start | bytes 1572872 | tf_op jit(solution)/shard_map/ppermute | solution.py:334
  9.8 24.1 %collective-permute-start.7 = (bf16[128,4096]{1,0:T(8,128)(2,1)S(1)}, bf16[128,4096]{1,0:T(8,128)(2,1)S(1)}, u32[]{:S(2)}, u32[]{:S(2)}) collective-permute-start(bf16[128,4096]{1,0:T(8,128)(2,1)S(1)} %pad_maximum_fusion.got_x.refs_3_), channel_id=1, source_target_pairs={{0,63},{1,2},{2,1},{3,4},{4,3},{5,6},{6,5},{7,8},{8,7},{9,10},{10,... | collective-permute-start | bytes 3145736 | tf_op jit(solution)/shard_map/ppermute | solution.py:334
  17.8 19.1 %copy-start = (bf16[1,128,4096]{2,1,0:T(8,128)(2,1)S(1)}, bf16[1,128,4096]{2,1,0:T(8,128)(2,1)}, u32[]{:S(2)}) copy-start(bf16[1,128,4096]{2,1,0:T(8,128)(2,1)} %param.7) | copy-start | bytes 3145732
  17.8 19.1 %copy-start.1 = (bf16[1,128,4096]{2,1,0:T(8,128)(2,1)S(1)}, bf16[1,128,4096]{2,1,0:T(8,128)(2,1)}, u32[]{:S(2)}) copy-start(bf16[1,128,4096]{2,1,0:T(8,128)(2,1)} %param.8) | copy-start | bytes 3145732
  17.8 19.1 %copy-start.2 = (bf16[1,128,4096]{2,1,0:T(8,128)(2,1)S(1)}, bf16[1,128,4096]{2,1,0:T(8,128)(2,1)}, u32[]{:S(2)}) copy-start(bf16[1,128,4096]{2,1,0:T(8,128)(2,1)} %param.9) | copy-start | bytes 3145732
  18.7 15.1 %collective-permute-start.8 = (bf16[128,4096]{1,0:T(8,128)(2,1)S(1)}, bf16[128,4096]{1,0:T(8,128)(2,1)S(1)}, u32[]{:S(2)}, u32[]{:S(2)}) collective-permute-start(bf16[128,4096]{1,0:T(8,128)(2,1)S(1)} %collective-permute-done.2.got_p.refs_2_), channel_id=1, source_target_pairs={{0,1},{1,0},{2,3},{3,2},{4,5},{5,4},{6,7},{7,6},{8,9},{9,8},{10,11... | collective-permute-start | bytes 3145736 | tf_op jit(solution)/shard_map/ppermute | solution.py:334
  21.5 4.7 %collective-permute-start.3 = (f32[16,256]{1,0:T(8,128)S(1)}, f32[16,256]{1,0:T(8,128)S(1)}, u32[]{:S(2)}, u32[]{:S(2)}) collective-permute-start(f32[16,256]{1,0:T(8,128)S(1)} %shard_map.97), channel_id=1, source_target_pairs={{0,193},{1,192},{2,195},{3,194},{4,197},{5,196},{6,199},{7,198},{8... | collective-permute-start | bytes 49160 | tf_op jit(solution)/shard_map/ppermute | solution.py:358
  26.1 3.4 %collective-permute-start.4 = (f32[16,256]{1,0:T(8,128)S(1)}, f32[16,256]{1,0:T(8,128)S(1)}, u32[]{:S(2)}, u32[]{:S(2)}) collective-permute-start(f32[16,256]{1,0:T(8,128)S(1)} %add.24), channel_id=1, source_target_pairs={{0,65},{1,64},{2,67},{3,66},{4,69},{5,68},{6,71},{7,70},{8,73},{9,... | collective-permute-start | bytes 49160 | tf_op jit(solution)/shard_map/ppermute | solution.py:358
  29.5 1.2 %collective-permute-start.5 = (f32[16,256]{1,0:T(8,128)S(1)}, f32[16,256]{1,0:T(8,128)S(1)}, u32[]{:S(2)}, u32[]{:S(2)}) collective-permute-start(f32[16,256]{1,0:T(8,128)S(1)} %add.25), channel_id=1, source_target_pairs={{0,1},{1,0},{2,3},{3,2},{4,5},{5,4},{6,7},{7,6},{8,9},{9,8},{10,11... | collective-permute-start | bytes 49160 | tf_op jit(solution)/shard_map/ppermute | solution.py:352
  30.7 3.2 %collective-permute-start.6 = (f32[16,256]{1,0:T(8,128)S(1)}, f32[16,256]{1,0:T(8,128)S(1)}, u32[]{:S(2)}, u32[]{:S(2)}) collective-permute-start(f32[16,256]{1,0:T(8,128)S(1)} %add.26), channel_id=1, source_target_pairs={{0,9},{1,8},{2,11},{3,10},{4,13},{5,12},{6,15},{7,14},{8,1},{9,0},... | collective-permute-start | bytes 49160 | tf_op jit(solution)/shard_map/ppermute | solution.py:352
  33.9 4.6 %collective-permute-start.9 = (f32[16,256]{1,0:T(8,128)S(1)}, f32[16,256]{1,0:T(8,128)S(1)}, u32[]{:S(2)}, u32[]{:S(2)}) collective-permute-start(f32[16,256]{1,0:T(8,128)S(1)} %add.27), channel_id=1, source_target_pairs={{0,17},{1,16},{2,19},{3,18},{4,21},{5,20},{6,23},{7,22},{8,25},{9,... | collective-permute-start | bytes 49160 | tf_op jit(solution)/shard_map/ppermute | solution.py:352
  38.5 6.5 %collective-permute-start.10 = (f32[16,256]{1,0:T(8,128)S(1)}, f32[16,256]{1,0:T(8,128)S(1)}, u32[]{:S(2)}, u32[]{:S(2)}) collective-permute-start(f32[16,256]{1,0:T(8,128)S(1)} %add.28), channel_id=1, source_target_pairs={{0,57},{1,56},{2,59},{3,58},{4,61},{5,60},{6,63},{7,62},{8,49},{9,... | collective-permute-start | bytes 49160 | tf_op jit(solution)/shard_map/ppermute | solution.py:352
  45.0 3.9 %collective-permute-start.11 = (f32[16,256]{1,0:T(8,128)S(1)}, f32[16,256]{1,0:T(8,128)S(1)}, u32[]{:S(2)}, u32[]{:S(2)}) collective-permute-start(f32[16,256]{1,0:T(8,128)S(1)} %add.29), channel_id=1, source_target_pairs={{0,6},{1,7},{2,4},{3,5},{4,2},{5,3},{6,0},{7,1},{8,14},{9,15},{10,... | collective-permute-start | bytes 49160 | tf_op jit(solution)/shard_map/ppermute | solution.py:352
  48.8 3.2 %collective-permute-start.12 = (f32[16,256]{1,0:T(8,128)S(1)}, f32[16,256]{1,0:T(8,128)S(1)}, u32[]{:S(2)}, u32[]{:S(2)}) collective-permute-start(f32[16,256]{1,0:T(8,128)S(1)} %add.30), channel_id=1, source_target_pairs={{0,3},{1,2},{2,1},{3,0},{4,7},{5,6},{6,5},{7,4},{8,11},{9,10},{10,... | collective-permute-start | bytes 49160 | tf_op jit(solution)/shard_map/ppermute | solution.py:352
